TPU v7x, 32 devices: a whole 2x2x4 slice. The times are simulated.
32 devices in a mesh: rep: 4 (over y, x), shard: 8 (over z, core).
Axes of the slice: x: 2, y: 2, z: 4, core: 2. Of those that a mesh axis runs over, the one named last changes fastest.
Arguments:
- inner_weights: float32 [4, 2, 512, 512], P('rep', None, 'shard'), may hold values from -6 to 6
- first_moment: float32 [4, 2, 512, 512], P('rep', None, 'shard'), may hold values from -1 to 1
- second_moment: float32 [4, 2, 512, 512], P('rep', None, 'shard'), may hold values from 0 to 1, as said below
- outer_weights: float32 [2, 512, 512], P(None, 'shard'), may hold values from -6 to 6
- outer_velocity: float32 [2, 512, 512], P(None, 'shard'), may hold values from -3 to 3
- tokens: bfloat16 [4, 2, 4096, 512], P('rep', None, 'shard'), may hold values from -6 to 6
- targets: bfloat16 [4, 2, 4096, 2, 512], P('rep', None, 'shard'), may hold values from -25 to 25
- step_count: int32 [1], replicated, may hold values from 10 to 39
- first_fragment: int32 [1], replicated, may hold values from 0 to 1
Outputs:
- new_outer: float32 [2, 512, 512], P(None, 'shard')
- new_inner: float32 [4, 2, 512, 512], P('rep', None, 'shard')
Inputs may be any that keep to these rules, and one draw needn't show every extreme that they name: `second_moment`: positive.
All inputs are finite; a program needn't handle non-finite values.
Results may differ from a plain program's by a relative error of at most 0.00085.
Values may be sent and summed in bfloat16 or wider, within the bound.
No kernel may reach another device: no remote copies, remote signals or barrier semaphores. Data moves between devices by JAX's collectives and lax.ppermute only.
A program may use at most 64 MiB of HBM per device.

v0:
```python
import math

import jax
import jax.numpy as jnp
from jax import lax
from jax.sharding import PartitionSpec as P

beta_one = 0.9
beta_two = 0.95
inner_rate = 0.1
adam_eps = 1e-08
decay_rate = 0.1
clip_norm = 0.02
outer_rate = 0.7
outer_momentum = 0.9
mixing = 0.5


def body(
    inner_weights,
    first_moment,
    second_moment,
    outer_weights,
    outer_velocity,
    tokens,
    targets,
    step_count,
    first_fragment,
):
    weights = inner_weights[0]
    moment_one = first_moment[0]
    moment_two = second_moment[0]
    outer = outer_weights
    velocity = outer_velocity
    width = weights.shape[2]
    replicas = lax.axis_size("rep")
    shards = lax.axis_size("shard")
    tok_dev = tokens.shape[2]
    scale = 1.0 / math.sqrt(width)
    grad_scale = scale / (tok_dev * shards)
    first = first_fragment[0]
    for step in range(tokens.shape[1]):
        frag = first if step == 0 else 1 - first
        theta = lax.dynamic_index_in_dim(outer, frag, 0, keepdims=False)
        speed = lax.dynamic_index_in_dim(velocity, frag, 0, keepdims=False)
        own = lax.dynamic_index_in_dim(weights, frag, 0, keepdims=False)
        batch = tokens[0, step]
        target = targets[0, step]
        lowered = weights.astype(jnp.bfloat16)
        raw = jnp.einsum(
            "td,fkd->tfk",
            batch,
            lax.all_gather(lowered, "shard", axis=1, tiled=True),
            preferred_element_type=jnp.float32,
        )
        residual = (raw * scale - target.astype(jnp.float32)).astype(jnp.bfloat16)
        partial_grad = (
            jnp.einsum("tfk,td->fkd", residual, batch, preferred_element_type=jnp.float32)
            * grad_scale
        )
        grad = lax.psum_scatter(
            partial_grad.astype(jnp.bfloat16), "shard", scatter_dimension=1, tiled=True
        ).astype(jnp.float32)
        summed = lax.psum(theta - own, "rep")
        delta = summed / replicas
        speed = outer_momentum * speed + delta
        theta = theta - outer_rate * (outer_momentum * speed + delta)
        outer = lax.dynamic_update_index_in_dim(outer, theta, frag, 0)
        velocity = lax.dynamic_update_index_in_dim(velocity, speed, frag, 0)
        squares = lax.psum(jnp.sum(grad * grad), "shard")
        norm = jnp.sqrt(squares)
        clipped = grad * jnp.minimum(1.0, clip_norm / (norm + 1e-06))
        count = step_count[0].astype(jnp.float32) + step
        moment_one = beta_one * moment_one + (1.0 - beta_one) * clipped
        moment_two = beta_two * moment_two + (1.0 - beta_two) * clipped * clipped
        correct_one = 1.0 - jnp.power(beta_one, count)
        correct_two = 1.0 - jnp.power(beta_two, count)
        update = moment_one / correct_one / (jnp.sqrt(moment_two / correct_two) + adam_eps)
        weights = weights - inner_rate * (update + decay_rate * weights)
        local = lax.dynamic_index_in_dim(weights, frag, 0, keepdims=False)
        merged = mixing * theta + (1.0 - mixing) * local
        weights = lax.dynamic_update_index_in_dim(weights, merged, frag, 0)
    return (outer, weights[None])


def solution(mesh):
    in_specs = (
        P("rep", None, "shard", None),
        P("rep", None, "shard", None),
        P("rep", None, "shard", None),
        P(None, "shard", None),
        P(None, "shard", None),
        P("rep", None, "shard", None),
        P("rep", None, "shard", None, None),
        P(),
        P(),
    )
    out_specs = (P(None, "shard", None), P("rep", None, "shard", None))
    return jax.shard_map(body, mesh=mesh, in_specs=in_specs, out_specs=out_specs, check_vma=False)
```

profile of v0, /device:TPU:0, one launch (start us, length us, event | category | flops | bytes accessed | tf_op | source)
XLA Modules:
  0.0 222.8 jit_solution(8486300861980709142)
XLA Ops:
  8.0 0.0 all-gather.3.cloned.1.call-start
  8.0 1.0 copy.34
  9.0 0.9 copy.35
  9.9 1.8 bitcast_convert_fusion
  11.7 0.0 all-gather.3.cloned.1.call-update
  11.7 0.0 reduce-scatter.3.cloned.1.call-start
  11.8 24.9 %all-gather.3.cloned.1.call-done = bf16[2,512,512]{2,1,0:T(8,128)(2,1)} async-done(((bf16[2,64,512]{2,1,0:T(8,128)(2,1)}), bf16[2,512,512]{2,1,0:T(8,128)(2,1)}) %all-gather.3.cloned.1.call-update) | async-done | bytes 1048592 | tf_op jit(solution)/shard_map/all_gather | solution.py:53
  36.7 2.1 fusion.7
  38.8 0.0 copy-start.4
  38.8 4.5 %fusion.1 = bf16[512,2,512]{2,1,0:T(2,128)(2,1)S(1)} fusion(f32[512,2,512]{2,0,1:T(8,128)S(1)} %fusion.7, bf16[1,2,512,2,512]{4,3,2,1,0:T(2,128)(2,1)S(1)} %copy-done.1), kind=kLoop, calls=%fused_computation.3 | loop fusion | flops 2097152 | bytes 4194304 | tf_op jit(solution)/shard_map/convert_element_type | solution.py:56
  43.4 0.0 copy-start.2
  43.4 1.7 multiply_convert_fusion.1
  45.1 0.0 reduce-scatter.3.cloned.1.call-update
  45.1 0.0 all-reduce.3.cloned.1.call-start
  45.9 0.0 copy-done.2
  45.9 0.7 bitcast_subtract_fusion.2
  46.6 0.0 all-reduce.3.cloned.1.call-update
  46.6 0.0 all-gather.5.cloned.1.call-start
  47.4 29.9 %reduce-scatter.3.cloned.1.call-done = bf16[2,64,512]{2,1,0:T(8,128)(2,1)} async-done(((bf16[2,512,512]{2,1,0:T(8,128)(2,1)}), bf16[2,64,512]{2,1,0:T(8,128)(2,1)}) %reduce-scatter.3.cloned.1.call-update) | async-done | bytes 131088 | tf_op jit(solution)/shard_map/reduce_scatter | solution.py:61
  77.3 1.6 fusion.21
  78.9 11.4 %all-reduce.3.cloned.1.call-done = f32[64,512]{1,0:T(8,128)} async-done(((f32[64,512]{1,0:T(8,128)}), f32[64,512]{1,0:T(8,128)}) %all-reduce.3.cloned.1.call-update) | async-done | bytes 131088 | tf_op jit(solution)/shard_map/psum | solution.py:64
  90.3 0.9 bitcast_add_fusion.3
  91.3 16.5 %psum.29 = f32[]{:T(128)} all-reduce(f32[]{:T(128)} %fusion.21), channel_id=1, replica_groups=mesh['rep'=4,'shard'=8] {'shard'}, use_global_device_ids=true, to_apply=%region_3.4 | all-reduce | flops 1 | bytes 8 | tf_op jit(solution)/shard_map/psum | solution.py:70
  108.5 0.0 copy-done.6
  108.5 1.1 bitcast_subtract_fusion
  109.7 1.0 bitcast_dynamic-update-slice_fusion.2
  110.7 0.7 convert_element_type.48
  111.3 0.0 all-gather.5.cloned.1.call-update
  111.4 0.0 reduce-scatter.5.cloned.1.call-start
  111.4 19.4 %all-gather.5.cloned.1.call-done = bf16[2,512,512]{2,1,0:T(8,128)(2,1)} async-done(((bf16[2,64,512]{2,1,0:T(8,128)(2,1)}), bf16[2,512,512]{2,1,0:T(8,128)(2,1)}) %all-gather.5.cloned.1.call-update) | async-done | bytes 1048592 | tf_op jit(solution)/shard_map/all_gather | solution.py:53
  130.8 2.1 convolution_multiply_fusion
  132.9 2.4 %copy.15 = f32[2,512,512]{1,0,2:T(2,128)} copy(f32[2,512,512]{2,1,0:T(8,128)S(1)} %convolution_multiply_fusion) | data formatting | bytes 4194304
  135.4 3.0 %fusion = bf16[512,2,512]{2,1,0:T(2,128)(2,1)S(1)} fusion(f32[2,512,512]{1,0,2:T(2,128)} %copy.15, bf16[1,2,512,2,512]{4,3,2,1,0:T(2,128)(2,1)} %param.15), kind=kLoop, calls=%fused_computation.1 | loop fusion | flops 1572864 | bytes 4194304 | tf_op jit(solution)/shard_map/convert_element_type | solution.py:56
  138.4 1.7 multiply_convert_fusion
  140.2 0.0 reduce-scatter.5.cloned.1.call-update
  140.2 0.0 all-reduce.5.cloned.1.call-start
  140.4 0.7 bitcast_subtract_fusion.1
  141.0 31.2 %reduce-scatter.5.cloned.1.call-done = bf16[2,64,512]{2,1,0:T(8,128)(2,1)} async-done(((bf16[2,512,512]{2,1,0:T(8,128)(2,1)}), bf16[2,64,512]{2,1,0:T(8,128)(2,1)}) %reduce-scatter.5.cloned.1.call-update) | async-done | bytes 131088 | tf_op jit(solution)/shard_map/reduce_scatter | solution.py:61
  172.2 1.6 fusion.22
  173.8 0.0 all-reduce.5.cloned.1.call-update
  173.8 14.6 %psum.31 = f32[]{:T(128)} all-reduce(f32[]{:T(128)} %fusion.22), channel_id=1, replica_groups=mesh['rep'=4,'shard'=8] {'shard'}, use_global_device_ids=true, to_apply=%region_7.8 | all-reduce | flops 1 | bytes 8 | tf_op jit(solution)/shard_map/psum | solution.py:70
  189.1 1.2 fusion.19
  190.3 23.6 %all-reduce.5.cloned.1.call-done = f32[64,512]{1,0:T(8,128)} async-done(((f32[64,512]{1,0:T(8,128)}), f32[64,512]{1,0:T(8,128)}) %all-reduce.5.cloned.1.call-update) | async-done | bytes 131088 | tf_op jit(solution)/shard_map/psum | solution.py:64
  213.9 1.0 bitcast_dynamic-update-slice_fusion
  214.8 0.0 copy-start.8
  214.9 0.0 copy-start
  214.9 0.7 copy-done.8
  215.6 0.1 copy-done
  (14 shorter events, 0.1 us)
Async XLA Ops:
  8.0 28.7 %all-gather.3.cloned.1.call-start = ((), (), s32[]{:S(2)}) async-start(), calls=%async_computation.3 | async-start | bytes 1179648 | tf_op jit(solution)/shard_map/all_gather | solution.py:53
  9.9 28.9 %copy-start.1 = (bf16[1,2,512,2,512]{4,3,2,1,0:T(2,128)(2,1)S(1)}, bf16[1,2,512,2,512]{4,3,2,1,0:T(2,128)(2,1)}, u32[]{:S(2)}) copy-start(bf16[1,2,512,2,512]{4,3,2,1,0:T(2,128)(2,1)} %param.15) | copy-start | bytes 6291460
  11.7 65.5 %reduce-scatter.3.cloned.1.call-start = ((), (), s32[]{:S(2)}) async-start(), calls=%async_computation.4 | async-start | bytes 1179648 | tf_op jit(solution)/shard_map/reduce_scatter | solution.py:61
  38.8 4.5 %copy-start.4 = (bf16[1,2,512,512]{3,2,1,0:T(8,128)(2,1)S(1)}, bf16[1,2,512,512]{3,2,1,0:T(8,128)(2,1)}, u32[]{:S(2)}) copy-start(bf16[1,2,512,512]{3,2,1,0:T(8,128)(2,1)} %param.14) | copy-start | bytes 3145732
  43.4 2.5 %copy-start.2 = (f32[1,2,64,512]{3,2,1,0:T(8,128)S(1)}, f32[1,2,64,512]{3,2,1,0:T(8,128)}, u32[]{:S(2)}) copy-start(f32[1,2,64,512]{3,2,1,0:T(8,128)} %param.9) | copy-start | bytes 786436
  45.1 63.4 %copy-start.6 = (f32[1,2,64,512]{3,2,1,0:T(8,128)S(1)}, f32[1,2,64,512]{3,2,1,0:T(8,128)}, u32[]{:S(2)}) copy-start(f32[1,2,64,512]{3,2,1,0:T(8,128)} %param.10) | copy-start | bytes 786436
  45.1 63.4 %copy-start.7 = (f32[1,2,64,512]{3,2,1,0:T(8,128)S(1)}, f32[1,2,64,512]{3,2,1,0:T(8,128)}, u32[]{:S(2)}) copy-start(f32[1,2,64,512]{3,2,1,0:T(8,128)} %param.11) | copy-start | bytes 786436
  45.1 45.2 %all-reduce.3.cloned.1.call-start = ((), (), s32[]{:S(2)}) async-start(), calls=%async_computation.2 | async-start | bytes 262144 | tf_op jit(solution)/shard_map/psum | solution.py:64
  46.6 84.2 %all-gather.5.cloned.1.call-start = ((), (), s32[]{:S(2)}) async-start(), calls=%async_computation.6 | async-start | bytes 1179648 | tf_op jit(solution)/shard_map/all_gather | solution.py:53
  111.4 60.8 %reduce-scatter.5.cloned.1.call-start = ((), (), s32[]{:S(2)}) async-start(), calls=%async_computation.7 | async-start | bytes 1179648 | tf_op jit(solution)/shard_map/reduce_scatter | solution.py:61
  135.4 3.0 %copy-start.5 = (bf16[1,2,512,512]{3,2,1,0:T(8,128)(2,1)S(1)}, bf16[1,2,512,512]{3,2,1,0:T(8,128)(2,1)}, u32[]{:S(2)}) copy-start(bf16[1,2,512,512]{3,2,1,0:T(8,128)(2,1)} %param.14) | copy-start | bytes 3145732
  140.2 48.9 %copy-start.3 = (bf16[2,64,512]{2,1,0:T(8,128)(2,1)S(1)}, bf16[2,64,512]{2,1,0:T(8,128)(2,1)}, u32[]{:S(2)}) copy-start(bf16[2,64,512]{2,1,0:T(8,128)(2,1)} %reduce-scatter.3.cloned.1.call-done) | copy-start | bytes 393220
  140.2 73.7 %all-reduce.5.cloned.1.call-start = ((), (), s32[]{:S(2)}) async-start(), calls=%async_computation.5 | async-start | bytes 262144 | tf_op jit(solution)/shard_map/psum | solution.py:64
  214.8 0.7 copy-start.8
  214.9 0.8 copy-start
Sparse Core Ops, SparseCore 0:
  11.9 24.7 all-gather.2
  45.3 31.9 reduce-scatter.2
  111.5 19.3 all-gather.4
  140.3 31.8 reduce-scatter.4
Sparse Core Ops, SparseCore 1:
  49.1 41.2 all-reduce.2
  173.9 40.0 all-reduce.4
where the time goes:
time: 223 us
  waiting for transfers between devices  140 us (63%)
  blocking collectives  31.1 us (14%)
  other arithmetic  19.7 us (9%)
  between operations  18.4 us (8%)
  matrix products  7.66 us (3%)
  local copies, waits for them, and re-layouts  5.19 us (2%)
    reduce_scatter x2, waiting for transfers between devices, body(): lax.psum_scatter(partial_grad.astype(jnp.bfloat16), 'shard', scatter_dime...  61 us
    all_gather x2, waiting for transfers between devices, body(): lax.all_gather(lowered, 'shard', axis=1, tiled=True)  44.3 us
    psum x2, waiting for transfers between devices, body(): summed = lax.psum(theta - own, 'rep')  35 us
    psum x2, blocking collectives, body(): squares = lax.psum(jnp.sum(grad * grad), 'shard')  31.1 us
    convert_element_type x2, other arithmetic, body(): residual = (raw * scale - target.astype(jnp.float32)).astype(jnp.bfloat16)  7.54 us
    unnamed x22, local copies, waits for them, and re-layouts  5.14 us
  transfers between devices with their start and end apart: 6, of which 6 were waited for; matrix products, arithmetic and copies ran while one was open for 2% of the time, Pallas kernels for 0%

commit v1 on v0

v1 whole, which is shorter than its diff:
```python
import functools
import math

import jax
import jax.numpy as jnp
from jax import lax
from jax.experimental import pallas as pl
from jax.experimental.pallas import tpu as pltpu
from jax.sharding import PartitionSpec as P

beta_one = 0.9
beta_two = 0.95
inner_rate = 0.1
adam_eps = 1e-08
decay_rate = 0.1
clip_norm = 0.02
outer_rate = 0.7
outer_momentum = 0.9
mixing = 0.5

F32 = jnp.float32
BF16 = jnp.bfloat16


def tree_sum(items):
    items = list(items)
    while len(items) > 1:
        items = [a + b for a, b in zip(items[0::2], items[1::2])]
    return items[0]


def nt(a, b):
    return lax.dot_general(a, b, (((1,), (1,)), ((), ())), preferred_element_type=F32)


def tn(a, b):
    return lax.dot_general(a, b, (((0,), (0,)), ((), ())), preferred_element_type=F32)


def chunk_kernel(scale, grad_scale, at_ref, w_ref, xo_ref, xs_ref, to_ref, ts_ref, out_ref):
    w = w_ref[...]
    total = None
    for x_ref, t_ref in ((xo_ref, to_ref), (xs_ref, ts_ref)):
        x = x_ref[...]
        res = (nt(x, w) * scale - t_ref[...].astype(F32)).astype(BF16)
        term = tn(res, x)
        total = term if total is None else total + term
    out_ref[...] = (total * grad_scale).astype(BF16)


def chunk_grad(scale, grad_scale, at, w, own_x, sib_x, own_t, sib_t):
    rows, width = w.shape
    toks = own_x.shape[0]
    full = lambda i, at: (0, 0)
    pick = lambda i, at: (at[0], 0, 0)
    return pl.pallas_call(
        functools.partial(chunk_kernel, scale, grad_scale),
        grid_spec=pltpu.PrefetchScalarGridSpec(
            num_scalar_prefetch=1,
            grid=(1,),
            in_specs=[
                pl.BlockSpec((rows, width), full),
                pl.BlockSpec((toks, width), full),
                pl.BlockSpec((toks, width), full),
                pl.BlockSpec((None, toks, rows), pick),
                pl.BlockSpec((None, toks, rows), pick),
            ],
            out_specs=pl.BlockSpec((rows, width), full),
        ),
        out_shape=jax.ShapeDtypeStruct((rows, width), BF16),
        cost_estimate=pl.CostEstimate(
            flops=8 * rows * toks * width, bytes_accessed=6 * toks * width, transcendentals=0
        ),
        name="chunk_grad",
    )(at, w, own_x, sib_x, own_t, sib_t)


def gram_kernel(at_ref, ho_ref, hs_ref, xo_ref, xs_ref, out_ref):
    out_ref[...] = (tn(ho_ref[...], xo_ref[...]) + tn(hs_ref[...], xs_ref[...])).astype(BF16)


def gram(at, own_x, sib_x):
    toks, width = own_x.shape
    full = lambda i, at: (0, 0)
    half = lambda i, at: (0, at[0])
    return pl.pallas_call(
        gram_kernel,
        grid_spec=pltpu.PrefetchScalarGridSpec(
            num_scalar_prefetch=1,
            grid=(1,),
            in_specs=[
                pl.BlockSpec((toks, width // 2), half),
                pl.BlockSpec((toks, width // 2), half),
                pl.BlockSpec((toks, width), full),
                pl.BlockSpec((toks, width), full),
            ],
            out_specs=pl.BlockSpec((width // 2, width), full),
        ),
        out_shape=jax.ShapeDtypeStruct((width // 2, width), BF16),
        cost_estimate=pl.CostEstimate(
            flops=2 * toks * width * width, bytes_accessed=4 * toks * width, transcendentals=0
        ),
        name="gram",
    )(at, own_x, sib_x, own_x, sib_x)


def fold(x):
    rows, width = x.shape
    tiles = [x[i : i + 8] for i in range(0, rows, 8)]
    while len(tiles) > 1:
        tiles = [a + b for a, b in zip(tiles[0::2], tiles[1::2])]
    x = tiles[0]
    lanes = [x[:, i : i + 128] for i in range(0, width, 128)]
    return functools.reduce(lambda a, b: a + b, lanes)


def sum_kernel(*refs):
    grad_ref, squares_ref = refs[-2:]
    grad = tree_sum(ref[...].astype(F32) for ref in refs[:-2])
    grad_ref[...] = grad
    squares_ref[...] = fold(grad * grad)


def sum_pieces(pieces):
    rows, width = pieces[0].shape
    return pl.pallas_call(
        sum_kernel,
        out_shape=[
            jax.ShapeDtypeStruct((rows, width), F32),
            jax.ShapeDtypeStruct((8, 128), F32),
        ],
        name="sum_pieces",
    )(*pieces)


def correct_kernel(count, factor, place_ref, *refs):
    grad_ref, squares_ref = refs[-2:]
    dw_ref, go_ref, gs_ref = refs[count : count + 3]
    half = go_ref.shape[0]
    total = tree_sum(ref[...].astype(F32) for ref in refs[:count])
    p = place_ref[0]
    extra = None
    for at, g_ref in ((p, go_ref), (1 - p, gs_ref)):
        dw = dw_ref[:, pl.ds(pl.multiple_of(at * half, half), half)]
        high = dw.astype(BF16)
        low = (dw - high.astype(F32)).astype(BF16)
        g = g_ref[...]
        term = jnp.dot(high, g, preferred_element_type=F32) + jnp.dot(
            low, g, preferred_element_type=F32
        )
        extra = term if extra is None else extra + term
    grad = total + factor * extra
    grad_ref[...] = grad
    squares_ref[...] = fold(grad * grad)


def corrected(factor, place, pieces, dw, own_g, sib_g):
    rows, width = dw.shape
    vmem = pl.BlockSpec(memory_space=pltpu.VMEM)
    return pl.pallas_call(
        functools.partial(correct_kernel, len(pieces), factor),
        in_specs=[pl.BlockSpec(memory_space=pltpu.SMEM)] + [vmem] * (len(pieces) + 3),
        out_specs=[vmem, vmem],
        out_shape=[
            jax.ShapeDtypeStruct((rows, width), F32),
            jax.ShapeDtypeStruct((8, 128), F32),
        ],
        name="corrected",
    )(place, *pieces, dw, own_g, sib_g)


def adam(grad, norm_refs, one, two, moment_one, moment_two, weights):
    squares = jnp.sum(tree_sum(ref[...] for ref in norm_refs))
    norm = jnp.sqrt(jnp.full((1, 1), squares, F32))
    clipped = grad * jnp.minimum(1.0, clip_norm / (norm + 1e-06))
    moment_one = beta_one * moment_one + (1.0 - beta_one) * clipped
    moment_two = beta_two * moment_two + (1.0 - beta_two) * clipped * clipped
    update = moment_one / one / (jnp.sqrt(moment_two / two) + adam_eps)
    return moment_one, moment_two, update, weights - inner_rate * (update + decay_rate * weights)


def outer_step(theta, speed, delta):
    speed = outer_momentum * speed + delta
    return theta - outer_rate * (outer_momentum * speed + delta)


def first_kernel(
    replicas, count, first_ref, correct_ref, grad_ref, m_ref, v_ref, w_ref, outer_ref, vel_ref, *refs
):
    sums = refs[:replicas]
    norms = refs[replicas : replicas + count]
    m_out, v_out, w_out, dw_out, theta_out, total_out, send_out = refs[replicas + count :]
    rows = grad_ref.shape[0] // 2
    first = first_ref[0]
    sends = []
    for frag in range(2):
        part = pl.ds(frag * rows, rows)
        m, v, update, after = adam(
            grad_ref[part, :], norms, correct_ref[0], correct_ref[1], m_ref[frag], v_ref[frag], w_ref[frag]
        )
        m_out[frag] = m
        v_out[frag] = v
        sends.append(update)
        total = tree_sum(ref[frag] for ref in sums)
        total_out[frag] = total
        old = outer_ref[frag]
        theta = outer_step(old, vel_ref[frag], old - total * (1.0 / replicas))
        now = first == frag
        theta_out[frag] = jnp.where(now, theta, old)
        after = jnp.where(now, mixing * theta + (1.0 - mixing) * after, after)
        w_out[frag] = after
        dw_out[part, :] = after.astype(BF16).astype(F32) - w_ref[frag].astype(BF16).astype(F32)
    send_out[...] = jnp.where(first == 0, sends[1], sends[0]).astype(BF16)


def last_kernel(
    replicas, count, first_ref, correct_ref, grad_ref, m_ref, v_ref, w_ref, outer_ref, vel_ref, total_ref, *refs
):
    updates = refs[:replicas]
    norms = refs[replicas : replicas + count]
    outer_out, inner_out = refs[replicas + count :]
    rows = grad_ref.shape[0] // 2
    first = first_ref[0]
    moved = tree_sum(ref[...].astype(F32) for ref in updates)
    for frag in range(2):
        part = pl.ds(frag * rows, rows)
        after = adam(
            grad_ref[part, :], norms, correct_ref[2], correct_ref[3], m_ref[frag], v_ref[frag], w_ref[frag]
        )[3]
        old = outer_ref[frag]
        mean = ((1.0 - inner_rate * decay_rate) * total_ref[frag] - inner_rate * moved) * (1.0 / replicas)
        theta = outer_step(old, vel_ref[frag], old - mean)
        now = first != frag
        outer_out[frag] = jnp.where(now, theta, old)
        inner_out[frag] = jnp.where(now, mixing * theta + (1.0 - mixing) * after, after)


def body(
    inner_weights,
    first_moment,
    second_moment,
    outer_weights,
    outer_velocity,
    tokens,
    targets,
    step_count,
    first_fragment,
):
    weights = inner_weights[0]
    rows, width = weights.shape[1:]
    replicas = lax.axis_size("rep")
    shards = lax.axis_size("shard")
    chips = shards // 2
    toks = tokens.shape[2]
    scale = 1.0 / math.sqrt(width)
    grad_scale = scale / (toks * shards)
    index = lax.axis_index("shard")
    core = index % 2
    chip = index // 2

    def swap(x, axis, size, by):
        return lax.ppermute(x, axis, [(i, i ^ by) for i in range(size)])

    sibling = lambda x: swap(x, "shard", shards, 1)
    across = lambda x, by: swap(x, "shard", shards, 2 * by)
    over_rep = lambda x, by: x if by == 0 else swap(x, "rep", replicas, by)

    lowered = weights.astype(BF16).reshape(2 * rows, width)
    held = [lowered] + [across(lowered, k) for k in range(1, chips)]

    own_x = [tokens[0, s] for s in range(2)]
    sib_x = [sibling(x) for x in own_x]

    own_t, sib_t = [], []
    for s in range(2):
        goal = targets[0, s].reshape(toks, 2, chips, 2, rows)
        arrange = lambda y: y.transpose(2, 0, 1, 3).reshape(chips, toks, 2 * rows)
        own_t.append(arrange(lax.dynamic_index_in_dim(goal, core, 3, keepdims=False)))
        sib_t.append(sibling(arrange(lax.dynamic_index_in_dim(goal, 1 - core, 3, keepdims=False))))

    place = [jnp.reshape(chip ^ k, (1,)).astype(jnp.int32) for k in range(chips)]
    side = jnp.reshape(core, (1,)).astype(jnp.int32)

    def pieces(s):
        made = [
            chunk_grad(scale, grad_scale, place[k], held[k], own_x[s], sib_x[s], own_t[s], sib_t[s])
            for k in range(chips)
        ]
        return [made[0]] + [across(made[k], k) for k in range(1, chips)]

    def norm_parts(squares):
        both = squares + sibling(squares)
        return [both] + [across(both, k) for k in range(1, chips)]

    sums = [over_rep(weights, k) for k in range(replicas)]

    grad, squares = sum_pieces(pieces(0))
    norms = norm_parts(squares)

    half = gram(side, own_x[1], sib_x[1]).reshape(chips, width // shards, width)
    strips = [lax.dynamic_index_in_dim(half, chip ^ k, 0, keepdims=False) for k in range(chips)]
    strip = tree_sum(
        x.astype(F32) for x in [strips[0]] + [across(strips[k], k) for k in range(1, chips)]
    ).astype(BF16)
    own_g = jnp.zeros((chips, width // shards, width), BF16)
    for k in range(chips):
        own_g = lax.dynamic_update_index_in_dim(
            own_g, strip if k == 0 else across(strip, k), chip ^ k, 0
        )
    own_g = own_g.reshape(width // 2, width)
    sib_g = sibling(own_g)

    count = step_count[0].astype(F32)
    correct = jnp.stack(
        [1.0 - jnp.power(beta, count + s) for s in range(2) for beta in (beta_one, beta_two)]
    )
    smem = pl.BlockSpec(memory_space=pltpu.SMEM)
    vmem = pl.BlockSpec(memory_space=pltpu.VMEM)
    state = jax.ShapeDtypeStruct((2, rows, width), F32)
    flat = jax.ShapeDtypeStruct((2 * rows, width), F32)
    m, v, middle, change, outer, total, moved = pl.pallas_call(
        functools.partial(first_kernel, replicas, chips),
        in_specs=[smem, smem] + [vmem] * (6 + replicas + chips),
        out_specs=[vmem] * 7,
        out_shape=[state, state, state, flat, state, state, jax.ShapeDtypeStruct((rows, width), BF16)],
        name="first_update",
    )(
        first_fragment,
        correct,
        grad,
        first_moment[0],
        second_moment[0],
        weights,
        outer_weights,
        outer_velocity,
        *sums,
        *norms,
    )
    updates = [over_rep(moved, k) for k in range(replicas)]

    grad, squares = corrected(scale * grad_scale, side, pieces(1), change, own_g, sib_g)
    norms = norm_parts(squares)
    new_outer, new_inner = pl.pallas_call(
        functools.partial(last_kernel, replicas, chips),
        in_specs=[smem, smem] + [vmem] * (7 + replicas + chips),
        out_specs=[vmem] * 2,
        out_shape=[state, state],
        name="last_update",
    )(first_fragment, correct, grad, m, v, middle, outer, outer_velocity, total, *updates, *norms)
    return (new_outer, new_inner[None])


def solution(mesh):
    in_specs = (
        P("rep", None, "shard", None),
        P("rep", None, "shard", None),
        P("rep", None, "shard", None),
        P(None, "shard", None),
        P(None, "shard", None),
        P("rep", None, "shard", None),
        P("rep", None, "shard", None, None),
        P(),
        P(),
    )
    out_specs = (P(None, "shard", None), P("rep", None, "shard", None))
    return jax.shard_map(body, mesh=mesh, in_specs=in_specs, out_specs=out_specs, check_vma=False)
```

time: 223 us -> 128 us (0.57)
  waiting for transfers between devices: 140 us -> 23.3 us
  starting transfers between devices: 0.25 us -> 40.3 us
  Pallas kernels: 0 us -> 34.3 us
  blocking collectives: 31.1 us -> 0 us
  local copies, waits for them, and re-layouts: 5.19 us -> 24.9 us
  other arithmetic: 19.7 us -> 2.3 us
  between operations: 18.4 us -> 2.52 us
  matrix products: 7.66 us -> 0 us
    reduce_scatter x2 -> x0, waiting for transfers between devices: 61 us -> none  [body(): lax.psum_scatter(partial_grad.astype(jnp.bfloat16), 'shard', scatter_dime...]
    all_gather x2 -> x0, waiting for transfers between devices: 44.3 us -> none  [body(): lax.all_gather(lowered, 'shard', axis=1, tiled=True)]
    ppermute x0 -> x34, starting transfers between devices: none -> 40.3 us  [swap(): return lax.ppermute(x, axis, [(i, i ^ by) for i in range(size)])]
    psum x2 -> x0, waiting for transfers between devices: 35 us -> none  [body(): summed = lax.psum(theta - own, 'rep')]
    pallas_call x0 -> x13, Pallas kernels: none -> 34.3 us  [the longest x8 21.5 us: chunk_grad(): pl.pallas_call(functools.partial(chunk_kernel, scale, grad_scale), grid_s...]
    psum x2 -> x0, blocking collectives: 31.1 us -> none  [body(): squares = lax.psum(jnp.sum(grad * grad), 'shard')]
    ppermute x0 -> x34, waiting for transfers between devices: none -> 23.3 us  [swap(): return lax.ppermute(x, axis, [(i, i ^ by) for i in range(size)])]
    convert_element_type x4 -> x1, other arithmetic: 9.99 us -> 0.02 us  [body(): lowered = weights.astype(BF16).reshape(2 * rows, width)]
  transfers between devices with their start and end apart: 6 -> 34, of which waited for: 6 -> 10; matrix products, arithmetic and copies ran while one was open for 2% -> 17% of each run, Pallas kernels for 0% -> 25%
where the time goes in v1:
time: 128 us
  starting transfers between devices  40.3 us (31%)
  Pallas kernels  34.3 us (27%)
  local copies, waits for them, and re-layouts  24.9 us (19%)
  waiting for transfers between devices  23.3 us (18%)
  between operations  2.52 us (2%)
  other arithmetic  2.3 us (2%)
    ppermute x34, starting transfers between devices, swap(): return lax.ppermute(x, axis, [(i, i ^ by) for i in range(size)])  40.3 us
    ppermute x34, waiting for transfers between devices, swap(): return lax.ppermute(x, axis, [(i, i ^ by) for i in range(size)])  23.3 us
    pallas_call x8, Pallas kernels, chunk_grad(): pl.pallas_call(functools.partial(chunk_kernel, scale, grad_scale), grid_s...  21.5 us
    unnamed x80, local copies, waits for them, and re-layouts  10.7 us
    reshape x4, local copies, waits for them, and re-layouts, body(): arrange = lambda y: y.transpose(2, 0, 1, 3).reshape(chips, toks, 2 * rows)  4.08 us
    transpose x5, local copies, waits for them, and re-layouts, body(): arrange = lambda y: y.transpose(2, 0, 1, 3).reshape(chips, toks, 2 * rows)  3.66 us
    slice x1, local copies, waits for them, and re-layouts, body(): goal = targets[0, s].reshape(toks, 2, chips, 2, rows)  3.63 us
    pallas_call x1, Pallas kernels, body(): pl.pallas_call(functools.partial(first_kernel, replicas, chips), in_specs...  3.21 us
  transfers between devices with their start and end apart: 34, of which 10 were waited for; matrix products, arithmetic and copies ran while one was open for 17% of the time, Pallas kernels for 25%

profile of v1, /device:TPU:0, one launch (start us, length us, event | category | flops | bytes accessed | tf_op | source)
XLA Modules:
  0.0 127.6 jit_solution(13720223169950089205)
XLA Ops:
  0.6 1.3 slice_bitcast_fusion
  2.5 3.6 %fusion.3 = (bf16[1,1,512,2,512]{4,3,2,1,0:T(2,128)(2,1)}, bf16[1,1,512,2,512]{4,3,2,1,0:T(2,128)(2,1)}) fusion(bf16[1,2,512,2,512]{4,3,2,1,0:T(2,128)(2,1)} %param.15), kind=kLoop, calls=%fused_computation.17 | loop fusion | bytes 4194304 | tf_op jit(solution)/shard_map/slice | solution.py:276
  6.2 2.5 %copy.44 = bf16[1,1,512,2,512]{2,4,3,1,0:T(8,128)(2,1)S(1)} copy(bf16[1,1,512,2,512]{4,3,2,1,0:T(2,128)(2,1)} %get-tuple-element.30) | data formatting | bytes 2097152
  8.6 3.7 %copy.43 = bf16[1,1,512,2,512]{2,4,3,1,0:T(8,128)(2,1)} copy(bf16[1,1,512,2,512]{4,3,2,1,0:T(2,128)(2,1)} %get-tuple-element.31) | data formatting | bytes 2097152
  12.3 2.4 %dynamic-slice_bitcast_fusion = (bf16[4,512,2,64]{1,3,0,2:T(8,128)(2,1)S(1)}, bf16[4,512,2,64]{1,3,0,2:T(8,128)(2,1)}, bf16[4,512,2,64]{1,3,0,2:T(8,128)(2,1)}, bf16[4,512,2,64]{1,3,0,2:T(8,128)(2,1)}) fusion(bf16[512,2,4,2,64]{0,4,3,2,1:T(8,128)(2,1)S(1)} %bitcast.56, s32[]{:T(128)S(6)} %select_n.41, s32[]{:T(128)S(6)} %select_n.40, ...), kind=kLoop, calls=%fused_computation | loop fusion | bytes 4194312 | tf_op jit(solution)/shard_map/transpose | solution.py:277
  14.8 1.0 copy.38
  17.1 2.6 %gram.1 = bf16[256,512]{1,0:T(8,128)(2,1)} custom-call(s32[1]{0:T(128)} %bitcast.at_ref.place_ref, bf16[512,512]{1,0:T(8,128)(2,1)} %copy-done, bf16[512,512]{1,0:T(8,128)(2,1)} %copy-done.1, bf16[512,512]{1,0:T(8,128)(2,1)} %copy-done, bf16[512,512]{1,0:T(8,128)(2,1)} %copy-done.1), custom_call_target="tpu_custom_call" | custom-call | flops 268435456 | bytes 1048576 | tf_op jit(solution)/shard_map/gram/pallas_call | solution.py:86
  19.6 1.6 %dynamic-slice_bitcast_fusion.6 = (bf16[64,512]{1,0:T(8,128)(2,1)}, bf16[64,512]{1,0:T(8,128)(2,1)}, bf16[64,512]{1,0:T(8,128)(2,1)}) fusion(bf16[4,64,512]{2,1,0:T(8,128)(2,1)} %bitcast.72, s32[]{:T(128)S(6)} %select_n.43, s32[]{:T(128)S(6)} %select_n.45, s32[]{:T(128)S(6)} %select_n.44), kind=kLoop, calls=%fused_computation.15 | loop fusion | bytes 393228 | tf_op jit(solution)/shard_map/jit(dynamic_index_in_dim)/squeeze | solution.py:301
  21.2 4.7 %collective-permute-start.22 = (bf16[64,512]{1,0:T(8,128)(2,1)}, bf16[64,512]{1,0:T(8,128)(2,1)}, u32[]{:S(2)}, u32[]{:S(2)}) collective-permute-start(bf16[64,512]{1,0:T(8,128)(2,1)} %get-tuple-element.39), channel_id=1, source_target_pairs={{0,6},{1,7},{2,4},{3,5},{4,2},{5,3},{6,0},{7,1},{8,14},{9,15},{10,... | collective-permute-start | bytes 196616 | tf_op jit(solution)/shard_map/ppermute | solution.py:262
  27.3 1.1 copy.28
  28.5 1.0 copy.31.to_ref
  31.6 1.5 %collective-permute-start.2 = (bf16[128,512]{1,0:T(8,128)(2,1)S(1)}, bf16[128,512]{1,0:T(8,128)(2,1)S(1)}, u32[]{:S(2)}, u32[]{:S(2)}) collective-permute-start(bf16[128,512]{1,0:T(8,128)(2,1)S(1)} %bitcast.67), channel_id=1, source_target_pairs={{0,2},{1,3},{2,0},{3,1},{4,6},{5,7},{6,4},{7,5},{8,10},{9,11},{10,... | collective-permute-start | bytes 393224 | tf_op jit(solution)/shard_map/ppermute | solution.py:262
  33.1 2.9 %collective-permute-start.4 = (bf16[128,512]{1,0:T(8,128)(2,1)S(1)}, bf16[128,512]{1,0:T(8,128)(2,1)S(1)}, u32[]{:S(2)}, u32[]{:S(2)}) collective-permute-start(bf16[128,512]{1,0:T(8,128)(2,1)S(1)} %bitcast.68), channel_id=1, source_target_pairs={{0,4},{1,5},{2,6},{3,7},{4,0},{5,1},{6,2},{7,3},{8,12},{9,13},{10,... | collective-permute-start | bytes 393224 | tf_op jit(solution)/shard_map/ppermute | solution.py:262
  37.0 1.5 %collective-permute-done.2.w_ref = bf16[128,512]{1,0:T(8,128)(2,1)S(1)} collective-permute-done((bf16[128,512]{1,0:T(8,128)(2,1)S(1)}, bf16[128,512]{1,0:T(8,128)(2,1)S(1)}, u32[]{:S(2)}, u32[]{:S(2)}) %collective-permute-start.2) | collective-permute-done | bytes 131104 | tf_op jit(solution)/shard_map/ppermute | solution.py:262
  38.6 1.5 %collective-permute-start.13 = (f32[2,64,512]{2,1,0:T(8,128)S(1)}, f32[2,64,512]{2,1,0:T(8,128)S(1)}, u32[]{:S(2)}, u32[]{:S(2)}) collective-permute-start(f32[2,64,512]{2,1,0:T(8,128)S(1)} %bitcast.60), channel_id=1, source_target_pairs={{0,8},{8,0},{16,24},{24,16},{1,9},{9,1},{17,25},{25,17},{2,10},{10... | collective-permute-start | bytes 786440 | tf_op jit(solution)/shard_map/ppermute | solution.py:262
  41.0 2.7 %chunk_grad.13 = bf16[128,512]{1,0:T(8,128)(2,1)} custom-call(s32[1]{0:T(128)} %bitcast.11.at_ref, bf16[128,512]{1,0:T(8,128)(2,1)} %copy-done.13, bf16[512,512]{1,0:T(8,128)(2,1)} %copy-done.2, bf16[512,512]{1,0:T(8,128)(2,1)} %copy-done.3, bf16[4,512,128]{2,1,0:T(8,128)(2,1)} %copy.39.to_ref, bf16[4,512,128]{2,1,0:T(8,128)(2,1)} %copy-done.4), custom_call_target="tpu_custom_call" | custom-call | flops 268435456 | bytes 1572864 | tf_op jit(solution)/shard_map/chunk_grad/pallas_call | solution.py:56
  43.7 2.4 %collective-permute-done.4.w_ref = bf16[128,512]{1,0:T(8,128)(2,1)S(1)} collective-permute-done((bf16[128,512]{1,0:T(8,128)(2,1)S(1)}, bf16[128,512]{1,0:T(8,128)(2,1)S(1)}, u32[]{:S(2)}, u32[]{:S(2)}) %collective-permute-start.4) | collective-permute-done | bytes 131104 | tf_op jit(solution)/shard_map/ppermute | solution.py:262
  46.0 1.5 %collective-permute-start.14 = (f32[2,64,512]{2,1,0:T(8,128)S(1)}, f32[2,64,512]{2,1,0:T(8,128)S(1)}, u32[]{:S(2)}, u32[]{:S(2)}) collective-permute-start(f32[2,64,512]{2,1,0:T(8,128)S(1)} %bitcast.61), channel_id=1, source_target_pairs={{0,16},{8,24},{16,0},{24,8},{1,17},{9,25},{17,1},{25,9},{2,18},{10... | collective-permute-start | bytes 786440 | tf_op jit(solution)/shard_map/ppermute | solution.py:262
  47.6 2.7 %chunk_grad.14 = bf16[128,512]{1,0:T(8,128)(2,1)} custom-call(s32[1]{0:T(128)} %bitcast.12.at_ref, bf16[128,512]{1,0:T(8,128)(2,1)} %copy-done.12, bf16[512,512]{1,0:T(8,128)(2,1)} %copy-done.2, bf16[512,512]{1,0:T(8,128)(2,1)} %copy-done.3, bf16[4,512,128]{2,1,0:T(8,128)(2,1)} %copy.39.to_ref, bf16[4,512,128]{2,1,0:T(8,128)(2,1)} %copy-done.4), custom_call_target="tpu_custom_call" | custom-call | flops 268435456 | bytes 1572864 | tf_op jit(solution)/shard_map/chunk_grad/pallas_call | solution.py:56
  50.9 2.7 %chunk_grad.15 = bf16[128,512]{1,0:T(8,128)(2,1)} custom-call(s32[1]{0:T(128)} %bitcast.13.at_ref, bf16[128,512]{1,0:T(8,128)(2,1)} %copy-done.11, bf16[512,512]{1,0:T(8,128)(2,1)} %copy-done.2, bf16[512,512]{1,0:T(8,128)(2,1)} %copy-done.3, bf16[4,512,128]{2,1,0:T(8,128)(2,1)} %copy.39.to_ref, bf16[4,512,128]{2,1,0:T(8,128)(2,1)} %copy-done.4), custom_call_target="tpu_custom_call" | custom-call | flops 268435456 | bytes 1572864 | tf_op jit(solution)/shard_map/chunk_grad/pallas_call | solution.py:56
  53.6 2.3 %collective-permute-start.24 = (bf16[64,512]{1,0:T(8,128)(2,1)S(1)}, bf16[64,512]{1,0:T(8,128)(2,1)S(1)}, u32[]{:S(2)}, u32[]{:S(2)}) collective-permute-start(bf16[64,512]{1,0:T(8,128)(2,1)S(1)} %get-tuple-element.29), channel_id=1, source_target_pairs={{0,4},{1,5},{2,6},{3,7},{4,0},{5,1},{6,2},{7,3},{8,12},{9,13},{10,... | collective-permute-start | bytes 196616 | tf_op jit(solution)/shard_map/ppermute | solution.py:262
  55.9 2.8 %collective-permute-done.24 = bf16[64,512]{1,0:T(8,128)(2,1)S(1)} collective-permute-done((bf16[64,512]{1,0:T(8,128)(2,1)S(1)}, bf16[64,512]{1,0:T(8,128)(2,1)S(1)}, u32[]{:S(2)}, u32[]{:S(2)}) %collective-permute-start.24) | collective-permute-done | bytes 65568 | tf_op jit(solution)/shard_map/ppermute | solution.py:262
  58.8 2.3 %collective-permute-start.25 = (bf16[64,512]{1,0:T(8,128)(2,1)S(1)}, bf16[64,512]{1,0:T(8,128)(2,1)S(1)}, u32[]{:S(2)}, u32[]{:S(2)}) collective-permute-start(bf16[64,512]{1,0:T(8,128)(2,1)S(1)} %get-tuple-element.29), channel_id=1, source_target_pairs={{0,6},{1,7},{2,4},{3,5},{4,2},{5,3},{6,0},{7,1},{8,14},{9,15},{10,... | collective-permute-start | bytes 196616 | tf_op jit(solution)/shard_map/ppermute | solution.py:262
  61.1 1.6 %collective-permute-start.15 = (f32[2,64,512]{2,1,0:T(8,128)S(1)}, f32[2,64,512]{2,1,0:T(8,128)S(1)}, u32[]{:S(2)}, u32[]{:S(2)}) collective-permute-start(f32[2,64,512]{2,1,0:T(8,128)S(1)} %bitcast.62), channel_id=1, source_target_pairs={{0,24},{8,16},{16,8},{24,0},{1,25},{9,17},{17,9},{25,1},{2,26},{10... | collective-permute-start | bytes 786440 | tf_op jit(solution)/shard_map/ppermute | solution.py:262
  62.8 2.1 %collective-permute-done.25 = bf16[64,512]{1,0:T(8,128)(2,1)S(1)} collective-permute-done((bf16[64,512]{1,0:T(8,128)(2,1)S(1)}, bf16[64,512]{1,0:T(8,128)(2,1)S(1)}, u32[]{:S(2)}, u32[]{:S(2)}) %collective-permute-start.25) | collective-permute-done | bytes 65568 | tf_op jit(solution)/shard_map/ppermute | solution.py:262
  65.4 2.6 %collective-permute-start.12 = (bf16[128,512]{1,0:T(8,128)(2,1)}, bf16[128,512]{1,0:T(8,128)(2,1)S(1)}, u32[]{:S(2)}, u32[]{:S(2)}) collective-permute-start(bf16[128,512]{1,0:T(8,128)(2,1)} %chunk_grad.15), channel_id=1, source_target_pairs={{0,6},{1,7},{2,4},{3,5},{4,2},{5,3},{6,0},{7,1},{8,14},{9,15},{10,... | collective-permute-start | bytes 393224 | tf_op jit(solution)/shard_map/ppermute | solution.py:262
  68.0 6.9 %collective-permute-done.11.refs_2_ = bf16[128,512]{1,0:T(8,128)(2,1)S(1)} collective-permute-done((bf16[128,512]{1,0:T(8,128)(2,1)S(1)}, bf16[128,512]{1,0:T(8,128)(2,1)S(1)}, u32[]{:S(2)}, u32[]{:S(2)}) %collective-permute-start.11) | collective-permute-done | bytes 131104 | tf_op jit(solution)/shard_map/ppermute | solution.py:262
  74.9 2.7 %chunk_grad.12.refs_0_ = bf16[128,512]{1,0:T(8,128)(2,1)} custom-call(s32[1]{0:T(128)} %bitcast.1.at_ref, bf16[128,512]{1,0:T(8,128)(2,1)} %bitcast.70, bf16[512,512]{1,0:T(8,128)(2,1)} %copy-done.2, bf16[512,512]{1,0:T(8,128)(2,1)} %copy-done.3, bf16[4,512,128]{2,1,0:T(8,128)(2,1)} %copy.39.to_ref, bf16[4,512,128]{2,1,0:T(8,128)(2,1)} %copy-done.4), custom_call_target="tpu_custom_call" | custom-call | flops 268435456 | bytes 1572864 | tf_op jit(solution)/shard_map/chunk_grad/pallas_call | solution.py:56
  77.7 2.7 %chunk_grad.9 = bf16[128,512]{1,0:T(8,128)(2,1)} custom-call(s32[1]{0:T(128)} %bitcast.11.at_ref, bf16[128,512]{1,0:T(8,128)(2,1)} %copy-done.13, bf16[512,512]{1,0:T(8,128)(2,1)} %copy-done, bf16[512,512]{1,0:T(8,128)(2,1)} %copy-done.1, bf16[4,512,128]{2,1,0:T(8,128)(2,1)} %copy.31.to_ref, bf16[4,512,128]{2,1,0:T(8,128)(2,1)} %copy-done.5), custom_call_target="tpu_custom_call" | custom-call | flops 268435456 | bytes 1572864 | tf_op jit(solution)/shard_map/chunk_grad/pallas_call | solution.py:56
  81.0 1.9 %sum_pieces.1 = (f32[128,512]{1,0:T(8,128)}, f32[8,128]{1,0:T(8,128)}) custom-call(bf16[128,512]{1,0:T(8,128)(2,1)} %chunk_grad.12.refs_0_, bf16[128,512]{1,0:T(8,128)(2,1)} %copy-done.24, bf16[128,512]{1,0:T(8,128)(2,1)} %copy-done.25, bf16[128,512]{1,0:T(8,128)(2,1)} %copy-done.26), custom_call_target="tpu_custom_call" | custom-call | tf_op jit(solution)/shard_map/sum_pieces/pallas_call | solution.py:126
  83.4 2.7 %chunk_grad.10 = bf16[128,512]{1,0:T(8,128)(2,1)} custom-call(s32[1]{0:T(128)} %bitcast.12.at_ref, bf16[128,512]{1,0:T(8,128)(2,1)} %copy-done.12, bf16[512,512]{1,0:T(8,128)(2,1)} %copy-done, bf16[512,512]{1,0:T(8,128)(2,1)} %copy-done.1, bf16[4,512,128]{2,1,0:T(8,128)(2,1)} %copy.31.to_ref, bf16[4,512,128]{2,1,0:T(8,128)(2,1)} %copy-done.5), custom_call_target="tpu_custom_call" | custom-call | flops 268435456 | bytes 1572864 | tf_op jit(solution)/shard_map/chunk_grad/pallas_call | solution.py:56
  86.1 2.3 %collective-permute-start.5 = (bf16[128,512]{1,0:T(8,128)(2,1)}, bf16[128,512]{1,0:T(8,128)(2,1)S(1)}, u32[]{:S(2)}, u32[]{:S(2)}) collective-permute-start(bf16[128,512]{1,0:T(8,128)(2,1)} %chunk_grad.10), channel_id=1, source_target_pairs={{0,4},{1,5},{2,6},{3,7},{4,0},{5,1},{6,2},{7,3},{8,12},{9,13},{10,... | collective-permute-start | bytes 393224 | tf_op jit(solution)/shard_map/ppermute | solution.py:262
  88.4 2.7 %collective-permute-start.18 = (f32[8,128]{1,0:T(8,128)S(1)}, f32[8,128]{1,0:T(8,128)S(1)}, u32[]{:S(2)}, u32[]{:S(2)}) collective-permute-start(f32[8,128]{1,0:T(8,128)S(1)} %add.57.refs_4_), channel_id=1, source_target_pairs={{0,4},{1,5},{2,6},{3,7},{4,0},{5,1},{6,2},{7,3},{8,12},{9,13},{10,... | collective-permute-start | bytes 12296 | tf_op jit(solution)/shard_map/ppermute | solution.py:262
  91.1 2.7 %chunk_grad.11 = bf16[128,512]{1,0:T(8,128)(2,1)} custom-call(s32[1]{0:T(128)} %bitcast.13.at_ref, bf16[128,512]{1,0:T(8,128)(2,1)} %copy-done.11, bf16[512,512]{1,0:T(8,128)(2,1)} %copy-done, bf16[512,512]{1,0:T(8,128)(2,1)} %copy-done.1, bf16[4,512,128]{2,1,0:T(8,128)(2,1)} %copy.31.to_ref, bf16[4,512,128]{2,1,0:T(8,128)(2,1)} %copy-done.5), custom_call_target="tpu_custom_call" | custom-call | flops 268435456 | bytes 1572864 | tf_op jit(solution)/shard_map/chunk_grad/pallas_call | solution.py:56
  93.8 1.7 %collective-permute-start.7 = (bf16[128,512]{1,0:T(8,128)(2,1)}, bf16[128,512]{1,0:T(8,128)(2,1)S(1)}, u32[]{:S(2)}, u32[]{:S(2)}) collective-permute-start(bf16[128,512]{1,0:T(8,128)(2,1)} %chunk_grad.11), channel_id=1, source_target_pairs={{0,6},{1,7},{2,4},{3,5},{4,2},{5,3},{6,0},{7,1},{8,14},{9,15},{10,... | collective-permute-start | bytes 393224 | tf_op jit(solution)/shard_map/ppermute | solution.py:262
  95.8 1.9 %collective-permute-start.19 = (f32[8,128]{1,0:T(8,128)S(1)}, f32[8,128]{1,0:T(8,128)S(1)}, u32[]{:S(2)}, u32[]{:S(2)}) collective-permute-start(f32[8,128]{1,0:T(8,128)S(1)} %add.57.refs_4_), channel_id=1, source_target_pairs={{0,6},{1,7},{2,4},{3,5},{4,2},{5,3},{6,0},{7,1},{8,14},{9,15},{10,... | collective-permute-start | bytes 12296 | tf_op jit(solution)/shard_map/ppermute | solution.py:262
  98.9 2.3 %collective-permute-done.19.refs_7_ = f32[8,128]{1,0:T(8,128)S(1)} collective-permute-done((f32[8,128]{1,0:T(8,128)S(1)}, f32[8,128]{1,0:T(8,128)S(1)}, u32[]{:S(2)}, u32[]{:S(2)}) %collective-permute-start.19) | collective-permute-done | bytes 4128 | tf_op jit(solution)/shard_map/ppermute | solution.py:262
  101.8 3.2 %first_update.1 = (f32[2,64,512]{2,1,0:T(8,128)}, f32[2,64,512]{2,1,0:T(8,128)}, f32[2,64,512]{2,1,0:T(8,128)}, f32[128,512]{1,0:T(8,128)}, f32[2,64,512]{2,1,0:...) custom-call(s32[1]{0:T(128)S(6)} %copy.50.first_ref, f32[4]{0:T(128)} %pad_maximum_fusion.correct_ref, ...), custom_call_target="tpu_custom_call" | custom-call | tf_op jit(solution)/shard_map/first_update/pallas_call | solution.py:321
  105.1 2.1 %collective-permute-start.28 = (bf16[64,512]{1,0:T(8,128)(2,1)}, bf16[64,512]{1,0:T(8,128)(2,1)S(1)}, u32[]{:S(2)}, u32[]{:S(2)}) collective-permute-start(bf16[64,512]{1,0:T(8,128)(2,1)} %get-tuple-element.24.refs_0_), channel_id=1, source_target_pairs={{0,16},{8,24},{16,0},{24,8},{1,17},{9,25},{17,1},{25,9},{2,18},{10... | collective-permute-start | bytes 196616 | tf_op jit(solution)/shard_map/ppermute | solution.py:262
  107.2 1.3 %collective-permute-start.29 = (bf16[64,512]{1,0:T(8,128)(2,1)}, bf16[64,512]{1,0:T(8,128)(2,1)S(1)}, u32[]{:S(2)}, u32[]{:S(2)}) collective-permute-start(bf16[64,512]{1,0:T(8,128)(2,1)} %get-tuple-element.24.refs_0_), channel_id=1, source_target_pairs={{0,24},{8,16},{16,8},{24,0},{1,25},{9,17},{17,9},{25,1},{2,26},{10... | collective-permute-start | bytes 196616 | tf_op jit(solution)/shard_map/ppermute | solution.py:262
  108.5 2.7 %chunk_grad.8.refs_0_ = bf16[128,512]{1,0:T(8,128)(2,1)} custom-call(s32[1]{0:T(128)} %bitcast.1.at_ref, bf16[128,512]{1,0:T(8,128)(2,1)} %bitcast.71, bf16[512,512]{1,0:T(8,128)(2,1)} %copy-done, bf16[512,512]{1,0:T(8,128)(2,1)} %copy-done.1, bf16[4,512,128]{2,1,0:T(8,128)(2,1)} %copy.31.to_ref, bf16[4,512,128]{2,1,0:T(8,128)(2,1)} %copy-done.5), custom_call_target="tpu_custom_call" | custom-call | flops 268435456 | bytes 1572864 | tf_op jit(solution)/shard_map/chunk_grad/pallas_call | solution.py:56
  111.9 2.3 %corrected.1 = (f32[128,512]{1,0:T(8,128)}, f32[8,128]{1,0:T(8,128)}) custom-call(s32[1]{0:T(128)} %bitcast.at_ref.place_ref, bf16[128,512]{1,0:T(8,128)(2,1)} %chunk_grad.8.refs_0_, bf16[128,512]{1,0:T(8,128)(2,1)} %copy-done.18, bf16[128,512]{1,0:T(8,128)(2,1)} %copy-done.20, bf16[128,512]{1,0:T(8,128)(2,1)} %copy-done.21, ...), custom_call_target="tpu_custom_call" | custom-call | tf_op jit(solution)/shard_map/corrected/pallas_call | solution.py:160
  114.3 1.4 %collective-permute-done.30 = f32[8,128]{1,0:T(8,128)S(1)} collective-permute-done((f32[8,128]{1,0:T(8,128)}, f32[8,128]{1,0:T(8,128)S(1)}, u32[]{:S(2)}, u32[]{:S(2)}) %collective-permute-start.30) | collective-permute-done | bytes 4128 | tf_op jit(solution)/shard_map/ppermute | solution.py:262
  116.3 1.7 %collective-permute-start.31 = (f32[8,128]{1,0:T(8,128)S(1)}, f32[8,128]{1,0:T(8,128)S(1)}, u32[]{:S(2)}, u32[]{:S(2)}) collective-permute-start(f32[8,128]{1,0:T(8,128)S(1)} %add.65.refs_4_), channel_id=1, source_target_pairs={{0,2},{1,3},{2,0},{3,1},{4,6},{5,7},{6,4},{7,5},{8,10},{9,11},{10,... | collective-permute-start | bytes 12296 | tf_op jit(solution)/shard_map/ppermute | solution.py:262
  118.9 1.9 %collective-permute-start.33 = (f32[8,128]{1,0:T(8,128)S(1)}, f32[8,128]{1,0:T(8,128)S(1)}, u32[]{:S(2)}, u32[]{:S(2)}) collective-permute-start(f32[8,128]{1,0:T(8,128)S(1)} %add.65.refs_4_), channel_id=1, source_target_pairs={{0,6},{1,7},{2,4},{3,5},{4,2},{5,3},{6,0},{7,1},{8,14},{9,15},{10,... | collective-permute-start | bytes 12296 | tf_op jit(solution)/shard_map/ppermute | solution.py:262
  120.8 1.7 %collective-permute-done.32.refs_6_ = f32[8,128]{1,0:T(8,128)S(1)} collective-permute-done((f32[8,128]{1,0:T(8,128)S(1)}, f32[8,128]{1,0:T(8,128)S(1)}, u32[]{:S(2)}, u32[]{:S(2)}) %collective-permute-start.32) | collective-permute-done | bytes 4128 | tf_op jit(solution)/shard_map/ppermute | solution.py:262
  122.5 1.7 %collective-permute-done.33.refs_7_ = f32[8,128]{1,0:T(8,128)S(1)} collective-permute-done((f32[8,128]{1,0:T(8,128)S(1)}, f32[8,128]{1,0:T(8,128)S(1)}, u32[]{:S(2)}, u32[]{:S(2)}) %collective-permute-start.33) | collective-permute-done | bytes 4128 | tf_op jit(solution)/shard_map/ppermute | solution.py:262
  124.9 2.8 %last_update.1 = (f32[2,64,512]{2,1,0:T(8,128)}, f32[2,64,512]{2,1,0:T(8,128)}) custom-call(s32[1]{0:T(128)S(6)} %copy.50.first_ref, f32[4]{0:T(128)} %pad_maximum_fusion.correct_ref, f32[128,512]{1,0:T(8,128)} %get-tuple-element.18.grad_ref, f32[2,64,512]{2,1,0:T(8,128)} %get-tuple-element.19.m_ref, f32[2,64,512]{2,1,0:T(8,128)} %get-tuple-element.20.v_ref, ...), custom_call_target="tpu_custom_call" | custom-call | tf_op jit(solution)/shard_map/last_update/pallas_call | solution.py:343
  (134 shorter events, 13.2 us)
Async XLA Ops:
  1.9 14.3 %collective-permute-start = (bf16[512,512]{1,0:T(8,128)(2,1)S(1)}, bf16[512,512]{1,0:T(8,128)(2,1)S(1)}, u32[]{:S(2)}, u32[]{:S(2)}) collective-permute-start(bf16[512,512]{1,0:T(8,128)(2,1)S(1)} %get-tuple-element.35.xo_ref.ho_ref), channel_id=1, source_target_pairs={{0,1},{1,0},{2,3},{3,2},{4,5},{5,4},{6,7},{7,6},{8,9},{9,8},{10,11... | collective-permute-start | bytes 1572872 | tf_op jit(solution)/shard_map/ppermute | solution.py:262
  2.4 36.1 %collective-permute-start.8 = (bf16[512,512]{1,0:T(8,128)(2,1)S(1)}, bf16[512,512]{1,0:T(8,128)(2,1)S(1)}, u32[]{:S(2)}, u32[]{:S(2)}) collective-permute-start(bf16[512,512]{1,0:T(8,128)(2,1)S(1)} %get-tuple-element.34.xo_ref), channel_id=1, source_target_pairs={{0,1},{1,0},{2,3},{3,2},{4,5},{5,4},{6,7},{7,6},{8,9},{9,8},{10,11... | collective-permute-start | bytes 1572872 | tf_op jit(solution)/shard_map/ppermute | solution.py:262
  14.8 12.5 %copy-start.6 = (f32[1,2,64,512]{3,2,1,0:T(8,128)S(1)}, f32[1,2,64,512]{3,2,1,0:T(8,128)}, u32[]{:S(2)}) copy-start(f32[1,2,64,512]{3,2,1,0:T(8,128)} %param.9) | copy-start | bytes 786436
  15.8 24.3 %collective-permute-start.9 = (bf16[4,512,128]{2,1,0:T(8,128)(2,1)}, bf16[4,512,128]{2,1,0:T(8,128)(2,1)S(1)}, u32[]{:S(2)}, u32[]{:S(2)}) collective-permute-start(bf16[4,512,128]{2,1,0:T(8,128)(2,1)} %copy.38), channel_id=1, source_target_pairs={{0,1},{1,0},{2,3},{3,2},{4,5},{5,4},{6,7},{7,6},{8,9},{9,8},{10,11... | collective-permute-start | bytes 1572872 | tf_op jit(solution)/shard_map/ppermute | solution.py:262
  17.0 12.5 %copy-start.8 = (bf16[4,512,2,64]{1,3,0,2:T(8,128)(2,1)S(1)}, bf16[4,512,2,64]{1,3,0,2:T(8,128)(2,1)}, u32[]{:S(2)}) copy-start(bf16[4,512,2,64]{1,3,0,2:T(8,128)(2,1)} %get-tuple-element.42) | copy-start | bytes 1572868
  21.2 10.4 %collective-permute-start.22 = (bf16[64,512]{1,0:T(8,128)(2,1)}, bf16[64,512]{1,0:T(8,128)(2,1)}, u32[]{:S(2)}, u32[]{:S(2)}) collective-permute-start(bf16[64,512]{1,0:T(8,128)(2,1)} %get-tuple-element.39), channel_id=1, source_target_pairs={{0,6},{1,7},{2,4},{3,5},{4,2},{5,3},{6,0},{7,1},{8,14},{9,15},{10,... | collective-permute-start | bytes 196616 | tf_op jit(solution)/shard_map/ppermute | solution.py:262
  25.9 7.2 %collective-permute-start.21 = (bf16[64,512]{1,0:T(8,128)(2,1)}, bf16[64,512]{1,0:T(8,128)(2,1)}, u32[]{:S(2)}, u32[]{:S(2)}) collective-permute-start(bf16[64,512]{1,0:T(8,128)(2,1)} %get-tuple-element.40), channel_id=1, source_target_pairs={{0,4},{1,5},{2,6},{3,7},{4,0},{5,1},{6,2},{7,3},{8,12},{9,13},{10,... | collective-permute-start | bytes 196616 | tf_op jit(solution)/shard_map/ppermute | solution.py:262
  25.9 10.1 %collective-permute-start.20 = (bf16[64,512]{1,0:T(8,128)(2,1)}, bf16[64,512]{1,0:T(8,128)(2,1)}, u32[]{:S(2)}, u32[]{:S(2)}) collective-permute-start(bf16[64,512]{1,0:T(8,128)(2,1)} %get-tuple-element.38), channel_id=1, source_target_pairs={{0,2},{1,3},{2,0},{3,1},{4,6},{5,7},{6,4},{7,5},{8,10},{9,11},{10,... | collective-permute-start | bytes 196616 | tf_op jit(solution)/shard_map/ppermute | solution.py:262
  27.3 8.7 %copy-start.9 = (bf16[1,2,64,512]{3,2,1,0:T(8,128)(2,1)}, bf16[1,2,64,512]{3,2,1,0:T(8,128)(2,1)S(1)}, u32[]{:S(2)}) copy-start(bf16[1,2,64,512]{3,2,1,0:T(8,128)(2,1)S(1)} %convert_element_type.30) | copy-start | bytes 393220
  31.6 6.9 %collective-permute-start.2 = (bf16[128,512]{1,0:T(8,128)(2,1)S(1)}, bf16[128,512]{1,0:T(8,128)(2,1)S(1)}, u32[]{:S(2)}, u32[]{:S(2)}) collective-permute-start(bf16[128,512]{1,0:T(8,128)(2,1)S(1)} %bitcast.67), channel_id=1, source_target_pairs={{0,2},{1,3},{2,0},{3,1},{4,6},{5,7},{6,4},{7,5},{8,10},{9,11},{10,... | collective-permute-start | bytes 393224 | tf_op jit(solution)/shard_map/ppermute | solution.py:262
  33.1 12.9 %collective-permute-start.4 = (bf16[128,512]{1,0:T(8,128)(2,1)S(1)}, bf16[128,512]{1,0:T(8,128)(2,1)S(1)}, u32[]{:S(2)}, u32[]{:S(2)}) collective-permute-start(bf16[128,512]{1,0:T(8,128)(2,1)S(1)} %bitcast.68), channel_id=1, source_target_pairs={{0,4},{1,5},{2,6},{3,7},{4,0},{5,1},{6,2},{7,3},{8,12},{9,13},{10,... | collective-permute-start | bytes 393224 | tf_op jit(solution)/shard_map/ppermute | solution.py:262
  36.0 14.2 %collective-permute-start.6 = (bf16[128,512]{1,0:T(8,128)(2,1)S(1)}, bf16[128,512]{1,0:T(8,128)(2,1)S(1)}, u32[]{:S(2)}, u32[]{:S(2)}) collective-permute-start(bf16[128,512]{1,0:T(8,128)(2,1)S(1)} %bitcast.69), channel_id=1, source_target_pairs={{0,6},{1,7},{2,4},{3,5},{4,2},{5,3},{6,0},{7,1},{8,14},{9,15},{10,... | collective-permute-start | bytes 393224 | tf_op jit(solution)/shard_map/ppermute | solution.py:262
  38.6 22.5 %collective-permute-start.1 = (bf16[4,512,128]{2,1,0:T(8,128)(2,1)}, bf16[4,512,128]{2,1,0:T(8,128)(2,1)S(1)}, u32[]{:S(2)}, u32[]{:S(2)}) collective-permute-start(bf16[4,512,128]{2,1,0:T(8,128)(2,1)} %copy.30), channel_id=1, source_target_pairs={{0,1},{1,0},{2,3},{3,2},{4,5},{5,4},{6,7},{7,6},{8,9},{9,8},{10,11... | collective-permute-start | bytes 1572872 | tf_op jit(solution)/shard_map/ppermute | solution.py:262
  38.6 47.5 %collective-permute-start.13 = (f32[2,64,512]{2,1,0:T(8,128)S(1)}, f32[2,64,512]{2,1,0:T(8,128)S(1)}, u32[]{:S(2)}, u32[]{:S(2)}) collective-permute-start(f32[2,64,512]{2,1,0:T(8,128)S(1)} %bitcast.60), channel_id=1, source_target_pairs={{0,8},{8,0},{16,24},{24,16},{1,9},{9,1},{17,25},{25,17},{2,10},{10... | collective-permute-start | bytes 786440 | tf_op jit(solution)/shard_map/ppermute | solution.py:262
  40.1 13.5 %collective-permute-start.23 = (bf16[64,512]{1,0:T(8,128)(2,1)S(1)}, bf16[64,512]{1,0:T(8,128)(2,1)S(1)}, u32[]{:S(2)}, u32[]{:S(2)}) collective-permute-start(bf16[64,512]{1,0:T(8,128)(2,1)S(1)} %get-tuple-element.29), channel_id=1, source_target_pairs={{0,2},{1,3},{2,0},{3,1},{4,6},{5,7},{6,4},{7,5},{8,10},{9,11},{10,... | collective-permute-start | bytes 196616 | tf_op jit(solution)/shard_map/ppermute | solution.py:262
  43.7 6.6 %copy-start.23 = (bf16[128,512]{1,0:T(8,128)(2,1)S(1)}, bf16[128,512]{1,0:T(8,128)(2,1)}, u32[]{:S(2)}) copy-start(bf16[128,512]{1,0:T(8,128)(2,1)} %chunk_grad.13) | copy-start | bytes 393220
  46.0 42.3 %collective-permute-start.14 = (f32[2,64,512]{2,1,0:T(8,128)S(1)}, f32[2,64,512]{2,1,0:T(8,128)S(1)}, u32[]{:S(2)}, u32[]{:S(2)}) collective-permute-start(f32[2,64,512]{2,1,0:T(8,128)S(1)} %bitcast.61), channel_id=1, source_target_pairs={{0,16},{8,24},{16,0},{24,8},{1,17},{9,25},{17,1},{25,9},{2,18},{10... | collective-permute-start | bytes 786440 | tf_op jit(solution)/shard_map/ppermute | solution.py:262
  50.2 14.6 %copy-start.22 = (bf16[128,512]{1,0:T(8,128)(2,1)S(1)}, bf16[128,512]{1,0:T(8,128)(2,1)}, u32[]{:S(2)}) copy-start(bf16[128,512]{1,0:T(8,128)(2,1)} %chunk_grad.14) | copy-start | bytes 393220
  50.3 15.1 %collective-permute-start.10 = (bf16[128,512]{1,0:T(8,128)(2,1)S(1)}, bf16[128,512]{1,0:T(8,128)(2,1)S(1)}, u32[]{:S(2)}, u32[]{:S(2)}) collective-permute-start(bf16[128,512]{1,0:T(8,128)(2,1)S(1)} %copy-done.23), channel_id=1, source_target_pairs={{0,2},{1,3},{2,0},{3,1},{4,6},{5,7},{6,4},{7,5},{8,10},{9,11},{10,... | collective-permute-start | bytes 393224 | tf_op jit(solution)/shard_map/ppermute | solution.py:262
  53.6 5.2 %collective-permute-start.24 = (bf16[64,512]{1,0:T(8,128)(2,1)S(1)}, bf16[64,512]{1,0:T(8,128)(2,1)S(1)}, u32[]{:S(2)}, u32[]{:S(2)}) collective-permute-start(bf16[64,512]{1,0:T(8,128)(2,1)S(1)} %get-tuple-element.29), channel_id=1, source_target_pairs={{0,4},{1,5},{2,6},{3,7},{4,0},{5,1},{6,2},{7,3},{8,12},{9,13},{10,... | collective-permute-start | bytes 196616 | tf_op jit(solution)/shard_map/ppermute | solution.py:262
  58.8 6.1 %collective-permute-start.25 = (bf16[64,512]{1,0:T(8,128)(2,1)S(1)}, bf16[64,512]{1,0:T(8,128)(2,1)S(1)}, u32[]{:S(2)}, u32[]{:S(2)}) collective-permute-start(bf16[64,512]{1,0:T(8,128)(2,1)S(1)} %get-tuple-element.29), channel_id=1, source_target_pairs={{0,6},{1,7},{2,4},{3,5},{4,2},{5,3},{6,0},{7,1},{8,14},{9,15},{10,... | collective-permute-start | bytes 196616 | tf_op jit(solution)/shard_map/ppermute | solution.py:262
  61.1 16.5 %copy-start.5 = (bf16[4,512,128]{2,1,0:T(8,128)(2,1)}, bf16[4,512,128]{2,1,0:T(8,128)(2,1)S(1)}, u32[]{:S(2)}) copy-start(bf16[4,512,128]{2,1,0:T(8,128)(2,1)S(1)} %collective-permute-done.1.ts_ref) | copy-start | bytes 1572868
  61.1 27.3 %collective-permute-start.15 = (f32[2,64,512]{2,1,0:T(8,128)S(1)}, f32[2,64,512]{2,1,0:T(8,128)S(1)}, u32[]{:S(2)}, u32[]{:S(2)}) collective-permute-start(f32[2,64,512]{2,1,0:T(8,128)S(1)} %bitcast.62), channel_id=1, source_target_pairs={{0,24},{8,16},{16,8},{24,0},{1,25},{9,17},{17,9},{25,1},{2,26},{10... | collective-permute-start | bytes 786440 | tf_op jit(solution)/shard_map/ppermute | solution.py:262
  64.8 10.1 %collective-permute-start.11 = (bf16[128,512]{1,0:T(8,128)(2,1)S(1)}, bf16[128,512]{1,0:T(8,128)(2,1)S(1)}, u32[]{:S(2)}, u32[]{:S(2)}) collective-permute-start(bf16[128,512]{1,0:T(8,128)(2,1)S(1)} %copy-done.22), channel_id=1, source_target_pairs={{0,4},{1,5},{2,6},{3,7},{4,0},{5,1},{6,2},{7,3},{8,12},{9,13},{10,... | collective-permute-start | bytes 393224 | tf_op jit(solution)/shard_map/ppermute | solution.py:262
  65.4 15.0 %copy-start.24 = (bf16[128,512]{1,0:T(8,128)(2,1)}, bf16[128,512]{1,0:T(8,128)(2,1)S(1)}, u32[]{:S(2)}) copy-start(bf16[128,512]{1,0:T(8,128)(2,1)S(1)} %collective-permute-done.10.refs_1_) | copy-start | bytes 393220
  65.4 15.0 %collective-permute-start.12 = (bf16[128,512]{1,0:T(8,128)(2,1)}, bf16[128,512]{1,0:T(8,128)(2,1)S(1)}, u32[]{:S(2)}, u32[]{:S(2)}) collective-permute-start(bf16[128,512]{1,0:T(8,128)(2,1)} %chunk_grad.15), channel_id=1, source_target_pairs={{0,6},{1,7},{2,4},{3,5},{4,2},{5,3},{6,0},{7,1},{8,14},{9,15},{10,... | collective-permute-start | bytes 393224 | tf_op jit(solution)/shard_map/ppermute | solution.py:262
  67.9 12.4 %copy-start.10 = (bf16[4,64,512]{2,1,0:T(8,128)(2,1)}, bf16[4,64,512]{2,1,0:T(8,128)(2,1)S(1)}, u32[]{:S(2)}) copy-start(bf16[4,64,512]{2,1,0:T(8,128)(2,1)S(1)} %bitcast_dynamic-update-slice_fusion) | copy-start | bytes 786436
  74.9 36.3 %collective-permute-start.26 = (bf16[256,512]{1,0:T(8,128)(2,1)S(1)}, bf16[256,512]{1,0:T(8,128)(2,1)S(1)}, u32[]{:S(2)}, u32[]{:S(2)}) collective-permute-start(bf16[256,512]{1,0:T(8,128)(2,1)S(1)} %bitcast.74), channel_id=1, source_target_pairs={{0,1},{1,0},{2,3},{3,2},{4,5},{5,4},{6,7},{7,6},{8,9},{9,8},{10,11... | collective-permute-start | bytes 786440 | tf_op jit(solution)/shard_map/ppermute | solution.py:262
  82.9 3.1 %collective-permute-start.16 = (f32[8,128]{1,0:T(8,128)}, f32[8,128]{1,0:T(8,128)S(1)}, u32[]{:S(2)}, u32[]{:S(2)}) collective-permute-start(f32[8,128]{1,0:T(8,128)} %get-tuple-element.16), channel_id=1, source_target_pairs={{0,1},{1,0},{2,3},{3,2},{4,5},{5,4},{6,7},{7,6},{8,9},{9,8},{10,11... | collective-permute-start | bytes 12296 | tf_op jit(solution)/shard_map/ppermute | solution.py:262
  86.0 19.0 %collective-permute-start.3 = (bf16[128,512]{1,0:T(8,128)(2,1)S(1)}, bf16[128,512]{1,0:T(8,128)(2,1)S(1)}, u32[]{:S(2)}, u32[]{:S(2)}) collective-permute-start(bf16[128,512]{1,0:T(8,128)(2,1)S(1)} %copy-done.19), channel_id=1, source_target_pairs={{0,2},{1,3},{2,0},{3,1},{4,6},{5,7},{6,4},{7,5},{8,10},{9,11},{10,... | collective-permute-start | bytes 393224 | tf_op jit(solution)/shard_map/ppermute | solution.py:262
  86.1 15.1 %copy-start.30 = (f32[8,128]{1,0:T(8,128)}, f32[8,128]{1,0:T(8,128)S(1)}, u32[]{:S(2)}) copy-start(f32[8,128]{1,0:T(8,128)S(1)} %add.57.refs_4_) | copy-start | bytes 12292
  86.1 15.1 %copy-start.14 = (f32[2,64,512]{2,1,0:T(8,128)}, f32[2,64,512]{2,1,0:T(8,128)S(1)}, u32[]{:S(2)}) copy-start(f32[2,64,512]{2,1,0:T(8,128)S(1)} %collective-permute-done.13.refs_1_) | copy-start | bytes 786436
  86.1 21.1 %collective-permute-start.5 = (bf16[128,512]{1,0:T(8,128)(2,1)}, bf16[128,512]{1,0:T(8,128)(2,1)S(1)}, u32[]{:S(2)}, u32[]{:S(2)}) collective-permute-start(bf16[128,512]{1,0:T(8,128)(2,1)} %chunk_grad.10), channel_id=1, source_target_pairs={{0,4},{1,5},{2,6},{3,7},{4,0},{5,1},{6,2},{7,3},{8,12},{9,13},{10,... | collective-permute-start | bytes 393224 | tf_op jit(solution)/shard_map/ppermute | solution.py:262
  88.4 12.8 %copy-start.15 = (f32[2,64,512]{2,1,0:T(8,128)}, f32[2,64,512]{2,1,0:T(8,128)S(1)}, u32[]{:S(2)}) copy-start(f32[2,64,512]{2,1,0:T(8,128)S(1)} %collective-permute-done.14.refs_2_) | copy-start | bytes 786436
  88.4 5.4 %collective-permute-start.17 = (f32[8,128]{1,0:T(8,128)S(1)}, f32[8,128]{1,0:T(8,128)S(1)}, u32[]{:S(2)}, u32[]{:S(2)}) collective-permute-start(f32[8,128]{1,0:T(8,128)S(1)} %add.57.refs_4_), channel_id=1, source_target_pairs={{0,2},{1,3},{2,0},{3,1},{4,6},{5,7},{6,4},{7,5},{8,10},{9,11},{10,... | collective-permute-start | bytes 12296 | tf_op jit(solution)/shard_map/ppermute | solution.py:262
  88.4 12.8 %copy-start.17 = (f32[2,64,512]{2,1,0:T(8,128)}, f32[2,64,512]{2,1,0:T(8,128)S(1)}, u32[]{:S(2)}) copy-start(f32[2,64,512]{2,1,0:T(8,128)S(1)} %collective-permute-done.15.refs_3_) | copy-start | bytes 786436
  88.4 7.3 %collective-permute-start.18 = (f32[8,128]{1,0:T(8,128)S(1)}, f32[8,128]{1,0:T(8,128)S(1)}, u32[]{:S(2)}, u32[]{:S(2)}) collective-permute-start(f32[8,128]{1,0:T(8,128)S(1)} %add.57.refs_4_), channel_id=1, source_target_pairs={{0,4},{1,5},{2,6},{3,7},{4,0},{5,1},{6,2},{7,3},{8,12},{9,13},{10,... | collective-permute-start | bytes 12296 | tf_op jit(solution)/shard_map/ppermute | solution.py:262
  93.8 7.4 %copy-start.32 = (f32[8,128]{1,0:T(8,128)}, f32[8,128]{1,0:T(8,128)S(1)}, u32[]{:S(2)}) copy-start(f32[8,128]{1,0:T(8,128)S(1)} %collective-permute-done.17.refs_5_) | copy-start | bytes 12292
  93.8 17.4 %collective-permute-start.7 = (bf16[128,512]{1,0:T(8,128)(2,1)}, bf16[128,512]{1,0:T(8,128)(2,1)S(1)}, u32[]{:S(2)}, u32[]{:S(2)}) collective-permute-start(bf16[128,512]{1,0:T(8,128)(2,1)} %chunk_grad.11), channel_id=1, source_target_pairs={{0,6},{1,7},{2,4},{3,5},{4,2},{5,3},{6,0},{7,1},{8,14},{9,15},{10,... | collective-permute-start | bytes 393224 | tf_op jit(solution)/shard_map/ppermute | solution.py:262
  95.8 5.4 %collective-permute-start.19 = (f32[8,128]{1,0:T(8,128)S(1)}, f32[8,128]{1,0:T(8,128)S(1)}, u32[]{:S(2)}, u32[]{:S(2)}) collective-permute-start(f32[8,128]{1,0:T(8,128)S(1)} %add.57.refs_4_), channel_id=1, source_target_pairs={{0,6},{1,7},{2,4},{3,5},{4,2},{5,3},{6,0},{7,1},{8,14},{9,15},{10,... | collective-permute-start | bytes 12296 | tf_op jit(solution)/shard_map/ppermute | solution.py:262
  105.0 13.9 %collective-permute-start.27 = (bf16[64,512]{1,0:T(8,128)(2,1)}, bf16[64,512]{1,0:T(8,128)(2,1)S(1)}, u32[]{:S(2)}, u32[]{:S(2)}) collective-permute-start(bf16[64,512]{1,0:T(8,128)(2,1)} %get-tuple-element.24.refs_0_), channel_id=1, source_target_pairs={{0,8},{8,0},{16,24},{24,16},{1,9},{9,1},{17,25},{25,17},{2,10},{10... | collective-permute-start | bytes 196616 | tf_op jit(solution)/shard_map/ppermute | solution.py:262
  105.1 15.7 %collective-permute-start.28 = (bf16[64,512]{1,0:T(8,128)(2,1)}, bf16[64,512]{1,0:T(8,128)(2,1)S(1)}, u32[]{:S(2)}, u32[]{:S(2)}) collective-permute-start(bf16[64,512]{1,0:T(8,128)(2,1)} %get-tuple-element.24.refs_0_), channel_id=1, source_target_pairs={{0,16},{8,24},{16,0},{24,8},{1,17},{9,25},{17,1},{25,9},{2,18},{10... | collective-permute-start | bytes 196616 | tf_op jit(solution)/shard_map/ppermute | solution.py:262
  107.2 13.6 %collective-permute-start.29 = (bf16[64,512]{1,0:T(8,128)(2,1)}, bf16[64,512]{1,0:T(8,128)(2,1)S(1)}, u32[]{:S(2)}, u32[]{:S(2)}) collective-permute-start(bf16[64,512]{1,0:T(8,128)(2,1)} %get-tuple-element.24.refs_0_), channel_id=1, source_target_pairs={{0,24},{8,16},{16,8},{24,0},{1,25},{9,17},{17,9},{25,1},{2,26},{10... | collective-permute-start | bytes 196616 | tf_op jit(solution)/shard_map/ppermute | solution.py:262
  114.3 1.4 %collective-permute-start.30 = (f32[8,128]{1,0:T(8,128)}, f32[8,128]{1,0:T(8,128)S(1)}, u32[]{:S(2)}, u32[]{:S(2)}) collective-permute-start(f32[8,128]{1,0:T(8,128)} %get-tuple-element.25), channel_id=1, source_target_pairs={{0,1},{1,0},{2,3},{3,2},{4,5},{5,4},{6,7},{7,6},{8,9},{9,8},{10,11... | collective-permute-start | bytes 12296 | tf_op jit(solution)/shard_map/ppermute | solution.py:262
  116.3 7.9 %copy-start.31 = (f32[8,128]{1,0:T(8,128)}, f32[8,128]{1,0:T(8,128)S(1)}, u32[]{:S(2)}) copy-start(f32[8,128]{1,0:T(8,128)S(1)} %add.65.refs_4_) | copy-start | bytes 12292
  116.3 4.4 %collective-permute-start.31 = (f32[8,128]{1,0:T(8,128)S(1)}, f32[8,128]{1,0:T(8,128)S(1)}, u32[]{:S(2)}, u32[]{:S(2)}) collective-permute-start(f32[8,128]{1,0:T(8,128)S(1)} %add.65.refs_4_), channel_id=1, source_target_pairs={{0,2},{1,3},{2,0},{3,1},{4,6},{5,7},{6,4},{7,5},{8,10},{9,11},{10,... | collective-permute-start | bytes 12296 | tf_op jit(solution)/shard_map/ppermute | solution.py:262
  118.0 4.5 %collective-permute-start.32 = (f32[8,128]{1,0:T(8,128)S(1)}, f32[8,128]{1,0:T(8,128)S(1)}, u32[]{:S(2)}, u32[]{:S(2)}) collective-permute-start(f32[8,128]{1,0:T(8,128)S(1)} %add.65.refs_4_), channel_id=1, source_target_pairs={{0,4},{1,5},{2,6},{3,7},{4,0},{5,1},{6,2},{7,3},{8,12},{9,13},{10,... | collective-permute-start | bytes 12296 | tf_op jit(solution)/shard_map/ppermute | solution.py:262
  118.9 5.4 %collective-permute-start.33 = (f32[8,128]{1,0:T(8,128)S(1)}, f32[8,128]{1,0:T(8,128)S(1)}, u32[]{:S(2)}, u32[]{:S(2)}) collective-permute-start(f32[8,128]{1,0:T(8,128)S(1)} %add.65.refs_4_), channel_id=1, source_target_pairs={{0,6},{1,7},{2,4},{3,5},{4,2},{5,3},{6,0},{7,1},{8,14},{9,15},{10,... | collective-permute-start | bytes 12296 | tf_op jit(solution)/shard_map/ppermute | solution.py:262
  (25 other events, 70.1 us)

commit v2 on v1

v2 whole, which is shorter than its diff:
```python
import functools
import math

import jax
import jax.numpy as jnp
from jax import lax
from jax.experimental import pallas as pl
from jax.experimental.pallas import tpu as pltpu
from jax.sharding import PartitionSpec as P

beta_one = 0.9
beta_two = 0.95
inner_rate = 0.1
adam_eps = 1e-08
decay_rate = 0.1
clip_norm = 0.02
outer_rate = 0.7
outer_momentum = 0.9
mixing = 0.5

F32 = jnp.float32
BF16 = jnp.bfloat16
VMEM_BYTES = 16 * 1024 * 1024


def tree_sum(items):
    items = list(items)
    while len(items) > 1:
        items = [a + b for a, b in zip(items[0::2], items[1::2])]
    return items[0]


def nt(a, b):
    return lax.dot_general(a, b, (((1,), (1,)), ((), ())), preferred_element_type=F32)


def tn(a, b):
    return lax.dot_general(a, b, (((0,), (0,)), ((), ())), preferred_element_type=F32)


def call(kernel, out_shape, scalars, arrays, name, after=(), flops=0):
    vmem = pl.BlockSpec(memory_space=pltpu.VMEM)

    def run(*refs):
        count = len(scalars) + len(arrays)
        kernel(*refs[:count], *refs[count + len(after) :])

    return pl.pallas_call(
        run,
        in_specs=[pl.BlockSpec(memory_space=pltpu.SMEM)] * len(scalars)
        + [vmem] * len(arrays)
        + [pl.BlockSpec(memory_space=pl.ANY)] * len(after),
        out_specs=[vmem] * len(out_shape),
        out_shape=out_shape,
        compiler_params=pltpu.CompilerParams(vmem_limit_bytes=VMEM_BYTES),
        cost_estimate=pl.CostEstimate(flops=flops, bytes_accessed=1024, transcendentals=0),
        name=name,
    )(*scalars, *arrays, *after)


def lower_kernel(w_ref, out_ref):
    rows = w_ref.shape[1]
    for frag in range(2):
        out_ref[pl.ds(frag * rows, rows), :] = w_ref[frag].astype(BF16)


def split_kernel(rows, side_ref, goal_ref, keep_ref, send_ref):
    core = side_ref[0]
    first, second = (goal_ref[:, frag, :].astype(F32) for frag in range(2))
    for chip in range(keep_ref.shape[0]):
        parts = []
        for which in range(2):
            at = (2 * chip + which) * rows
            parts.append(
                jnp.concatenate([first[:, at : at + rows], second[:, at : at + rows]], 1).astype(BF16)
            )

        @pl.when(core == 0)
        def _():
            keep_ref[chip] = parts[0]
            send_ref[chip] = parts[1]

        @pl.when(core != 0)
        def _():
            keep_ref[chip] = parts[1]
            send_ref[chip] = parts[0]


def chunk_kernel(scale, grad_scale, group, place_ref, *refs):
    size = len(group)
    w_refs = refs[:size]
    xo_ref, xs_ref, to_ref, ts_ref = refs[size : size + 4]
    outs = refs[size + 4 :]
    rows = w_refs[0].shape[0]
    w = jnp.concatenate([ref[...] for ref in w_refs], 0)
    total = None
    for x_ref, t_ref in ((xo_ref, to_ref), (xs_ref, ts_ref)):
        x = x_ref[...]
        goal = jnp.concatenate([t_ref[place_ref[k]] for k in group], 1)
        res = (nt(x, w) * scale - goal.astype(F32)).astype(BF16)
        term = tn(res, x)
        total = term if total is None else total + term
    total = (total * grad_scale).astype(BF16)
    for i, ref in enumerate(outs):
        ref[...] = total[i * rows : (i + 1) * rows]


def gram_kernel(side_ref, place_ref, xo_ref, xs_ref, *refs):
    outs, scratch = refs[:-1], refs[-1]
    rows, width = outs[0].shape
    part = pl.ds(pl.multiple_of(side_ref[0] * (width // 2), width // 2), width // 2)
    scratch[...] = (tn(xo_ref[:, part], xo_ref[...]) + tn(xs_ref[:, part], xs_ref[...])).astype(BF16)
    for k, ref in enumerate(outs):
        ref[...] = scratch[pl.ds(pl.multiple_of(place_ref[k] * rows, rows), rows), :]


def gather_kernel(place_ref, *refs):
    strips, out_ref = refs[:-1], refs[-1]
    rows = strips[0].shape[0]
    for k, ref in enumerate(strips):
        out_ref[pl.ds(pl.multiple_of(place_ref[k] * rows, rows), rows), :] = ref[...]


def add_kernel(*refs):
    refs[-1][...] = tree_sum(ref[...].astype(F32) for ref in refs[:-1]).astype(refs[-1].dtype)


def fold(x):
    rows, width = x.shape
    tiles = [x[i : i + 8] for i in range(0, rows, 8)]
    while len(tiles) > 1:
        tiles = [a + b for a, b in zip(tiles[0::2], tiles[1::2])]
    x = tiles[0]
    lanes = [x[:, i : i + 128] for i in range(0, width, 128)]
    return functools.reduce(lambda a, b: a + b, lanes)


def sum_kernel(*refs):
    grad_ref, squares_ref = refs[-2:]
    grad = tree_sum(ref[...].astype(F32) for ref in refs[:-2])
    grad_ref[...] = grad
    squares_ref[...] = fold(grad * grad)


def correct_kernel(count, factor, side_ref, *refs):
    grad_ref, squares_ref = refs[-2:]
    dw_ref, go_ref, gs_ref = refs[count : count + 3]
    half = go_ref.shape[0]
    total = tree_sum(ref[...].astype(F32) for ref in refs[:count])
    p = side_ref[0]
    extra = None
    for at, g_ref in ((p, go_ref), (1 - p, gs_ref)):
        dw = dw_ref[:, pl.ds(pl.multiple_of(at * half, half), half)]
        high = dw.astype(BF16)
        low = (dw - high.astype(F32)).astype(BF16)
        g = g_ref[...]
        term = jnp.dot(high, g, preferred_element_type=F32) + jnp.dot(
            low, g, preferred_element_type=F32
        )
        extra = term if extra is None else extra + term
    grad = total + factor * extra
    grad_ref[...] = grad
    squares_ref[...] = fold(grad * grad)


def adam(grad, norm_refs, one, two, moment_one, moment_two, weights):
    squares = jnp.sum(tree_sum(ref[...] for ref in norm_refs))
    norm = jnp.sqrt(jnp.full((1, 1), squares, F32))
    clipped = grad * jnp.minimum(1.0, clip_norm / (norm + 1e-06))
    moment_one = beta_one * moment_one + (1.0 - beta_one) * clipped
    moment_two = beta_two * moment_two + (1.0 - beta_two) * clipped * clipped
    update = moment_one / one / (jnp.sqrt(moment_two / two) + adam_eps)
    return moment_one, moment_two, update, weights - inner_rate * (update + decay_rate * weights)


def outer_step(theta, speed, delta):
    speed = outer_momentum * speed + delta
    return theta - outer_rate * (outer_momentum * speed + delta)


def first_kernel(
    replicas, count, first_ref, correct_ref, grad_ref, m_ref, v_ref, w_ref, outer_ref, vel_ref, *refs
):
    sums = refs[:replicas]
    norms = refs[replicas : replicas + count]
    m_out, v_out, w_out, dw_out, theta_out, total_out, send_out = refs[replicas + count :]
    rows = grad_ref.shape[0] // 2
    first = first_ref[0]
    sends = []
    for frag in range(2):
        part = pl.ds(frag * rows, rows)
        m, v, update, after = adam(
            grad_ref[part, :], norms, correct_ref[0], correct_ref[1], m_ref[frag], v_ref[frag], w_ref[frag]
        )
        m_out[frag] = m
        v_out[frag] = v
        sends.append(update)
        total = tree_sum(ref[frag] for ref in sums)
        total_out[frag] = total
        old = outer_ref[frag]
        theta = outer_step(old, vel_ref[frag], old - total * (1.0 / replicas))
        now = first == frag
        theta_out[frag] = jnp.where(now, theta, old)
        after = jnp.where(now, mixing * theta + (1.0 - mixing) * after, after)
        w_out[frag] = after
        dw_out[part, :] = after.astype(BF16).astype(F32) - w_ref[frag].astype(BF16).astype(F32)
    send_out[...] = jnp.where(first == 0, sends[1], sends[0]).astype(BF16)


def last_kernel(
    replicas, count, first_ref, correct_ref, grad_ref, m_ref, v_ref, w_ref, outer_ref, vel_ref, total_ref, *refs
):
    updates = refs[:replicas]
    norms = refs[replicas : replicas + count]
    outer_out, inner_out = refs[replicas + count :]
    rows = grad_ref.shape[0] // 2
    first = first_ref[0]
    moved = tree_sum(ref[...].astype(F32) for ref in updates)
    for frag in range(2):
        part = pl.ds(frag * rows, rows)
        after = adam(
            grad_ref[part, :], norms, correct_ref[2], correct_ref[3], m_ref[frag], v_ref[frag], w_ref[frag]
        )[3]
        old = outer_ref[frag]
        mean = ((1.0 - inner_rate * decay_rate) * total_ref[frag] - inner_rate * moved) * (1.0 / replicas)
        theta = outer_step(old, vel_ref[frag], old - mean)
        now = first != frag
        outer_out[frag] = jnp.where(now, theta, old)
        inner_out[frag] = jnp.where(now, mixing * theta + (1.0 - mixing) * after, after)


def body(
    inner_weights,
    first_moment,
    second_moment,
    outer_weights,
    outer_velocity,
    tokens,
    targets,
    step_count,
    first_fragment,
):
    weights = inner_weights[0]
    rows, width = weights.shape[1:]
    replicas = lax.axis_size("rep")
    shards = lax.axis_size("shard")
    chips = shards // 2
    toks = tokens.shape[2]
    scale = 1.0 / math.sqrt(width)
    grad_scale = scale / (toks * shards)
    index = lax.axis_index("shard")
    core = index % 2
    chip = index // 2

    def swap(x, axis, size, by):
        return lax.ppermute(x, axis, [(i, i ^ by) for i in range(size)])

    sibling = lambda x: swap(x, "shard", shards, 1)
    across = lambda x, by: swap(x, "shard", shards, 2 * by)
    over_rep = lambda x, by: x if by == 0 else swap(x, "rep", replicas, by)

    shape = jax.ShapeDtypeStruct
    block = shape((2 * rows, width), BF16)
    strip_shape = shape((width // shards, width), BF16)
    tile = shape((8, 128), F32)
    state = shape((2, rows, width), F32)
    flat = shape((2 * rows, width), F32)
    side = jnp.reshape(core, (1,)).astype(jnp.int32)
    place = jnp.stack([chip ^ k for k in range(chips)]).astype(jnp.int32)

    (lowered,) = call(lower_kernel, [block], [], [weights], "lower")
    held = [lowered] + [across(lowered, k) for k in range(1, chips)]

    own_x = [tokens[0, s] for s in range(2)]
    sib_x = [sibling(x) for x in own_x]

    def split(s, after):
        out = shape((chips, toks, 2 * rows), BF16)
        return pl.pallas_call(
            lambda side_ref, goal_ref, after_ref, *outs: split_kernel(rows, side_ref, goal_ref, *outs),
            grid_spec=pltpu.PrefetchScalarGridSpec(
                num_scalar_prefetch=1,
                grid=(1,),
                in_specs=[
                    pl.BlockSpec((None, None, toks, 2, width), lambda i, side: (0, s, 0, 0, 0)),
                    pl.BlockSpec(memory_space=pl.ANY),
                ],
                out_specs=[pl.BlockSpec(out.shape, lambda i, side: (0, 0, 0))] * 2,
            ),
            out_shape=[out, out],
            compiler_params=pltpu.CompilerParams(vmem_limit_bytes=VMEM_BYTES),
            cost_estimate=pl.CostEstimate(flops=0, bytes_accessed=1024, transcendentals=0),
            name="split",
        )(side, targets, after)

    own_t, sib_t = [], []
    after = lowered
    for s in range(2):
        keep, send = split(s, after)
        own_t.append(keep)
        sib_t.append(sibling(send))
        after = keep

    def chunk_grad(s, group, after):
        return call(
            functools.partial(chunk_kernel, scale, grad_scale, group),
            [block] * len(group),
            [place],
            [held[k] for k in group] + [own_x[s], sib_x[s], own_t[s], sib_t[s]],
            "chunk_grad",
            after,
        )

    def spread(made):
        return [made[0]] + [across(made[k], k) for k in range(1, chips)]

    def norm_parts(squares):
        both = squares + sibling(squares)
        return [both] + [across(both, k) for k in range(1, chips)]

    near = list(range(max(1, chips // 2)))
    far = list(range(max(1, chips // 2), chips))
    made = chunk_grad(0, near, [])
    made = made + chunk_grad(0, far, [made[0]])
    pieces_one = spread(made)
    strips = pl.pallas_call(
        lambda side_ref, place_ref, xo, xs, after_ref, *refs: gram_kernel(side_ref, place_ref, xo, xs, *refs),
        in_specs=[pl.BlockSpec(memory_space=pltpu.SMEM)] * 2
        + [pl.BlockSpec(memory_space=pltpu.VMEM)] * 2
        + [pl.BlockSpec(memory_space=pl.ANY)],
        out_specs=[pl.BlockSpec(memory_space=pltpu.VMEM)] * chips,
        out_shape=[strip_shape] * chips,
        scratch_shapes=[pltpu.VMEM((width // 2, width), BF16)],
        compiler_params=pltpu.CompilerParams(vmem_limit_bytes=VMEM_BYTES),
        cost_estimate=pl.CostEstimate(flops=0, bytes_accessed=1024, transcendentals=0),
        name="gram",
    )(side, place, own_x[1], sib_x[1], made[-1])
    strips = spread(strips)
    made = chunk_grad(1, near + far, [strips[0]])
    pieces_two = spread(made)

    sums = [over_rep(weights, k) for k in range(replicas)]

    grad, squares = call(sum_kernel, [flat, tile], [], pieces_one, "sum_pieces")
    norms = norm_parts(squares)

    (strip,) = call(add_kernel, [strip_shape], [], strips, "strip")
    (own_g,) = call(
        gather_kernel,
        [shape((width // 2, width), BF16)],
        [place],
        [strip] + [across(strip, k) for k in range(1, chips)],
        "gather_strips",
    )
    sib_g = sibling(own_g)

    count = step_count[0].astype(F32)
    correct = jnp.stack(
        [1.0 - jnp.power(beta, count + s) for s in range(2) for beta in (beta_one, beta_two)]
    )
    m, v, middle, change, outer, total, moved = call(
        functools.partial(first_kernel, replicas, chips),
        [state, state, state, flat, state, state, shape((rows, width), BF16)],
        [first_fragment, correct],
        [grad, first_moment[0], second_moment[0], weights, outer_weights, outer_velocity, *sums, *norms],
        "first_update",
    )
    updates = [over_rep(moved, k) for k in range(replicas)]

    grad, squares = call(
        functools.partial(correct_kernel, chips, scale * grad_scale),
        [flat, tile],
        [side],
        [*pieces_two, change, own_g, sib_g],
        "corrected",
    )
    norms = norm_parts(squares)
    new_outer, new_inner = call(
        functools.partial(last_kernel, replicas, chips),
        [state, state],
        [first_fragment, correct],
        [grad, m, v, middle, outer, outer_velocity, total, *updates, *norms],
        "last_update",
    )
    return (new_outer, new_inner[None])


def solution(mesh):
    in_specs = (
        P("rep", None, "shard", None),
        P("rep", None, "shard", None),
        P("rep", None, "shard", None),
        P(None, "shard", None),
        P(None, "shard", None),
        P("rep", None, "shard", None),
        P("rep", None, "shard", None, None),
        P(),
        P(),
    )
    out_specs = (P(None, "shard", None), P("rep", None, "shard", None))
    return jax.shard_map(body, mesh=mesh, in_specs=in_specs, out_specs=out_specs, check_vma=False)
```

time: 128 us -> 94.2 us (0.74)
  local copies, waits for them, and re-layouts: 24.9 us -> 2.91 us
  Pallas kernels: 34.3 us -> 15.9 us
  waiting for transfers between devices: 23.3 us -> 30.8 us
  other arithmetic: 2.3 us -> 0.16 us
  starting transfers between devices: 40.3 us -> 41.9 us
    pallas_call x13, Pallas kernels: 34.3 us -> 15.9 us  [the longest x10 11 us: call(): pl.pallas_call(run, in_specs=[pl.BlockSpec(memory_space=pltpu.SMEM)] * le...]
    unnamed x80 -> x16, local copies, waits for them, and re-layouts: 10.7 us -> 0.69 us
    ppermute x34, waiting for transfers between devices: 23.3 us -> 30.8 us  [swap(): return lax.ppermute(x, axis, [(i, i ^ by) for i in range(size)])]
    reshape x4 -> x0, local copies, waits for them, and re-layouts: 4.08 us -> none  [body(): arrange = lambda y: y.transpose(2, 0, 1, 3).reshape(chips, toks, 2 * rows)]
    transpose x5 -> x0, local copies, waits for them, and re-layouts: 3.66 us -> none  [body(): arrange = lambda y: y.transpose(2, 0, 1, 3).reshape(chips, toks, 2 * rows)]
    slice x1 -> x0, local copies, waits for them, and re-layouts: 3.63 us -> none  [body(): goal = targets[0, s].reshape(toks, 2, chips, 2, rows)]
    ppermute x34, starting transfers between devices: 40.3 us -> 41.9 us  [swap(): return lax.ppermute(x, axis, [(i, i ^ by) for i in range(size)])]
    squeeze x1 -> x0, local copies, waits for them, and re-layouts: 1.58 us -> none  [body(): lax.dynamic_index_in_dim(half, chip ^ k, 0, keepdims=False)]
  transfers between devices with their start and end apart: 34 -> 34, of which waited for: 10 -> 12; matrix products, arithmetic and copies ran while one was open for 17% -> 0% of each run, Pallas kernels for 25% -> 15%
where the time goes in v2:
time: 94.2 us; the launch traced here: 94 us
  starting transfers between devices  41.9 us (44%)
  waiting for transfers between devices  30.8 us (33%)
  Pallas kernels  15.9 us (17%)
  local copies, waits for them, and re-layouts  2.91 us (3%)
  between operations  2.36 us (3%)
    ppermute x34, starting transfers between devices, swap(): return lax.ppermute(x, axis, [(i, i ^ by) for i in range(size)])  41.9 us
    ppermute x34, waiting for transfers between devices, swap(): return lax.ppermute(x, axis, [(i, i ^ by) for i in range(size)])  30.8 us
    pallas_call x10, Pallas kernels, call(): pl.pallas_call(run, in_specs=[pl.BlockSpec(memory_space=pltpu.SMEM)] * le...  11 us
    pallas_call x2, Pallas kernels, split(): pl.pallas_call(lambda side_ref, goal_ref, after_ref, *outs: split_kernel(...  3.17 us
    squeeze x1, local copies, waits for them, and re-layouts, body(): own_x = [tokens[0, s] for s in range(2)]  2.21 us
  transfers between devices with their start and end apart: 34, of which 12 were waited for; matrix products, arithmetic and copies ran while one was open for 0% of the time, Pallas kernels for 15%

profile of v2, /device:TPU:0, one launch (start us, length us, event | category | flops | bytes accessed | tf_op | source)
XLA Modules:
  0.0 94.0 jit_solution(8276942382170350238)
XLA Ops:
  0.6 2.2 %slice_bitcast_fusion = (bf16[512,512]{1,0:T(8,128)(2,1)S(1)}, bf16[512,512]{1,0:T(8,128)(2,1)}) fusion(bf16[1,2,512,512]{3,2,1,0:T(8,128)(2,1)} %param.14), kind=kLoop, calls=%fused_computation | loop fusion | bytes 2097152 | tf_op jit(solution)/shard_map/squeeze | solution.py:274
  2.9 0.5 collective-permute-start.5
  3.4 2.0 %split.2 = (bf16[4,512,128]{2,1,0:T(8,128)(2,1)S(1)}, bf16[4,512,128]{2,1,0:T(8,128)(2,1)}) custom-call(s32[1]{0:T(128)} %bitcast.side_ref.refs_0_, bf16[1,2,512,2,512]{4,3,2,1,0:T(2,128)(2,1)S(1)} %copy-done, bf16[128,512]{1,0:T(8,128)(2,1)S(1)} %lower.1.after_ref.refs_1_), custom_call_target="tpu_custom_call" | custom-call | bytes 1024 | tf_op jit(solution)/shard_map/split/pallas_call | solution.py:279
  5.4 0.4 collective-permute-start.3
  5.8 2.6 %collective-permute-start = (bf16[128,512]{1,0:T(8,128)(2,1)S(1)}, bf16[128,512]{1,0:T(8,128)(2,1)S(1)}, u32[]{:S(2)}, u32[]{:S(2)}) collective-permute-start(bf16[128,512]{1,0:T(8,128)(2,1)S(1)} %lower.1.after_ref.refs_1_), channel_id=1, source_target_pairs={{0,2},{1,3},{2,0},{3,1},{4,6},{5,7},{6,4},{7,5},{8,10},{9,11},{10,... | collective-permute-start | bytes 393224 | tf_op jit(solution)/shard_map/ppermute | solution.py:256
  8.4 2.6 %collective-permute-start.1 = (bf16[128,512]{1,0:T(8,128)(2,1)S(1)}, bf16[128,512]{1,0:T(8,128)(2,1)}, u32[]{:S(2)}, u32[]{:S(2)}) collective-permute-start(bf16[128,512]{1,0:T(8,128)(2,1)S(1)} %lower.1.after_ref.refs_1_), channel_id=1, source_target_pairs={{0,4},{1,5},{2,6},{3,7},{4,0},{5,1},{6,2},{7,3},{8,12},{9,13},{10,... | collective-permute-start | bytes 393224 | tf_op jit(solution)/shard_map/ppermute | solution.py:256
  11.0 4.2 %collective-permute-done.refs_2_ = bf16[128,512]{1,0:T(8,128)(2,1)S(1)} collective-permute-done((bf16[128,512]{1,0:T(8,128)(2,1)S(1)}, bf16[128,512]{1,0:T(8,128)(2,1)S(1)}, u32[]{:S(2)}, u32[]{:S(2)}) %collective-permute-start) | collective-permute-done | bytes 131104 | tf_op jit(solution)/shard_map/ppermute | solution.py:256
  15.2 0.7 copy-done.3
  15.9 2.7 %collective-permute-start.2 = (bf16[128,512]{1,0:T(8,128)(2,1)S(1)}, bf16[128,512]{1,0:T(8,128)(2,1)}, u32[]{:S(2)}, u32[]{:S(2)}) collective-permute-start(bf16[128,512]{1,0:T(8,128)(2,1)S(1)} %lower.1.after_ref.refs_1_), channel_id=1, source_target_pairs={{0,6},{1,7},{2,4},{3,5},{4,2},{5,3},{6,0},{7,1},{8,14},{9,15},{10,... | collective-permute-start | bytes 393224 | tf_op jit(solution)/shard_map/ppermute | solution.py:256
  18.6 1.2 %split.3 = (bf16[4,512,128]{2,1,0:T(8,128)(2,1)S(1)}, bf16[4,512,128]{2,1,0:T(8,128)(2,1)S(1)}) custom-call(s32[1]{0:T(128)} %bitcast.side_ref.refs_0_, bf16[1,2,512,2,512]{4,3,2,1,0:T(2,128)(2,1)S(1)} %copy-done, bf16[4,512,128]{2,1,0:T(8,128)(2,1)S(1)} %get-tuple-element.31.after_ref.refs_5_), custom_call_target="tpu_custom_call" | custom-call | bytes 1024 | tf_op jit(solution)/shard_map/split/pallas_call | solution.py:279
  20.0 2.1 %chunk_grad.3 = (bf16[128,512]{1,0:T(8,128)(2,1)S(1)}, bf16[128,512]{1,0:T(8,128)(2,1)S(1)}) custom-call(s32[4]{0:T(128)S(1)} %pad_add_fusion.refs_0_.place_ref, bf16[128,512]{1,0:T(8,128)(2,1)S(1)} %lower.1.after_ref.refs_1_, bf16[128,512]{1,0:T(8,128)(2,1)S(1)} %copy-done.4, bf16[512,512]{1,0:T(8,128)(2,1)S(1)} %get-tuple-element.60.refs_3_, ...), custom_call_target="tpu_custom_call" | custom-call | bytes 1024 | tf_op jit(solution)/shard_map/chunk_grad/pallas_call | solution.py:48
  22.1 1.1 %collective-permute-done.2.refs_2_.refs_4_ = bf16[128,512]{1,0:T(8,128)(2,1)} collective-permute-done((bf16[128,512]{1,0:T(8,128)(2,1)S(1)}, bf16[128,512]{1,0:T(8,128)(2,1)}, u32[]{:S(2)}, u32[]{:S(2)}) %collective-permute-start.2) | collective-permute-done | bytes 131104 | tf_op jit(solution)/shard_map/ppermute | solution.py:256
  23.1 2.2 %chunk_grad.4 = (bf16[128,512]{1,0:T(8,128)(2,1)S(1)}, bf16[128,512]{1,0:T(8,128)(2,1)S(1)}) custom-call(s32[4]{0:T(128)S(1)} %pad_add_fusion.refs_0_.place_ref, bf16[128,512]{1,0:T(8,128)(2,1)} %collective-permute-done.1.refs_1_.refs_3_, bf16[128,512]{1,0:T(8,128)(2,1)} %collective-permute-done.2.refs_2_.refs_4_, ...), custom_call_target="tpu_custom_call" | custom-call | bytes 1024 | tf_op jit(solution)/shard_map/chunk_grad/pallas_call | solution.py:48
  25.3 1.7 %gram.1 = (bf16[64,512]{1,0:T(8,128)(2,1)S(1)}, bf16[64,512]{1,0:T(8,128)(2,1)S(1)}, bf16[64,512]{1,0:T(8,128)(2,1)S(1)}, bf16[64,512]{1,0:T(8,128)(2,1)S(1)}) custom-call(s32[1]{0:T(128)} %bitcast.side_ref.refs_0_, s32[4]{0:T(128)S(1)} %pad_add_fusion.refs_0_.place_ref, bf16[512,512]{1,0:T(8,128)(2,1)} %get-tuple-element.61.xo.refs_5_, ...), custom_call_target="tpu_custom_call" | custom-call | bytes 1024 | tf_op jit(solution)/shard_map/gram/pallas_call | solution.py:326
  27.1 1.0 %collective-permute-start.20 = (bf16[64,512]{1,0:T(8,128)(2,1)S(1)}, bf16[64,512]{1,0:T(8,128)(2,1)S(1)}, u32[]{:S(2)}, u32[]{:S(2)}) collective-permute-start(bf16[64,512]{1,0:T(8,128)(2,1)S(1)} %get-tuple-element.47), channel_id=1, source_target_pairs={{0,2},{1,3},{2,0},{3,1},{4,6},{5,7},{6,4},{7,5},{8,10},{9,11},{10,... | collective-permute-start | bytes 196616 | tf_op jit(solution)/shard_map/ppermute | solution.py:256
  28.1 2.3 %collective-permute-start.21 = (bf16[64,512]{1,0:T(8,128)(2,1)S(1)}, bf16[64,512]{1,0:T(8,128)(2,1)S(1)}, u32[]{:S(2)}, u32[]{:S(2)}) collective-permute-start(bf16[64,512]{1,0:T(8,128)(2,1)S(1)} %get-tuple-element.48), channel_id=1, source_target_pairs={{0,4},{1,5},{2,6},{3,7},{4,0},{5,1},{6,2},{7,3},{8,12},{9,13},{10,... | collective-permute-start | bytes 196616 | tf_op jit(solution)/shard_map/ppermute | solution.py:256
  30.4 1.1 %collective-permute-start.22 = (bf16[64,512]{1,0:T(8,128)(2,1)S(1)}, bf16[64,512]{1,0:T(8,128)(2,1)S(1)}, u32[]{:S(2)}, u32[]{:S(2)}) collective-permute-start(bf16[64,512]{1,0:T(8,128)(2,1)S(1)} %get-tuple-element.49), channel_id=1, source_target_pairs={{0,6},{1,7},{2,4},{3,5},{4,2},{5,3},{6,0},{7,1},{8,14},{9,15},{10,... | collective-permute-start | bytes 196616 | tf_op jit(solution)/shard_map/ppermute | solution.py:256
  31.6 3.1 %collective-permute-done.21.refs_2_ = bf16[64,512]{1,0:T(8,128)(2,1)S(1)} collective-permute-done((bf16[64,512]{1,0:T(8,128)(2,1)S(1)}, bf16[64,512]{1,0:T(8,128)(2,1)S(1)}, u32[]{:S(2)}, u32[]{:S(2)}) %collective-permute-start.21) | collective-permute-done | bytes 65568 | tf_op jit(solution)/shard_map/ppermute | solution.py:256
  34.7 2.0 %collective-permute-done.22.refs_3_ = bf16[64,512]{1,0:T(8,128)(2,1)S(1)} collective-permute-done((bf16[64,512]{1,0:T(8,128)(2,1)S(1)}, bf16[64,512]{1,0:T(8,128)(2,1)S(1)}, u32[]{:S(2)}, u32[]{:S(2)}) %collective-permute-start.22) | collective-permute-done | bytes 65568 | tf_op jit(solution)/shard_map/ppermute | solution.py:256
  36.8 2.0 %collective-permute-start.10 = (bf16[128,512]{1,0:T(8,128)(2,1)S(1)}, bf16[128,512]{1,0:T(8,128)(2,1)S(1)}, u32[]{:S(2)}, u32[]{:S(2)}) collective-permute-start(bf16[128,512]{1,0:T(8,128)(2,1)S(1)} %get-tuple-element.42), channel_id=1, source_target_pairs={{0,2},{1,3},{2,0},{3,1},{4,6},{5,7},{6,4},{7,5},{8,10},{9,11},{10,... | collective-permute-start | bytes 393224 | tf_op jit(solution)/shard_map/ppermute | solution.py:256
  38.8 0.8 collective-permute-start.11
  39.6 2.1 %collective-permute-start.24 = (bf16[64,512]{1,0:T(8,128)(2,1)S(1)}, bf16[64,512]{1,0:T(8,128)(2,1)S(1)}, u32[]{:S(2)}, u32[]{:S(2)}) collective-permute-start(bf16[64,512]{1,0:T(8,128)(2,1)S(1)} %strip.1.refs_1_), channel_id=1, source_target_pairs={{0,4},{1,5},{2,6},{3,7},{4,0},{5,1},{6,2},{7,3},{8,12},{9,13},{10,... | collective-permute-start | bytes 196616 | tf_op jit(solution)/shard_map/ppermute | solution.py:256
  41.8 1.4 %collective-permute-start.25 = (bf16[64,512]{1,0:T(8,128)(2,1)S(1)}, bf16[64,512]{1,0:T(8,128)(2,1)S(1)}, u32[]{:S(2)}, u32[]{:S(2)}) collective-permute-start(bf16[64,512]{1,0:T(8,128)(2,1)S(1)} %strip.1.refs_1_), channel_id=1, source_target_pairs={{0,6},{1,7},{2,4},{3,5},{4,2},{5,3},{6,0},{7,1},{8,14},{9,15},{10,... | collective-permute-start | bytes 196616 | tf_op jit(solution)/shard_map/ppermute | solution.py:256
  43.2 6.6 %collective-permute-done.24.refs_3_ = bf16[64,512]{1,0:T(8,128)(2,1)S(1)} collective-permute-done((bf16[64,512]{1,0:T(8,128)(2,1)S(1)}, bf16[64,512]{1,0:T(8,128)(2,1)S(1)}, u32[]{:S(2)}, u32[]{:S(2)}) %collective-permute-start.24) | collective-permute-done | bytes 65568 | tf_op jit(solution)/shard_map/ppermute | solution.py:256
  49.8 1.5 %collective-permute-start.13 = (f32[2,64,512]{2,1,0:T(8,128)S(1)}, f32[2,64,512]{2,1,0:T(8,128)S(1)}, u32[]{:S(2)}, u32[]{:S(2)}) collective-permute-start(f32[2,64,512]{2,1,0:T(8,128)S(1)} %bitcast.14), channel_id=1, source_target_pairs={{0,8},{8,0},{16,24},{24,16},{1,9},{9,1},{17,25},{25,17},{2,10},{10... | collective-permute-start | bytes 786440 | tf_op jit(solution)/shard_map/ppermute | solution.py:256
  51.3 1.6 %collective-permute-start.14 = (f32[2,64,512]{2,1,0:T(8,128)S(1)}, f32[2,64,512]{2,1,0:T(8,128)S(1)}, u32[]{:S(2)}, u32[]{:S(2)}) collective-permute-start(f32[2,64,512]{2,1,0:T(8,128)S(1)} %bitcast.15), channel_id=1, source_target_pairs={{0,16},{8,24},{16,0},{24,8},{1,17},{9,25},{17,1},{25,9},{2,18},{10... | collective-permute-start | bytes 786440 | tf_op jit(solution)/shard_map/ppermute | solution.py:256
  52.9 0.4 collective-permute-start.15
  53.3 1.2 %collective-permute-start.12 = (bf16[128,512]{1,0:T(8,128)(2,1)S(1)}, bf16[128,512]{1,0:T(8,128)(2,1)S(1)}, u32[]{:S(2)}, u32[]{:S(2)}) collective-permute-start(bf16[128,512]{1,0:T(8,128)(2,1)S(1)} %get-tuple-element.36.after_ref), channel_id=1, source_target_pairs={{0,6},{1,7},{2,4},{3,5},{4,2},{5,3},{6,0},{7,1},{8,14},{9,15},{10,... | collective-permute-start | bytes 393224 | tf_op jit(solution)/shard_map/ppermute | solution.py:256
  54.5 0.6 gather_strips.1.refs_6_
  55.1 5.0 %collective-permute-done.12.refs_3_ = bf16[128,512]{1,0:T(8,128)(2,1)S(1)} collective-permute-done((bf16[128,512]{1,0:T(8,128)(2,1)S(1)}, bf16[128,512]{1,0:T(8,128)(2,1)S(1)}, u32[]{:S(2)}, u32[]{:S(2)}) %collective-permute-start.12) | collective-permute-done | bytes 131104 | tf_op jit(solution)/shard_map/ppermute | solution.py:256
  60.2 0.6 collective-permute-start.16
  60.8 2.8 %chunk_grad.5 = (bf16[128,512]{1,0:T(8,128)(2,1)S(1)}, bf16[128,512]{1,0:T(8,128)(2,1)S(1)}, bf16[128,512]{1,0:T(8,128)(2,1)S(1)}, bf16[128,512]{1,0:T(8,128)(2,1)S(1)}) custom-call(s32[4]{0:T(128)S(1)} %pad_add_fusion.refs_0_.place_ref, bf16[128,512]{1,0:T(8,128)(2,1)S(1)} %lower.1.after_ref.refs_1_, bf16[128,512]{1,0:T(8,128)(2,1)S(1)} %copy-done.4, ...), custom_call_target="tpu_custom_call" | custom-call | bytes 1024 | tf_op jit(solution)/shard_map/chunk_grad/pallas_call | solution.py:48
  63.7 1.7 %collective-permute-start.8 = (bf16[128,512]{1,0:T(8,128)(2,1)S(1)}, bf16[128,512]{1,0:T(8,128)(2,1)S(1)}, u32[]{:S(2)}, u32[]{:S(2)}) collective-permute-start(bf16[128,512]{1,0:T(8,128)(2,1)S(1)} %get-tuple-element.40), channel_id=1, source_target_pairs={{0,4},{1,5},{2,6},{3,7},{4,0},{5,1},{6,2},{7,3},{8,12},{9,13},{10,... | collective-permute-start | bytes 393224 | tf_op jit(solution)/shard_map/ppermute | solution.py:256
  65.7 2.8 %collective-permute-start.18 = (f32[8,128]{1,0:T(8,128)S(1)}, f32[8,128]{1,0:T(8,128)S(1)}, u32[]{:S(2)}, u32[]{:S(2)}) collective-permute-start(f32[8,128]{1,0:T(8,128)S(1)} %add.18.refs_12_), channel_id=1, source_target_pairs={{0,4},{1,5},{2,6},{3,7},{4,0},{5,1},{6,2},{7,3},{8,12},{9,13},{10,... | collective-permute-start | bytes 12296 | tf_op jit(solution)/shard_map/ppermute | solution.py:256
  69.4 1.0 %collective-permute-done.17.refs_13_ = f32[8,128]{1,0:T(8,128)S(1)} collective-permute-done((f32[8,128]{1,0:T(8,128)S(1)}, f32[8,128]{1,0:T(8,128)S(1)}, u32[]{:S(2)}, u32[]{:S(2)}) %collective-permute-start.17) | collective-permute-done | bytes 4128 | tf_op jit(solution)/shard_map/ppermute | solution.py:256
  70.5 2.4 %collective-permute-start.9 = (bf16[128,512]{1,0:T(8,128)(2,1)S(1)}, bf16[128,512]{1,0:T(8,128)(2,1)S(1)}, u32[]{:S(2)}, u32[]{:S(2)}) collective-permute-start(bf16[128,512]{1,0:T(8,128)(2,1)S(1)} %get-tuple-element.41), channel_id=1, source_target_pairs={{0,6},{1,7},{2,4},{3,5},{4,2},{5,3},{6,0},{7,1},{8,14},{9,15},{10,... | collective-permute-start | bytes 393224 | tf_op jit(solution)/shard_map/ppermute | solution.py:256
  73.1 1.4 %collective-permute-start.19 = (f32[8,128]{1,0:T(8,128)S(1)}, f32[8,128]{1,0:T(8,128)S(1)}, u32[]{:S(2)}, u32[]{:S(2)}) collective-permute-start(f32[8,128]{1,0:T(8,128)S(1)} %add.18.refs_12_), channel_id=1, source_target_pairs={{0,6},{1,7},{2,4},{3,5},{4,2},{5,3},{6,0},{7,1},{8,14},{9,15},{10,... | collective-permute-start | bytes 12296 | tf_op jit(solution)/shard_map/ppermute | solution.py:256
  75.2 3.4 %collective-permute-done.19.refs_15_ = f32[8,128]{1,0:T(8,128)S(1)} collective-permute-done((f32[8,128]{1,0:T(8,128)S(1)}, f32[8,128]{1,0:T(8,128)S(1)}, u32[]{:S(2)}, u32[]{:S(2)}) %collective-permute-start.19) | collective-permute-done | bytes 4128 | tf_op jit(solution)/shard_map/ppermute | solution.py:256
  78.6 1.1 %first_update.1 = (f32[2,64,512]{2,1,0:T(8,128)S(1)}, f32[2,64,512]{2,1,0:T(8,128)S(1)}, f32[2,64,512]{2,1,0:T(8,128)S(1)}, f32[128,512]{1,0:T(8,128)S(1)}, f32[...) custom-call(s32[1]{0:T(128)S(6)} %copy.12.refs_0_, f32[4]{0:T(128)S(1)} %pad_maximum_fusion.refs_1_, ...), custom_call_target="tpu_custom_call" | custom-call | bytes 1024 | tf_op jit(solution)/shard_map/first_update/pallas_call | solution.py:48
  79.7 1.5 %collective-permute-start.27 = (bf16[64,512]{1,0:T(8,128)(2,1)S(1)}, bf16[64,512]{1,0:T(8,128)(2,1)S(1)}, u32[]{:S(2)}, u32[]{:S(2)}) collective-permute-start(bf16[64,512]{1,0:T(8,128)(2,1)S(1)} %get-tuple-element.56.refs_9_), channel_id=1, source_target_pairs={{0,8},{8,0},{16,24},{24,16},{1,9},{9,1},{17,25},{25,17},{2,10},{10... | collective-permute-start | bytes 196616 | tf_op jit(solution)/shard_map/ppermute | solution.py:256
  81.3 1.6 %collective-permute-start.28 = (bf16[64,512]{1,0:T(8,128)(2,1)S(1)}, bf16[64,512]{1,0:T(8,128)(2,1)S(1)}, u32[]{:S(2)}, u32[]{:S(2)}) collective-permute-start(bf16[64,512]{1,0:T(8,128)(2,1)S(1)} %get-tuple-element.56.refs_9_), channel_id=1, source_target_pairs={{0,16},{8,24},{16,0},{24,8},{1,17},{9,25},{17,1},{25,9},{2,18},{10... | collective-permute-start | bytes 196616 | tf_op jit(solution)/shard_map/ppermute | solution.py:256
  82.9 0.4 collective-permute-start.29
  83.7 1.2 %collective-permute-done.30 = f32[8,128]{1,0:T(8,128)S(1)} collective-permute-done((f32[8,128]{1,0:T(8,128)S(1)}, f32[8,128]{1,0:T(8,128)S(1)}, u32[]{:S(2)}, u32[]{:S(2)}) %collective-permute-start.30) | collective-permute-done | bytes 4128 | tf_op jit(solution)/shard_map/ppermute | solution.py:256
  84.9 1.6 %collective-permute-start.31 = (f32[8,128]{1,0:T(8,128)S(1)}, f32[8,128]{1,0:T(8,128)S(1)}, u32[]{:S(2)}, u32[]{:S(2)}) collective-permute-start(f32[8,128]{1,0:T(8,128)S(1)} %add.19.refs_13_), channel_id=1, source_target_pairs={{0,2},{1,3},{2,0},{3,1},{4,6},{5,7},{6,4},{7,5},{8,10},{9,11},{10,... | collective-permute-start | bytes 12296 | tf_op jit(solution)/shard_map/ppermute | solution.py:256
  86.7 2.5 %collective-permute-start.33 = (f32[8,128]{1,0:T(8,128)S(1)}, f32[8,128]{1,0:T(8,128)S(1)}, u32[]{:S(2)}, u32[]{:S(2)}) collective-permute-start(f32[8,128]{1,0:T(8,128)S(1)} %add.19.refs_13_), channel_id=1, source_target_pairs={{0,6},{1,7},{2,4},{3,5},{4,2},{5,3},{6,0},{7,1},{8,14},{9,15},{10,... | collective-permute-start | bytes 12296 | tf_op jit(solution)/shard_map/ppermute | solution.py:256
  89.3 1.7 %collective-permute-done.32.refs_15_ = f32[8,128]{1,0:T(8,128)S(1)} collective-permute-done((f32[8,128]{1,0:T(8,128)S(1)}, f32[8,128]{1,0:T(8,128)S(1)}, u32[]{:S(2)}, u32[]{:S(2)}) %collective-permute-start.32) | collective-permute-done | bytes 4128 | tf_op jit(solution)/shard_map/ppermute | solution.py:256
  91.0 1.2 %collective-permute-done.33.refs_16_ = f32[8,128]{1,0:T(8,128)S(1)} collective-permute-done((f32[8,128]{1,0:T(8,128)S(1)}, f32[8,128]{1,0:T(8,128)S(1)}, u32[]{:S(2)}, u32[]{:S(2)}) %collective-permute-start.33) | collective-permute-done | bytes 4128 | tf_op jit(solution)/shard_map/ppermute | solution.py:256
  92.1 1.8 %last_update.1 = (f32[2,64,512]{2,1,0:T(8,128)}, f32[2,64,512]{2,1,0:T(8,128)}) custom-call(s32[1]{0:T(128)S(6)} %copy.12.refs_0_, f32[4]{0:T(128)S(1)} %pad_maximum_fusion.refs_1_, f32[128,512]{1,0:T(8,128)S(1)} %get-tuple-element.50.refs_2_, f32[2,64,512]{2,1,0:T(8,128)S(1)} %get-tuple-element.51.refs_3_, f32[2,64,512]{2,1,0:T(8,128)S(1)} %get-tuple-element.52.refs_4_, ...), custom_call_target="tpu_custom_call" | custom-call | bytes 1024 | tf_op jit(solution)/shard_map/last_update/pallas_call | solution.py:48
  (54 shorter events, 1.9 us)
Async XLA Ops:
  0.6 2.7 %copy-start.1 = (f32[1,2,64,512]{3,2,1,0:T(8,128)S(1)}, f32[1,2,64,512]{3,2,1,0:T(8,128)}, u32[]{:S(2)}) copy-start(f32[1,2,64,512]{3,2,1,0:T(8,128)} %param.9) | copy-start | bytes 786436
  0.6 2.7 %copy-start = (bf16[1,2,512,2,512]{4,3,2,1,0:T(2,128)(2,1)S(1)}, bf16[1,2,512,2,512]{4,3,2,1,0:T(2,128)(2,1)}, u32[]{:S(2)}) copy-start(bf16[1,2,512,2,512]{4,3,2,1,0:T(2,128)(2,1)} %goal_ref.3) | copy-start | bytes 6291460
  2.9 16.9 %collective-permute-start.5 = (bf16[512,512]{1,0:T(8,128)(2,1)S(1)}, bf16[512,512]{1,0:T(8,128)(2,1)}, u32[]{:S(2)}, u32[]{:S(2)}) collective-permute-start(bf16[512,512]{1,0:T(8,128)(2,1)S(1)} %get-tuple-element.60.refs_3_), channel_id=1, source_target_pairs={{0,1},{1,0},{2,3},{3,2},{4,5},{5,4},{6,7},{7,6},{8,9},{9,8},{10,11... | collective-permute-start | bytes 1572872 | tf_op jit(solution)/shard_map/ppermute | solution.py:256
  5.3 14.6 %collective-permute-start.6 = (bf16[4,512,128]{2,1,0:T(8,128)(2,1)}, bf16[4,512,128]{2,1,0:T(8,128)(2,1)}, u32[]{:S(2)}, u32[]{:S(2)}) collective-permute-start(bf16[4,512,128]{2,1,0:T(8,128)(2,1)} %get-tuple-element.34), channel_id=1, source_target_pairs={{0,1},{1,0},{2,3},{3,2},{4,5},{5,4},{6,7},{7,6},{8,9},{9,8},{10,11... | collective-permute-start | bytes 1572872 | tf_op jit(solution)/shard_map/ppermute | solution.py:256
  5.4 19.9 %collective-permute-start.3 = (bf16[512,512]{1,0:T(8,128)(2,1)}, bf16[512,512]{1,0:T(8,128)(2,1)}, u32[]{:S(2)}, u32[]{:S(2)}) collective-permute-start(bf16[512,512]{1,0:T(8,128)(2,1)} %get-tuple-element.61.xo.refs_5_), channel_id=1, source_target_pairs={{0,1},{1,0},{2,3},{3,2},{4,5},{5,4},{6,7},{7,6},{8,9},{9,8},{10,11... | collective-permute-start | bytes 1572872 | tf_op jit(solution)/shard_map/ppermute | solution.py:256
  5.8 9.4 %collective-permute-start = (bf16[128,512]{1,0:T(8,128)(2,1)S(1)}, bf16[128,512]{1,0:T(8,128)(2,1)S(1)}, u32[]{:S(2)}, u32[]{:S(2)}) collective-permute-start(bf16[128,512]{1,0:T(8,128)(2,1)S(1)} %lower.1.after_ref.refs_1_), channel_id=1, source_target_pairs={{0,2},{1,3},{2,0},{3,1},{4,6},{5,7},{6,4},{7,5},{8,10},{9,11},{10,... | collective-permute-start | bytes 393224 | tf_op jit(solution)/shard_map/ppermute | solution.py:256
  8.4 13.6 %collective-permute-start.1 = (bf16[128,512]{1,0:T(8,128)(2,1)S(1)}, bf16[128,512]{1,0:T(8,128)(2,1)}, u32[]{:S(2)}, u32[]{:S(2)}) collective-permute-start(bf16[128,512]{1,0:T(8,128)(2,1)S(1)} %lower.1.after_ref.refs_1_), channel_id=1, source_target_pairs={{0,4},{1,5},{2,6},{3,7},{4,0},{5,1},{6,2},{7,3},{8,12},{9,13},{10,... | collective-permute-start | bytes 393224 | tf_op jit(solution)/shard_map/ppermute | solution.py:256
  15.2 0.7 copy-start.3
  15.9 7.2 %collective-permute-start.2 = (bf16[128,512]{1,0:T(8,128)(2,1)S(1)}, bf16[128,512]{1,0:T(8,128)(2,1)}, u32[]{:S(2)}, u32[]{:S(2)}) collective-permute-start(bf16[128,512]{1,0:T(8,128)(2,1)S(1)} %lower.1.after_ref.refs_1_), channel_id=1, source_target_pairs={{0,6},{1,7},{2,4},{3,5},{4,2},{5,3},{6,0},{7,1},{8,14},{9,15},{10,... | collective-permute-start | bytes 393224 | tf_op jit(solution)/shard_map/ppermute | solution.py:256
  18.6 1.4 %copy-start.4 = (bf16[128,512]{1,0:T(8,128)(2,1)S(1)}, bf16[128,512]{1,0:T(8,128)(2,1)}, u32[]{:S(2)}) copy-start(bf16[128,512]{1,0:T(8,128)(2,1)} %copy-done.3) | copy-start | bytes 393220
  19.8 40.4 %collective-permute-start.4 = (bf16[4,512,128]{2,1,0:T(8,128)(2,1)S(1)}, bf16[4,512,128]{2,1,0:T(8,128)(2,1)S(1)}, u32[]{:S(2)}, u32[]{:S(2)}) collective-permute-start(bf16[4,512,128]{2,1,0:T(8,128)(2,1)S(1)} %get-tuple-element.33), channel_id=1, source_target_pairs={{0,1},{1,0},{2,3},{3,2},{4,5},{5,4},{6,7},{7,6},{8,9},{9,8},{10,11... | collective-permute-start | bytes 1572872 | tf_op jit(solution)/shard_map/ppermute | solution.py:256
  27.0 51.5 %copy-start.2 = (f32[2,64,512]{2,1,0:T(8,128)S(1)}, f32[2,64,512]{2,1,0:T(8,128)}, u32[]{:S(2)}) copy-start(f32[2,64,512]{2,1,0:T(8,128)} %refs_7_.3) | copy-start | bytes 786436
  27.1 51.5 %copy-start.5 = (f32[1,2,64,512]{3,2,1,0:T(8,128)S(1)}, f32[1,2,64,512]{3,2,1,0:T(8,128)}, u32[]{:S(2)}) copy-start(f32[1,2,64,512]{3,2,1,0:T(8,128)} %param.10) | copy-start | bytes 786436
  27.1 51.5 %copy-start.6 = (f32[1,2,64,512]{3,2,1,0:T(8,128)S(1)}, f32[1,2,64,512]{3,2,1,0:T(8,128)}, u32[]{:S(2)}) copy-start(f32[1,2,64,512]{3,2,1,0:T(8,128)} %param.11) | copy-start | bytes 786436
  27.1 51.5 %copy-start.7 = (f32[2,64,512]{2,1,0:T(8,128)S(1)}, f32[2,64,512]{2,1,0:T(8,128)}, u32[]{:S(2)}) copy-start(f32[2,64,512]{2,1,0:T(8,128)} %refs_6_.1) | copy-start | bytes 786436
  27.1 4.5 %collective-permute-start.20 = (bf16[64,512]{1,0:T(8,128)(2,1)S(1)}, bf16[64,512]{1,0:T(8,128)(2,1)S(1)}, u32[]{:S(2)}, u32[]{:S(2)}) collective-permute-start(bf16[64,512]{1,0:T(8,128)(2,1)S(1)} %get-tuple-element.47), channel_id=1, source_target_pairs={{0,2},{1,3},{2,0},{3,1},{4,6},{5,7},{6,4},{7,5},{8,10},{9,11},{10,... | collective-permute-start | bytes 196616 | tf_op jit(solution)/shard_map/ppermute | solution.py:256
  28.1 6.6 %collective-permute-start.21 = (bf16[64,512]{1,0:T(8,128)(2,1)S(1)}, bf16[64,512]{1,0:T(8,128)(2,1)S(1)}, u32[]{:S(2)}, u32[]{:S(2)}) collective-permute-start(bf16[64,512]{1,0:T(8,128)(2,1)S(1)} %get-tuple-element.48), channel_id=1, source_target_pairs={{0,4},{1,5},{2,6},{3,7},{4,0},{5,1},{6,2},{7,3},{8,12},{9,13},{10,... | collective-permute-start | bytes 196616 | tf_op jit(solution)/shard_map/ppermute | solution.py:256
  30.4 6.3 %collective-permute-start.22 = (bf16[64,512]{1,0:T(8,128)(2,1)S(1)}, bf16[64,512]{1,0:T(8,128)(2,1)S(1)}, u32[]{:S(2)}, u32[]{:S(2)}) collective-permute-start(bf16[64,512]{1,0:T(8,128)(2,1)S(1)} %get-tuple-element.49), channel_id=1, source_target_pairs={{0,6},{1,7},{2,4},{3,5},{4,2},{5,3},{6,0},{7,1},{8,14},{9,15},{10,... | collective-permute-start | bytes 196616 | tf_op jit(solution)/shard_map/ppermute | solution.py:256
  36.8 5.0 %collective-permute-start.23 = (bf16[64,512]{1,0:T(8,128)(2,1)S(1)}, bf16[64,512]{1,0:T(8,128)(2,1)S(1)}, u32[]{:S(2)}, u32[]{:S(2)}) collective-permute-start(bf16[64,512]{1,0:T(8,128)(2,1)S(1)} %strip.1.refs_1_), channel_id=1, source_target_pairs={{0,2},{1,3},{2,0},{3,1},{4,6},{5,7},{6,4},{7,5},{8,10},{9,11},{10,... | collective-permute-start | bytes 196616 | tf_op jit(solution)/shard_map/ppermute | solution.py:256
  36.8 16.1 %collective-permute-start.10 = (bf16[128,512]{1,0:T(8,128)(2,1)S(1)}, bf16[128,512]{1,0:T(8,128)(2,1)S(1)}, u32[]{:S(2)}, u32[]{:S(2)}) collective-permute-start(bf16[128,512]{1,0:T(8,128)(2,1)S(1)} %get-tuple-element.42), channel_id=1, source_target_pairs={{0,2},{1,3},{2,0},{3,1},{4,6},{5,7},{6,4},{7,5},{8,10},{9,11},{10,... | collective-permute-start | bytes 393224 | tf_op jit(solution)/shard_map/ppermute | solution.py:256
  38.8 14.5 %collective-permute-start.11 = (bf16[128,512]{1,0:T(8,128)(2,1)S(1)}, bf16[128,512]{1,0:T(8,128)(2,1)S(1)}, u32[]{:S(2)}, u32[]{:S(2)}) collective-permute-start(bf16[128,512]{1,0:T(8,128)(2,1)S(1)} %get-tuple-element.43), channel_id=1, source_target_pairs={{0,4},{1,5},{2,6},{3,7},{4,0},{5,1},{6,2},{7,3},{8,12},{9,13},{10,... | collective-permute-start | bytes 393224 | tf_op jit(solution)/shard_map/ppermute | solution.py:256
  39.6 10.2 %collective-permute-start.24 = (bf16[64,512]{1,0:T(8,128)(2,1)S(1)}, bf16[64,512]{1,0:T(8,128)(2,1)S(1)}, u32[]{:S(2)}, u32[]{:S(2)}) collective-permute-start(bf16[64,512]{1,0:T(8,128)(2,1)S(1)} %strip.1.refs_1_), channel_id=1, source_target_pairs={{0,4},{1,5},{2,6},{3,7},{4,0},{5,1},{6,2},{7,3},{8,12},{9,13},{10,... | collective-permute-start | bytes 196616 | tf_op jit(solution)/shard_map/ppermute | solution.py:256
  41.8 9.5 %collective-permute-start.25 = (bf16[64,512]{1,0:T(8,128)(2,1)S(1)}, bf16[64,512]{1,0:T(8,128)(2,1)S(1)}, u32[]{:S(2)}, u32[]{:S(2)}) collective-permute-start(bf16[64,512]{1,0:T(8,128)(2,1)S(1)} %strip.1.refs_1_), channel_id=1, source_target_pairs={{0,6},{1,7},{2,4},{3,5},{4,2},{5,3},{6,0},{7,1},{8,14},{9,15},{10,... | collective-permute-start | bytes 196616 | tf_op jit(solution)/shard_map/ppermute | solution.py:256
  49.8 13.7 %collective-permute-start.13 = (f32[2,64,512]{2,1,0:T(8,128)S(1)}, f32[2,64,512]{2,1,0:T(8,128)S(1)}, u32[]{:S(2)}, u32[]{:S(2)}) collective-permute-start(f32[2,64,512]{2,1,0:T(8,128)S(1)} %bitcast.14), channel_id=1, source_target_pairs={{0,8},{8,0},{16,24},{24,16},{1,9},{9,1},{17,25},{25,17},{2,10},{10... | collective-permute-start | bytes 786440 | tf_op jit(solution)/shard_map/ppermute | solution.py:256
  51.3 14.1 %collective-permute-start.14 = (f32[2,64,512]{2,1,0:T(8,128)S(1)}, f32[2,64,512]{2,1,0:T(8,128)S(1)}, u32[]{:S(2)}, u32[]{:S(2)}) collective-permute-start(f32[2,64,512]{2,1,0:T(8,128)S(1)} %bitcast.15), channel_id=1, source_target_pairs={{0,16},{8,24},{16,0},{24,8},{1,17},{9,25},{17,1},{25,9},{2,18},{10... | collective-permute-start | bytes 786440 | tf_op jit(solution)/shard_map/ppermute | solution.py:256
  52.9 12.8 %collective-permute-start.15 = (f32[2,64,512]{2,1,0:T(8,128)S(1)}, f32[2,64,512]{2,1,0:T(8,128)S(1)}, u32[]{:S(2)}, u32[]{:S(2)}) collective-permute-start(f32[2,64,512]{2,1,0:T(8,128)S(1)} %bitcast.16), channel_id=1, source_target_pairs={{0,24},{8,16},{16,8},{24,0},{1,25},{9,17},{17,9},{25,1},{2,26},{10... | collective-permute-start | bytes 786440 | tf_op jit(solution)/shard_map/ppermute | solution.py:256
  53.3 6.8 %collective-permute-start.12 = (bf16[128,512]{1,0:T(8,128)(2,1)S(1)}, bf16[128,512]{1,0:T(8,128)(2,1)S(1)}, u32[]{:S(2)}, u32[]{:S(2)}) collective-permute-start(bf16[128,512]{1,0:T(8,128)(2,1)S(1)} %get-tuple-element.36.after_ref), channel_id=1, source_target_pairs={{0,6},{1,7},{2,4},{3,5},{4,2},{5,3},{6,0},{7,1},{8,14},{9,15},{10,... | collective-permute-start | bytes 393224 | tf_op jit(solution)/shard_map/ppermute | solution.py:256
  60.1 23.2 %collective-permute-start.26 = (bf16[256,512]{1,0:T(8,128)(2,1)S(1)}, bf16[256,512]{1,0:T(8,128)(2,1)S(1)}, u32[]{:S(2)}, u32[]{:S(2)}) collective-permute-start(bf16[256,512]{1,0:T(8,128)(2,1)S(1)} %gather_strips.1.refs_6_), channel_id=1, source_target_pairs={{0,1},{1,0},{2,3},{3,2},{4,5},{5,4},{6,7},{7,6},{8,9},{9,8},{10,11... | collective-permute-start | bytes 786440 | tf_op jit(solution)/shard_map/ppermute | solution.py:256
  60.2 3.4 %collective-permute-start.16 = (f32[8,128]{1,0:T(8,128)S(1)}, f32[8,128]{1,0:T(8,128)S(1)}, u32[]{:S(2)}, u32[]{:S(2)}) collective-permute-start(f32[8,128]{1,0:T(8,128)S(1)} %get-tuple-element.45), channel_id=1, source_target_pairs={{0,1},{1,0},{2,3},{3,2},{4,5},{5,4},{6,7},{7,6},{8,9},{9,8},{10,11... | collective-permute-start | bytes 12296 | tf_op jit(solution)/shard_map/ppermute | solution.py:256
  63.6 17.7 %collective-permute-start.7 = (bf16[128,512]{1,0:T(8,128)(2,1)S(1)}, bf16[128,512]{1,0:T(8,128)(2,1)S(1)}, u32[]{:S(2)}, u32[]{:S(2)}) collective-permute-start(bf16[128,512]{1,0:T(8,128)(2,1)S(1)} %get-tuple-element.39), channel_id=1, source_target_pairs={{0,2},{1,3},{2,0},{3,1},{4,6},{5,7},{6,4},{7,5},{8,10},{9,11},{10,... | collective-permute-start | bytes 393224 | tf_op jit(solution)/shard_map/ppermute | solution.py:256
  63.7 19.2 %collective-permute-start.8 = (bf16[128,512]{1,0:T(8,128)(2,1)S(1)}, bf16[128,512]{1,0:T(8,128)(2,1)S(1)}, u32[]{:S(2)}, u32[]{:S(2)}) collective-permute-start(bf16[128,512]{1,0:T(8,128)(2,1)S(1)} %get-tuple-element.40), channel_id=1, source_target_pairs={{0,4},{1,5},{2,6},{3,7},{4,0},{5,1},{6,2},{7,3},{8,12},{9,13},{10,... | collective-permute-start | bytes 393224 | tf_op jit(solution)/shard_map/ppermute | solution.py:256
  65.4 5.1 %collective-permute-start.17 = (f32[8,128]{1,0:T(8,128)S(1)}, f32[8,128]{1,0:T(8,128)S(1)}, u32[]{:S(2)}, u32[]{:S(2)}) collective-permute-start(f32[8,128]{1,0:T(8,128)S(1)} %add.18.refs_12_), channel_id=1, source_target_pairs={{0,2},{1,3},{2,0},{3,1},{4,6},{5,7},{6,4},{7,5},{8,10},{9,11},{10,... | collective-permute-start | bytes 12296 | tf_op jit(solution)/shard_map/ppermute | solution.py:256
  65.7 7.3 %collective-permute-start.18 = (f32[8,128]{1,0:T(8,128)S(1)}, f32[8,128]{1,0:T(8,128)S(1)}, u32[]{:S(2)}, u32[]{:S(2)}) collective-permute-start(f32[8,128]{1,0:T(8,128)S(1)} %add.18.refs_12_), channel_id=1, source_target_pairs={{0,4},{1,5},{2,6},{3,7},{4,0},{5,1},{6,2},{7,3},{8,12},{9,13},{10,... | collective-permute-start | bytes 12296 | tf_op jit(solution)/shard_map/ppermute | solution.py:256
  70.5 12.8 %collective-permute-start.9 = (bf16[128,512]{1,0:T(8,128)(2,1)S(1)}, bf16[128,512]{1,0:T(8,128)(2,1)S(1)}, u32[]{:S(2)}, u32[]{:S(2)}) collective-permute-start(bf16[128,512]{1,0:T(8,128)(2,1)S(1)} %get-tuple-element.41), channel_id=1, source_target_pairs={{0,6},{1,7},{2,4},{3,5},{4,2},{5,3},{6,0},{7,1},{8,14},{9,15},{10,... | collective-permute-start | bytes 393224 | tf_op jit(solution)/shard_map/ppermute | solution.py:256
  73.1 5.5 %collective-permute-start.19 = (f32[8,128]{1,0:T(8,128)S(1)}, f32[8,128]{1,0:T(8,128)S(1)}, u32[]{:S(2)}, u32[]{:S(2)}) collective-permute-start(f32[8,128]{1,0:T(8,128)S(1)} %add.18.refs_12_), channel_id=1, source_target_pairs={{0,6},{1,7},{2,4},{3,5},{4,2},{5,3},{6,0},{7,1},{8,14},{9,15},{10,... | collective-permute-start | bytes 12296 | tf_op jit(solution)/shard_map/ppermute | solution.py:256
  79.7 7.0 %collective-permute-start.27 = (bf16[64,512]{1,0:T(8,128)(2,1)S(1)}, bf16[64,512]{1,0:T(8,128)(2,1)S(1)}, u32[]{:S(2)}, u32[]{:S(2)}) collective-permute-start(bf16[64,512]{1,0:T(8,128)(2,1)S(1)} %get-tuple-element.56.refs_9_), channel_id=1, source_target_pairs={{0,8},{8,0},{16,24},{24,16},{1,9},{9,1},{17,25},{25,17},{2,10},{10... | collective-permute-start | bytes 196616 | tf_op jit(solution)/shard_map/ppermute | solution.py:256
  81.3 8.0 %collective-permute-start.28 = (bf16[64,512]{1,0:T(8,128)(2,1)S(1)}, bf16[64,512]{1,0:T(8,128)(2,1)S(1)}, u32[]{:S(2)}, u32[]{:S(2)}) collective-permute-start(bf16[64,512]{1,0:T(8,128)(2,1)S(1)} %get-tuple-element.56.refs_9_), channel_id=1, source_target_pairs={{0,16},{8,24},{16,0},{24,8},{1,17},{9,25},{17,1},{25,9},{2,18},{10... | collective-permute-start | bytes 196616 | tf_op jit(solution)/shard_map/ppermute | solution.py:256
  82.9 6.4 %collective-permute-start.29 = (bf16[64,512]{1,0:T(8,128)(2,1)S(1)}, bf16[64,512]{1,0:T(8,128)(2,1)S(1)}, u32[]{:S(2)}, u32[]{:S(2)}) collective-permute-start(bf16[64,512]{1,0:T(8,128)(2,1)S(1)} %get-tuple-element.56.refs_9_), channel_id=1, source_target_pairs={{0,24},{8,16},{16,8},{24,0},{1,25},{9,17},{17,9},{25,1},{2,26},{10... | collective-permute-start | bytes 196616 | tf_op jit(solution)/shard_map/ppermute | solution.py:256
  83.6 1.2 %collective-permute-start.30 = (f32[8,128]{1,0:T(8,128)S(1)}, f32[8,128]{1,0:T(8,128)S(1)}, u32[]{:S(2)}, u32[]{:S(2)}) collective-permute-start(f32[8,128]{1,0:T(8,128)S(1)} %get-tuple-element.57), channel_id=1, source_target_pairs={{0,1},{1,0},{2,3},{3,2},{4,5},{5,4},{6,7},{7,6},{8,9},{9,8},{10,11... | collective-permute-start | bytes 12296 | tf_op jit(solution)/shard_map/ppermute | solution.py:256
  84.9 4.4 %collective-permute-start.31 = (f32[8,128]{1,0:T(8,128)S(1)}, f32[8,128]{1,0:T(8,128)S(1)}, u32[]{:S(2)}, u32[]{:S(2)}) collective-permute-start(f32[8,128]{1,0:T(8,128)S(1)} %add.19.refs_13_), channel_id=1, source_target_pairs={{0,2},{1,3},{2,0},{3,1},{4,6},{5,7},{6,4},{7,5},{8,10},{9,11},{10,... | collective-permute-start | bytes 12296 | tf_op jit(solution)/shard_map/ppermute | solution.py:256
  86.5 4.5 %collective-permute-start.32 = (f32[8,128]{1,0:T(8,128)S(1)}, f32[8,128]{1,0:T(8,128)S(1)}, u32[]{:S(2)}, u32[]{:S(2)}) collective-permute-start(f32[8,128]{1,0:T(8,128)S(1)} %add.19.refs_13_), channel_id=1, source_target_pairs={{0,4},{1,5},{2,6},{3,7},{4,0},{5,1},{6,2},{7,3},{8,12},{9,13},{10,... | collective-permute-start | bytes 12296 | tf_op jit(solution)/shard_map/ppermute | solution.py:256
  86.7 5.4 %collective-permute-start.33 = (f32[8,128]{1,0:T(8,128)S(1)}, f32[8,128]{1,0:T(8,128)S(1)}, u32[]{:S(2)}, u32[]{:S(2)}) collective-permute-start(f32[8,128]{1,0:T(8,128)S(1)} %add.19.refs_13_), channel_id=1, source_target_pairs={{0,6},{1,7},{2,4},{3,5},{4,2},{5,3},{6,0},{7,1},{8,14},{9,15},{10,... | collective-permute-start | bytes 12296 | tf_op jit(solution)/shard_map/ppermute | solution.py:256

commit v3 on v2

v3 whole, which is shorter than its diff:
```python
import functools
import math

import jax
import jax.numpy as jnp
from jax import lax
from jax.experimental import pallas as pl
from jax.experimental.pallas import tpu as pltpu
from jax.sharding import PartitionSpec as P

beta_one = 0.9
beta_two = 0.95
inner_rate = 0.1
adam_eps = 1e-08
decay_rate = 0.1
clip_norm = 0.02
outer_rate = 0.7
outer_momentum = 0.9
mixing = 0.5

F32 = jnp.float32
BF16 = jnp.bfloat16
VMEM_BYTES = 16 * 1024 * 1024


def tree_sum(items):
    items = list(items)
    while len(items) > 1:
        items = [a + b for a, b in zip(items[0::2], items[1::2])]
    return items[0]


def nt(a, b):
    return lax.dot_general(a, b, (((1,), (1,)), ((), ())), preferred_element_type=F32)


def tn(a, b):
    return lax.dot_general(a, b, (((0,), (0,)), ((), ())), preferred_element_type=F32)


def call(kernel, out_shape, scalars, arrays, name, after=(), scratch=(), flops=0):
    vmem = pl.BlockSpec(memory_space=pltpu.VMEM)

    def run(*refs):
        count = len(scalars) + len(arrays)
        kernel(*refs[:count], *refs[count + len(after) :])

    return pl.pallas_call(
        run,
        in_specs=[pl.BlockSpec(memory_space=pltpu.SMEM)] * len(scalars)
        + [vmem] * len(arrays)
        + [pl.BlockSpec(memory_space=pl.ANY)] * len(after),
        out_specs=[vmem] * len(out_shape),
        out_shape=out_shape,
        scratch_shapes=list(scratch),
        compiler_params=pltpu.CompilerParams(vmem_limit_bytes=VMEM_BYTES),
        cost_estimate=pl.CostEstimate(flops=flops, bytes_accessed=1024, transcendentals=0),
        name=name,
    )(*scalars, *arrays, *after)


def lower_kernel(w_ref, out_ref):
    rows = w_ref.shape[1]
    for frag in range(2):
        out_ref[pl.ds(frag * rows, rows), :] = w_ref[frag].astype(BF16)


def split_kernel(rows, side_ref, own_ref, sib_ref, *outs):
    core = side_ref[0]
    for step in range(2):
        for goal_ref, out_ref in zip((own_ref, sib_ref), outs):
            first, second = (goal_ref[0, step, :, frag, :].astype(F32) for frag in range(2))
            for chip in range(out_ref.shape[1]):
                for which in range(2):

                    @pl.when(core == which)
                    def _():
                        at = (2 * chip + which) * rows
                        pair = [first[:, at : at + rows], second[:, at : at + rows]]
                        out_ref[step, chip] = jnp.concatenate(pair, 1).astype(BF16)


def chunk_grad(scale, grad_scale, step, group, place_ref, w_refs, token_refs, goal_refs):
    w = jnp.concatenate([ref[...] for ref in w_refs], 0)
    total = None
    for x_ref, t_ref in zip(token_refs, goal_refs):
        x = x_ref[step]
        goal = jnp.concatenate([t_ref[step, place_ref[k]] for k in group], 1)
        res = (nt(x, w) * scale - goal.astype(F32)).astype(BF16)
        term = tn(res, x)
        total = term if total is None else total + term
    total = (total * grad_scale).astype(BF16)
    rows = w_refs[0].shape[0]
    return [total[i * rows : (i + 1) * rows] for i in range(len(group))]


def near_kernel(scales, group, place_ref, *refs):
    size = len(group)
    w_refs, token_refs, goal_refs = refs[:size], refs[size : size + 2], refs[size + 2 : size + 4]
    outs = refs[size + 4 :]
    for step in range(2):
        made = chunk_grad(*scales, step, group, place_ref, w_refs, token_refs, goal_refs)
        for ref, value in zip(outs[step * size :], made):
            ref[...] = value


def far_kernel(scales, near, far, place_ref, *refs):
    size = len(far)
    chips = len(near) + size
    w_refs, token_refs, goal_refs = refs[:size], refs[size : size + 2], refs[size + 2 : size + 4]
    near_refs = refs[size + 4 : size + 4 + len(near)]
    strip_refs = refs[size + 4 + len(near) : size + 4 + len(near) + chips]
    weights_ref, *outs, copy_ref = refs[size + 4 + len(near) + chips :]
    made = dict(zip(near, (ref[...] for ref in near_refs)))
    made.update(zip(far, chunk_grad(*scales, 0, far, place_ref, w_refs, token_refs, goal_refs)))
    strip = tree_sum(ref[...].astype(F32) for ref in strip_refs).astype(BF16)
    for k, ref in enumerate(outs[:chips]):
        rows = made[k].shape[0]
        ref[pl.ds(0, rows), :] = made[k]
        ref[pl.ds(rows, strip.shape[0]), :] = strip
    made = chunk_grad(*scales, 1, far, place_ref, w_refs, token_refs, goal_refs)
    for ref, value in zip(outs[chips:], made):
        ref[...] = value
    copy_ref[...] = weights_ref[...]


def halve_kernel(*refs):
    count = len(refs) // 3
    for keep_ref, got_ref, out_ref in zip(refs[:count], refs[count:], refs[2 * count :]):
        out_ref[...] = (keep_ref[...].astype(F32) + got_ref[...].astype(F32)).astype(BF16)


def gram_kernel(step, side_ref, place_ref, xo_ref, xs_ref, *refs):
    outs, scratch = refs[:-1], refs[-1]
    rows, width = outs[0].shape
    part = pl.ds(pl.multiple_of(side_ref[0] * (width // 2), width // 2), width // 2)
    total = tn(xo_ref[step, :, part], xo_ref[step]) + tn(xs_ref[step, :, part], xs_ref[step])
    scratch[...] = total.astype(BF16)
    for k, ref in enumerate(outs):
        ref[...] = scratch[pl.ds(pl.multiple_of(place_ref[k] * rows, rows), rows), :]


def add_kernel(*refs):
    refs[-1][...] = tree_sum(ref[...] for ref in refs[:-1])


def sum_kernel(place_ref, *refs):
    pieces, (grad_ref, squares_ref, gram_ref) = refs[:-3], refs[-3:]
    rows = grad_ref.shape[0]
    strip = pieces[0].shape[0] - rows
    grad = tree_sum(ref[pl.ds(0, rows), :].astype(F32) for ref in pieces)
    grad_ref[...] = grad
    squares_ref[...] = fold(grad * grad)
    for k, ref in enumerate(pieces):
        gram_ref[pl.ds(pl.multiple_of(place_ref[k] * strip, strip), strip), :] = ref[pl.ds(rows, strip), :]


def fold(x):
    rows, width = x.shape
    tiles = [x[i : i + 8] for i in range(0, rows, 8)]
    while len(tiles) > 1:
        tiles = [a + b for a, b in zip(tiles[0::2], tiles[1::2])]
    x = tiles[0]
    lanes = [x[:, i : i + 128] for i in range(0, width, 128)]
    return functools.reduce(lambda a, b: a + b, lanes)


def correct_kernel(count, factor, side_ref, *refs):
    grad_ref, squares_ref = refs[-2:]
    dw_ref, go_ref, gs_ref = refs[count : count + 3]
    half = go_ref.shape[0]
    total = tree_sum(ref[...].astype(F32) for ref in refs[:count])
    p = side_ref[0]
    extra = None
    for at, g_ref in ((p, go_ref), (1 - p, gs_ref)):
        dw = dw_ref[:, pl.ds(pl.multiple_of(at * half, half), half)]
        high = dw.astype(BF16)
        low = (dw - high.astype(F32)).astype(BF16)
        g = g_ref[...]
        term = jnp.dot(high, g, preferred_element_type=F32) + jnp.dot(
            low, g, preferred_element_type=F32
        )
        extra = term if extra is None else extra + term
    grad = total + factor * extra
    grad_ref[...] = grad
    squares_ref[...] = fold(grad * grad)


def adam(grad, norm_refs, one, two, moment_one, moment_two, weights):
    squares = jnp.sum(tree_sum(ref[...] for ref in norm_refs))
    norm = jnp.sqrt(jnp.full((1, 1), squares, F32))
    clipped = grad * jnp.minimum(1.0, clip_norm / (norm + 1e-06))
    moment_one = beta_one * moment_one + (1.0 - beta_one) * clipped
    moment_two = beta_two * moment_two + (1.0 - beta_two) * clipped * clipped
    update = moment_one / one / (jnp.sqrt(moment_two / two) + adam_eps)
    return moment_one, moment_two, update, weights - inner_rate * (update + decay_rate * weights)


def outer_step(theta, speed, delta):
    speed = outer_momentum * speed + delta
    return theta - outer_rate * (outer_momentum * speed + delta)


def first_kernel(
    replicas, count, first_ref, correct_ref, grad_ref, m_ref, v_ref, w_ref, outer_ref, vel_ref, total_ref, *refs
):
    norms = refs[:count]
    m_out, v_out, w_out, dw_out, theta_out, send_out = refs[count:]
    rows = grad_ref.shape[0] // 2
    first = first_ref[0]
    sends = []
    for frag in range(2):
        part = pl.ds(frag * rows, rows)
        m, v, update, after = adam(
            grad_ref[part, :], norms, correct_ref[0], correct_ref[1], m_ref[frag], v_ref[frag], w_ref[frag]
        )
        m_out[frag] = m
        v_out[frag] = v
        sends.append(update)
        old = outer_ref[frag]
        theta = outer_step(old, vel_ref[frag], old - total_ref[frag] * (1.0 / replicas))
        now = first == frag
        theta_out[frag] = jnp.where(now, theta, old)
        after = jnp.where(now, mixing * theta + (1.0 - mixing) * after, after)
        w_out[frag] = after
        dw_out[part, :] = after.astype(BF16).astype(F32) - w_ref[frag].astype(BF16).astype(F32)
    send_out[...] = jnp.where(first == 0, sends[1], sends[0]).astype(BF16)


def last_kernel(
    replicas, count, first_ref, correct_ref, grad_ref, m_ref, v_ref, w_ref, outer_ref, vel_ref, total_ref, *refs
):
    updates = refs[:replicas]
    norms = refs[replicas : replicas + count]
    outer_out, inner_out = refs[replicas + count :]
    rows = grad_ref.shape[0] // 2
    first = first_ref[0]
    moved = tree_sum(ref[...].astype(F32) for ref in updates)
    for frag in range(2):
        part = pl.ds(frag * rows, rows)
        after = adam(
            grad_ref[part, :], norms, correct_ref[2], correct_ref[3], m_ref[frag], v_ref[frag], w_ref[frag]
        )[3]
        old = outer_ref[frag]
        mean = ((1.0 - inner_rate * decay_rate) * total_ref[frag] - inner_rate * moved) * (1.0 / replicas)
        theta = outer_step(old, vel_ref[frag], old - mean)
        now = first != frag
        outer_out[frag] = jnp.where(now, theta, old)
        inner_out[frag] = jnp.where(now, mixing * theta + (1.0 - mixing) * after, after)


def body(
    inner_weights,
    first_moment,
    second_moment,
    outer_weights,
    outer_velocity,
    tokens,
    targets,
    step_count,
    first_fragment,
):
    weights = inner_weights[0]
    rows, width = weights.shape[1:]
    replicas = lax.axis_size("rep")
    shards = lax.axis_size("shard")
    chips = shards // 2
    toks = tokens.shape[2]
    scale = 1.0 / math.sqrt(width)
    grad_scale = scale / (toks * shards)
    index = lax.axis_index("shard")
    core = index % 2
    chip = index // 2

    def swap(x, axis, size, by):
        return lax.ppermute(x, axis, [(i, i ^ by) for i in range(size)])

    sibling = lambda x: swap(x, "shard", shards, 1)
    across = lambda x, by: swap(x, "shard", shards, 2 * by)
    over_rep = lambda x, by: x if by == 0 else swap(x, "rep", replicas, by)

    shape = jax.ShapeDtypeStruct
    block = shape((2 * rows, width), BF16)
    tile = shape((8, 128), F32)
    state = shape((2, rows, width), F32)
    flat = shape((2 * rows, width), F32)
    side = jnp.reshape(core, (1,)).astype(jnp.int32)
    place = jnp.stack([chip ^ k for k in range(chips)]).astype(jnp.int32)

    (lowered,) = call(lower_kernel, [block], [], [weights], "lower")
    held = [lowered] + [across(lowered, k) for k in range(1, chips)]

    own_x = tokens[0]
    sib_x = sibling(own_x)

    swapped = sibling(targets)

    strip_shape = shape((width // shards, width), BF16)
    strips = call(
        functools.partial(gram_kernel, 1),
        [strip_shape] * chips,
        [side, place],
        [own_x, sib_x],
        "gram",
        [lowered],
        [pltpu.VMEM((width // 2, width), BF16)],
    )

    def spread(made):
        return [made[0]] + [across(made[k], k) for k in range(1, chips)]

    def norm_parts(squares, after):
        (both,) = call(add_kernel, [tile], [], [squares, sibling(squares)], "add_cores", after)
        return [both] + [across(both, k) for k in range(1, chips)]

    parts = shape((2, chips, toks, 2 * rows), BF16)
    own_t, sib_t = call(
        functools.partial(split_kernel, rows), [parts, parts], [side], [targets, swapped], "split", [strips[0]]
    )

    near = list(range(max(1, chips // 2)))
    far = list(range(max(1, chips // 2), chips))
    scales = (scale, grad_scale)
    made = call(
        functools.partial(near_kernel, scales, near),
        [block] * (2 * len(near)),
        [place],
        [held[k] for k in near] + [own_x, sib_x, own_t, sib_t],
        "near_grad",
    )
    joint = call(
        functools.partial(far_kernel, scales, near, far),
        [shape((2 * rows + width // shards, width), BF16)] * chips + [block] * len(far) + [state],
        [place],
        [held[k] for k in far] + [own_x, sib_x, own_t, sib_t, *made[: len(near)], *spread(strips), weights],
        "far_grad",
    )
    pieces_one = spread(joint[:chips])
    made = [*made[len(near) :], *joint[chips:-1]]
    early = joint[-1]
    keep, got = made[0::2], [across(x, 1) for x in made[1::2]]
    ready = got
    bit = 2
    while bit < chips:
        made = call(halve_kernel, [block] * len(keep), [], [*keep, *got], "halve")
        keep, got = made[0::2], [across(x, bit) for x in made[1::2]]
        bit *= 2
    pieces_two = [keep[0], got[0]]

    sums = early
    by = 1
    while by < replicas:
        (sums,) = call(add_kernel, [state], [], [sums, swap(sums, "rep", replicas, by)], "add_reps")
        by *= 2

    grad, squares, own_g = call(
        sum_kernel,
        [flat, tile, shape((width // 2, width), BF16)],
        [place],
        pieces_one,
        "sum_pieces",
        ready,
    )
    sib_g = sibling(own_g)
    norms = norm_parts(squares, [sib_g])

    count = step_count[0].astype(F32)
    correct = jnp.stack(
        [1.0 - jnp.power(beta, count + s) for s in range(2) for beta in (beta_one, beta_two)]
    )
    m, v, middle, change, outer, moved = call(
        functools.partial(first_kernel, replicas, chips),
        [state, state, state, flat, state, shape((rows, width), BF16)],
        [first_fragment, correct],
        [grad, first_moment[0], second_moment[0], weights, outer_weights, outer_velocity, sums, *norms],
        "first_update",
        pieces_two[1:],
    )
    updates = [over_rep(moved, k) for k in range(replicas)]

    grad, squares = call(
        functools.partial(correct_kernel, len(pieces_two), scale * grad_scale),
        [flat, tile],
        [side],
        [*pieces_two, change, own_g, sib_g],
        "corrected",
    )
    norms = norm_parts(squares, [])
    new_outer, new_inner = call(
        functools.partial(last_kernel, replicas, chips),
        [state, state],
        [first_fragment, correct],
        [grad, m, v, middle, outer, outer_velocity, sums, *updates, *norms],
        "last_update",
    )
    return (new_outer, new_inner[None])


def solution(mesh):
    in_specs = (
        P("rep", None, "shard", None),
        P("rep", None, "shard", None),
        P("rep", None, "shard", None),
        P(None, "shard", None),
        P(None, "shard", None),
        P("rep", None, "shard", None),
        P("rep", None, "shard", None, None),
        P(),
        P(),
    )
    out_specs = (P(None, "shard", None), P("rep", None, "shard", None))
    return jax.shard_map(body, mesh=mesh, in_specs=in_specs, out_specs=out_specs, check_vma=False)
```

time: 94.2 us -> 79.1 us (0.84)
  waiting for transfers between devices: 30.8 us -> 18.6 us
  starting transfers between devices: 41.9 us -> 38 us
  Pallas kernels: 15.9 us -> 17.6 us
    ppermute x34 -> x28, waiting for transfers between devices: 30.8 us -> 18.6 us  [swap(): return lax.ppermute(x, axis, [(i, i ^ by) for i in range(size)])]
    pallas_call x10 -> x14, Pallas kernels: 11 us -> 17.6 us  [call(): pl.pallas_call(run, in_specs=[pl.BlockSpec(memory_space=pltpu.SMEM)] * le...]
    pallas_call x3 -> x0, Pallas kernels: 4.87 us -> none  [the longest x2 3.17 us: split(): pl.pallas_call(lambda side_ref, goal_ref, after_ref, *outs: split_kernel(...]
    ppermute x34 -> x28, starting transfers between devices: 41.9 us -> 38 us  [swap(): return lax.ppermute(x, axis, [(i, i ^ by) for i in range(size)])]
    squeeze x1 -> x0, local copies, waits for them, and re-layouts: 2.21 us -> none  [body(): own_x = [tokens[0, s] for s in range(2)]]
    unnamed x16 -> x18, local copies, waits for them, and re-layouts: 0.69 us -> 2.22 us
  transfers between devices with their start and end apart: 34 -> 28, of which waited for: 12 -> 8; matrix products, arithmetic and copies ran while one was open for 0% -> 0% of each run, Pallas kernels for 15% -> 16%
where the time goes in v3:
time: 79.1 us; the launch traced here: 78.9 us
  starting transfers between devices  38 us (48%)
  waiting for transfers between devices  18.6 us (24%)
  Pallas kernels  17.6 us (22%)
  between operations  2.35 us (3%)
  local copies, waits for them, and re-layouts  2.22 us (3%)
    ppermute x28, starting transfers between devices, swap(): return lax.ppermute(x, axis, [(i, i ^ by) for i in range(size)])  38 us
    ppermute x28, waiting for transfers between devices, swap(): return lax.ppermute(x, axis, [(i, i ^ by) for i in range(size)])  18.6 us
    pallas_call x14, Pallas kernels, call(): pl.pallas_call(run, in_specs=[pl.BlockSpec(memory_space=pltpu.SMEM)] * le...  17.6 us
    unnamed x18, local copies, waits for them, and re-layouts  2.22 us
  transfers between devices with their start and end apart: 28, of which 8 were waited for; matrix products, arithmetic and copies ran while one was open for 0% of the time, Pallas kernels for 16%

profile of v3, /device:TPU:0, one launch (start us, length us, event | category | flops | bytes accessed | tf_op | source)
XLA Modules:
  0.0 78.9 jit_solution(14120326131774548945)
XLA Ops:
  0.6 0.5 collective-permute-start.2
  1.1 0.1 collective-permute-start.1
  1.2 0.9 %copy-done.2 = f32[1,2,64,512]{3,2,1,0:T(8,128)S(1)} copy-done((f32[1,2,64,512]{3,2,1,0:T(8,128)S(1)}, f32[1,2,64,512]{3,2,1,0:T(8,128)}, u32[]{:S(2)}) %copy-start.2) | copy-done | bytes 262168
  2.2 3.1 %collective-permute-start = (bf16[128,512]{1,0:T(8,128)(2,1)S(1)}, bf16[128,512]{1,0:T(8,128)(2,1)}, u32[]{:S(2)}, u32[]{:S(2)}) collective-permute-start(bf16[128,512]{1,0:T(8,128)(2,1)S(1)} %lower.1.refs_4_.refs_1_), channel_id=1, source_target_pairs={{0,2},{1,3},{2,0},{3,1},{4,6},{5,7},{6,4},{7,5},{8,10},{9,11},{10,... | collective-permute-start | bytes 393224 | tf_op jit(solution)/shard_map/ppermute | solution.py:276
  5.3 2.6 %collective-permute-start.3 = (bf16[128,512]{1,0:T(8,128)(2,1)S(1)}, bf16[128,512]{1,0:T(8,128)(2,1)S(1)}, u32[]{:S(2)}, u32[]{:S(2)}) collective-permute-start(bf16[128,512]{1,0:T(8,128)(2,1)S(1)} %lower.1.refs_4_.refs_1_), channel_id=1, source_target_pairs={{0,4},{1,5},{2,6},{3,7},{4,0},{5,1},{6,2},{7,3},{8,12},{9,13},{10,... | collective-permute-start | bytes 393224 | tf_op jit(solution)/shard_map/ppermute | solution.py:276
  7.9 0.1 pad_add_fusion.refs_1_.refs_0_
  7.9 1.2 %copy-done = bf16[1,2,512,512]{3,2,1,0:T(8,128)(2,1)S(1)} copy-done((bf16[1,2,512,512]{3,2,1,0:T(8,128)(2,1)S(1)}, bf16[1,2,512,512]{3,2,1,0:T(8,128)(2,1)}, u32[]{:S(2)}) %copy-start) | copy-done | bytes 1048600
  9.2 1.0 %gram.1 = (bf16[64,512]{1,0:T(8,128)(2,1)S(1)}, bf16[64,512]{1,0:T(8,128)(2,1)S(1)}, bf16[64,512]{1,0:T(8,128)(2,1)S(1)}, bf16[64,512]{1,0:T(8,128)(2,1)S(1)}) custom-call(s32[1]{0:T(128)} %bitcast.refs_0_, s32[4]{0:T(128)S(1)} %pad_add_fusion.refs_1_.refs_0_, bf16[2,512,512]{2,1,0:T(8,128)(2,1)S(1)} %bitcast.11, ...), custom_call_target="tpu_custom_call" | custom-call | bytes 1024 | tf_op jit(solution)/shard_map/gram/pallas_call | solution.py:48
  10.2 1.7 %collective-permute-start.5 = (bf16[64,512]{1,0:T(8,128)(2,1)S(1)}, bf16[64,512]{1,0:T(8,128)(2,1)S(1)}, u32[]{:S(2)}, u32[]{:S(2)}) collective-permute-start(bf16[64,512]{1,0:T(8,128)(2,1)S(1)} %get-tuple-element.40), channel_id=1, source_target_pairs={{0,2},{1,3},{2,0},{3,1},{4,6},{5,7},{6,4},{7,5},{8,10},{9,11},{10,... | collective-permute-start | bytes 196616 | tf_op jit(solution)/shard_map/ppermute | solution.py:276
  11.9 2.7 %collective-permute-start.6 = (bf16[64,512]{1,0:T(8,128)(2,1)S(1)}, bf16[64,512]{1,0:T(8,128)(2,1)S(1)}, u32[]{:S(2)}, u32[]{:S(2)}) collective-permute-start(bf16[64,512]{1,0:T(8,128)(2,1)S(1)} %get-tuple-element.41), channel_id=1, source_target_pairs={{0,4},{1,5},{2,6},{3,7},{4,0},{5,1},{6,2},{7,3},{8,12},{9,13},{10,... | collective-permute-start | bytes 196616 | tf_op jit(solution)/shard_map/ppermute | solution.py:276
  14.7 0.0 copy-start.1
  14.7 8.0 %split.1 = (bf16[2,4,512,128]{3,2,1,0:T(8,128)(2,1)S(1)}, bf16[2,4,512,128]{3,2,1,0:T(8,128)(2,1)S(1)}) custom-call(s32[1]{0:T(128)} %bitcast.refs_0_, bf16[1,2,512,2,512]{4,3,2,1,0:T(2,128)(2,1)S(1)} %copy-done.4, bf16[1,2,512,2,512]{4,3,2,1,0:T(2,128)(2,1)S(1)} %collective-permute-done.2.refs_2_, bf16[64,512]{1,0:T(8,128)(2,1)S(1)} %get-tuple-element.34.refs_3_.refs_9_), custom_call_target="tpu_custom_call" | custom-call | bytes 1024 | tf_op jit(solution)/shard_map/split/pallas_call | solution.py:48
  22.7 2.5 %near_grad.1 = (bf16[128,512]{1,0:T(8,128)(2,1)S(1)}, bf16[128,512]{1,0:T(8,128)(2,1)S(1)}, bf16[128,512]{1,0:T(8,128)(2,1)S(1)}, bf16[128,512]{1,0:T(8,128)(2,1)S(1)}) custom-call(s32[4]{0:T(128)S(1)} %pad_add_fusion.refs_1_.refs_0_, bf16[128,512]{1,0:T(8,128)(2,1)S(1)} %lower.1.refs_4_.refs_1_, bf16[128,512]{1,0:T(8,128)(2,1)} %collective-permute-done.refs_2_, ...), custom_call_target="tpu_custom_call" | custom-call | bytes 1024 | tf_op jit(solution)/shard_map/near_grad/pallas_call | solution.py:48
  25.2 2.1 %far_grad.1 = (bf16[192,512]{1,0:T(8,128)(2,1)S(1)}, bf16[192,512]{1,0:T(8,128)(2,1)S(1)}, bf16[192,512]{1,0:T(8,128)(2,1)S(1)}, bf16[192,512]{1,0:T(8,128)(2,1)...) custom-call(s32[4]{0:T(128)S(1)} %pad_add_fusion.refs_1_.refs_0_, ...), custom_call_target="tpu_custom_call" | custom-call | bytes 1024 | tf_op jit(solution)/shard_map/far_grad/pallas_call | solution.py:48
  27.3 0.0 copy-start.6
  27.4 0.9 %collective-permute-start.9 = (bf16[128,512]{1,0:T(8,128)(2,1)S(1)}, bf16[128,512]{1,0:T(8,128)(2,1)S(1)}, u32[]{:S(2)}, u32[]{:S(2)}) collective-permute-start(bf16[128,512]{1,0:T(8,128)(2,1)S(1)} %get-tuple-element.45), channel_id=1, source_target_pairs={{0,2},{1,3},{2,0},{3,1},{4,6},{5,7},{6,4},{7,5},{8,10},{9,11},{10,... | collective-permute-start | bytes 393224 | tf_op jit(solution)/shard_map/ppermute | solution.py:276
  28.3 1.2 %collective-permute-start.11 = (bf16[192,512]{1,0:T(8,128)(2,1)S(1)}, bf16[192,512]{1,0:T(8,128)(2,1)S(1)}, u32[]{:S(2)}, u32[]{:S(2)}) collective-permute-start(bf16[192,512]{1,0:T(8,128)(2,1)S(1)} %get-tuple-element.49), channel_id=1, source_target_pairs={{0,2},{1,3},{2,0},{3,1},{4,6},{5,7},{6,4},{7,5},{8,10},{9,11},{10,... | collective-permute-start | bytes 589832 | tf_op jit(solution)/shard_map/ppermute | solution.py:276
  29.5 2.4 %collective-permute-start.12 = (bf16[192,512]{1,0:T(8,128)(2,1)S(1)}, bf16[192,512]{1,0:T(8,128)(2,1)S(1)}, u32[]{:S(2)}, u32[]{:S(2)}) collective-permute-start(bf16[192,512]{1,0:T(8,128)(2,1)S(1)} %get-tuple-element.50), channel_id=1, source_target_pairs={{0,4},{1,5},{2,6},{3,7},{4,0},{5,1},{6,2},{7,3},{8,12},{9,13},{10,... | collective-permute-start | bytes 589832 | tf_op jit(solution)/shard_map/ppermute | solution.py:276
  31.9 1.4 %collective-permute-start.13 = (bf16[192,512]{1,0:T(8,128)(2,1)S(1)}, bf16[192,512]{1,0:T(8,128)(2,1)S(1)}, u32[]{:S(2)}, u32[]{:S(2)}) collective-permute-start(bf16[192,512]{1,0:T(8,128)(2,1)S(1)} %get-tuple-element.51), channel_id=1, source_target_pairs={{0,6},{1,7},{2,4},{3,5},{4,2},{5,3},{6,0},{7,1},{8,14},{9,15},{10,... | collective-permute-start | bytes 589832 | tf_op jit(solution)/shard_map/ppermute | solution.py:276
  33.3 1.5 %collective-permute-start.14 = (f32[2,64,512]{2,1,0:T(8,128)S(1)}, f32[2,64,512]{2,1,0:T(8,128)S(1)}, u32[]{:S(2)}, u32[]{:S(2)}) collective-permute-start(f32[2,64,512]{2,1,0:T(8,128)S(1)} %get-tuple-element.53.refs_0_), channel_id=1, source_target_pairs={{0,8},{8,0},{16,24},{24,16},{1,9},{9,1},{17,25},{25,17},{2,10},{10... | collective-permute-start | bytes 786440 | tf_op jit(solution)/shard_map/ppermute | solution.py:276
  34.8 2.9 %collective-permute-done.9.refs_3_.refs_6_ = bf16[128,512]{1,0:T(8,128)(2,1)S(1)} collective-permute-done((bf16[128,512]{1,0:T(8,128)(2,1)S(1)}, bf16[128,512]{1,0:T(8,128)(2,1)S(1)}, u32[]{:S(2)}, u32[]{:S(2)}) %collective-permute-start.9) | collective-permute-done | bytes 131104 | tf_op jit(solution)/shard_map/ppermute | solution.py:276
  37.7 9.5 %collective-permute-done.8.refs_2_.refs_5_ = bf16[128,512]{1,0:T(8,128)(2,1)S(1)} collective-permute-done((bf16[128,512]{1,0:T(8,128)(2,1)S(1)}, bf16[128,512]{1,0:T(8,128)(2,1)S(1)}, u32[]{:S(2)}, u32[]{:S(2)}) %collective-permute-start.8) | collective-permute-done | bytes 131104 | tf_op jit(solution)/shard_map/ppermute | solution.py:276
  47.2 1.0 %collective-permute-done.13.refs_4_ = bf16[192,512]{1,0:T(8,128)(2,1)S(1)} collective-permute-done((bf16[192,512]{1,0:T(8,128)(2,1)S(1)}, bf16[192,512]{1,0:T(8,128)(2,1)S(1)}, u32[]{:S(2)}, u32[]{:S(2)}) %collective-permute-start.13) | collective-permute-done | bytes 196640 | tf_op jit(solution)/shard_map/ppermute | solution.py:276
  48.2 0.6 sum_pieces.1
  48.9 0.1 collective-permute-start.17
  49.0 1.6 %collective-permute-start.15 = (f32[2,64,512]{2,1,0:T(8,128)S(1)}, f32[2,64,512]{2,1,0:T(8,128)S(1)}, u32[]{:S(2)}, u32[]{:S(2)}) collective-permute-start(f32[2,64,512]{2,1,0:T(8,128)S(1)} %add_reps.2.refs_0_), channel_id=1, source_target_pairs={{0,16},{8,24},{16,0},{24,8},{1,17},{9,25},{17,1},{25,9},{2,18},{10... | collective-permute-start | bytes 786440 | tf_op jit(solution)/shard_map/ppermute | solution.py:276
  50.6 0.1 halve.1
  50.7 3.2 %collective-permute-start.10 = (bf16[128,512]{1,0:T(8,128)(2,1)S(1)}, bf16[128,512]{1,0:T(8,128)(2,1)S(1)}, u32[]{:S(2)}, u32[]{:S(2)}) collective-permute-start(bf16[128,512]{1,0:T(8,128)(2,1)S(1)} %get-tuple-element.47), channel_id=1, source_target_pairs={{0,4},{1,5},{2,6},{3,7},{4,0},{5,1},{6,2},{7,3},{8,12},{9,13},{10,... | collective-permute-start | bytes 393224 | tf_op jit(solution)/shard_map/ppermute | solution.py:276
  54.7 0.3 collective-permute-done.16.refs_1_
  55.1 0.5 collective-permute-start.18
  55.5 0.5 collective-permute-start.19
  56.1 3.4 %collective-permute-start.20 = (f32[8,128]{1,0:T(8,128)S(1)}, f32[8,128]{1,0:T(8,128)S(1)}, u32[]{:S(2)}, u32[]{:S(2)}) collective-permute-start(f32[8,128]{1,0:T(8,128)S(1)} %add_cores.2.refs_9_), channel_id=1, source_target_pairs={{0,6},{1,7},{2,4},{3,5},{4,2},{5,3},{6,0},{7,1},{8,14},{9,15},{10,... | collective-permute-start | bytes 12296 | tf_op jit(solution)/shard_map/ppermute | solution.py:276
  59.4 0.1 pad_maximum_fusion.refs_1_
  60.2 0.5 collective-permute-done.10.refs_13_.refs_2_
  60.7 0.0 collective-permute-done.19.refs_11_
  60.8 0.7 collective-permute-done.20.refs_12_
  61.5 1.1 %first_update.1 = (f32[2,64,512]{2,1,0:T(8,128)S(1)}, f32[2,64,512]{2,1,0:T(8,128)S(1)}, f32[2,64,512]{2,1,0:T(8,128)S(1)}, f32[128,512]{1,0:T(8,128)S(1)}, f32[...) custom-call(s32[1]{0:T(128)S(6)} %copy.12.refs_0_, f32[4]{0:T(128)S(1)} %pad_maximum_fusion.refs_1_, ...), custom_call_target="tpu_custom_call" | custom-call | bytes 1024 | tf_op jit(solution)/shard_map/first_update/pallas_call | solution.py:48
  62.6 1.6 %collective-permute-start.21 = (bf16[64,512]{1,0:T(8,128)(2,1)S(1)}, bf16[64,512]{1,0:T(8,128)(2,1)S(1)}, u32[]{:S(2)}, u32[]{:S(2)}) collective-permute-start(bf16[64,512]{1,0:T(8,128)(2,1)S(1)} %get-tuple-element.62.refs_9_), channel_id=1, source_target_pairs={{0,8},{8,0},{16,24},{24,16},{1,9},{9,1},{17,25},{25,17},{2,10},{10... | collective-permute-start | bytes 196616 | tf_op jit(solution)/shard_map/ppermute | solution.py:276
  64.1 0.5 collective-permute-start.22
  64.6 1.5 %collective-permute-start.23 = (bf16[64,512]{1,0:T(8,128)(2,1)S(1)}, bf16[64,512]{1,0:T(8,128)(2,1)S(1)}, u32[]{:S(2)}, u32[]{:S(2)}) collective-permute-start(bf16[64,512]{1,0:T(8,128)(2,1)S(1)} %get-tuple-element.62.refs_9_), channel_id=1, source_target_pairs={{0,24},{8,16},{16,8},{24,0},{1,25},{9,17},{17,9},{25,1},{2,26},{10... | collective-permute-start | bytes 196616 | tf_op jit(solution)/shard_map/ppermute | solution.py:276
  66.1 0.3 corrected.1
  66.5 0.1 collective-permute-start.24
  66.5 1.2 %collective-permute-done.24.refs_1_ = f32[8,128]{1,0:T(8,128)S(1)} collective-permute-done((f32[8,128]{1,0:T(8,128)S(1)}, f32[8,128]{1,0:T(8,128)S(1)}, u32[]{:S(2)}, u32[]{:S(2)}) %collective-permute-start.24) | collective-permute-done | bytes 4128 | tf_op jit(solution)/shard_map/ppermute | solution.py:276
  67.7 0.1 collective-permute-start.25
  67.8 3.8 %collective-permute-start.26 = (f32[8,128]{1,0:T(8,128)S(1)}, f32[8,128]{1,0:T(8,128)S(1)}, u32[]{:S(2)}, u32[]{:S(2)}) collective-permute-start(f32[8,128]{1,0:T(8,128)S(1)} %add_cores.3.refs_13_), channel_id=1, source_target_pairs={{0,4},{1,5},{2,6},{3,7},{4,0},{5,1},{6,2},{7,3},{8,12},{9,13},{10,... | collective-permute-start | bytes 12296 | tf_op jit(solution)/shard_map/ppermute | solution.py:276
  71.6 3.0 %collective-permute-start.27 = (f32[8,128]{1,0:T(8,128)S(1)}, f32[8,128]{1,0:T(8,128)S(1)}, u32[]{:S(2)}, u32[]{:S(2)}) collective-permute-start(f32[8,128]{1,0:T(8,128)S(1)} %add_cores.3.refs_13_), channel_id=1, source_target_pairs={{0,6},{1,7},{2,4},{3,5},{4,2},{5,3},{6,0},{7,1},{8,14},{9,15},{10,... | collective-permute-start | bytes 12296 | tf_op jit(solution)/shard_map/ppermute | solution.py:276
  74.7 2.4 %collective-permute-done.27.refs_16_ = f32[8,128]{1,0:T(8,128)S(1)} collective-permute-done((f32[8,128]{1,0:T(8,128)S(1)}, f32[8,128]{1,0:T(8,128)S(1)}, u32[]{:S(2)}, u32[]{:S(2)}) %collective-permute-start.27) | collective-permute-done | bytes 4128 | tf_op jit(solution)/shard_map/ppermute | solution.py:276
  77.1 1.8 %last_update.1 = (f32[2,64,512]{2,1,0:T(8,128)}, f32[2,64,512]{2,1,0:T(8,128)}) custom-call(s32[1]{0:T(128)S(6)} %copy.12.refs_0_, f32[4]{0:T(128)S(1)} %pad_maximum_fusion.refs_1_, f32[128,512]{1,0:T(8,128)S(1)} %get-tuple-element.57.refs_2_, f32[2,64,512]{2,1,0:T(8,128)S(1)} %get-tuple-element.58.refs_3_, f32[2,64,512]{2,1,0:T(8,128)S(1)} %get-tuple-element.59.refs_4_, ...), custom_call_target="tpu_custom_call" | custom-call | bytes 1024 | tf_op jit(solution)/shard_map/last_update/pallas_call | solution.py:48
  (42 shorter events, 0.2 us)
Async XLA Ops:
  0.6 14.0 %collective-permute-start.2 = (bf16[1,2,512,2,512]{4,3,2,1,0:T(2,128)(2,1)}, bf16[1,2,512,2,512]{4,3,2,1,0:T(2,128)(2,1)S(1)}, u32[]{:S(2)}, u32[]{:S(2)}) collective-permute-start(bf16[1,2,512,2,512]{4,3,2,1,0:T(2,128)(2,1)} %refs_1_.1), channel_id=1, source_target_pairs={{0,1},{1,0},{2,3},{3,2},{4,5},{5,4},{6,7},{7,6},{8,9},{9,8},{10,11... | collective-permute-start | bytes 6291464 | tf_op jit(solution)/shard_map/ppermute | solution.py:276
  1.1 6.8 %collective-permute-start.1 = (bf16[2,512,512]{2,1,0:T(8,128)(2,1)}, bf16[2,512,512]{2,1,0:T(8,128)(2,1)S(1)}, u32[]{:S(2)}, u32[]{:S(2)}) collective-permute-start(bf16[2,512,512]{2,1,0:T(8,128)(2,1)} %bitcast.10), channel_id=1, source_target_pairs={{0,1},{1,0},{2,3},{3,2},{4,5},{5,4},{6,7},{7,6},{8,9},{9,8},{10,11... | collective-permute-start | bytes 3145736 | tf_op jit(solution)/shard_map/ppermute | solution.py:276
  1.2 0.9 %copy-start.2 = (f32[1,2,64,512]{3,2,1,0:T(8,128)S(1)}, f32[1,2,64,512]{3,2,1,0:T(8,128)}, u32[]{:S(2)}) copy-start(f32[1,2,64,512]{3,2,1,0:T(8,128)} %param.9) | copy-start | bytes 786436
  2.2 9.7 %collective-permute-start = (bf16[128,512]{1,0:T(8,128)(2,1)S(1)}, bf16[128,512]{1,0:T(8,128)(2,1)}, u32[]{:S(2)}, u32[]{:S(2)}) collective-permute-start(bf16[128,512]{1,0:T(8,128)(2,1)S(1)} %lower.1.refs_4_.refs_1_), channel_id=1, source_target_pairs={{0,2},{1,3},{2,0},{3,1},{4,6},{5,7},{6,4},{7,5},{8,10},{9,11},{10,... | collective-permute-start | bytes 393224 | tf_op jit(solution)/shard_map/ppermute | solution.py:276
  5.3 19.9 %collective-permute-start.3 = (bf16[128,512]{1,0:T(8,128)(2,1)S(1)}, bf16[128,512]{1,0:T(8,128)(2,1)S(1)}, u32[]{:S(2)}, u32[]{:S(2)}) collective-permute-start(bf16[128,512]{1,0:T(8,128)(2,1)S(1)} %lower.1.refs_4_.refs_1_), channel_id=1, source_target_pairs={{0,4},{1,5},{2,6},{3,7},{4,0},{5,1},{6,2},{7,3},{8,12},{9,13},{10,... | collective-permute-start | bytes 393224 | tf_op jit(solution)/shard_map/ppermute | solution.py:276
  7.9 17.3 %collective-permute-start.4 = (bf16[128,512]{1,0:T(8,128)(2,1)S(1)}, bf16[128,512]{1,0:T(8,128)(2,1)S(1)}, u32[]{:S(2)}, u32[]{:S(2)}) collective-permute-start(bf16[128,512]{1,0:T(8,128)(2,1)S(1)} %lower.1.refs_4_.refs_1_), channel_id=1, source_target_pairs={{0,6},{1,7},{2,4},{3,5},{4,2},{5,3},{6,0},{7,1},{8,14},{9,15},{10,... | collective-permute-start | bytes 393224 | tf_op jit(solution)/shard_map/ppermute | solution.py:276
  7.9 1.2 %copy-start = (bf16[1,2,512,512]{3,2,1,0:T(8,128)(2,1)S(1)}, bf16[1,2,512,512]{3,2,1,0:T(8,128)(2,1)}, u32[]{:S(2)}) copy-start(bf16[1,2,512,512]{3,2,1,0:T(8,128)(2,1)} %param.14) | copy-start | bytes 3145732
  9.2 5.5 %copy-start.4 = (bf16[1,2,512,2,512]{4,3,2,1,0:T(2,128)(2,1)S(1)}, bf16[1,2,512,2,512]{4,3,2,1,0:T(2,128)(2,1)}, u32[]{:S(2)}) copy-start(bf16[1,2,512,2,512]{4,3,2,1,0:T(2,128)(2,1)} %refs_1_.1) | copy-start | bytes 6291460
  10.2 15.0 %collective-permute-start.5 = (bf16[64,512]{1,0:T(8,128)(2,1)S(1)}, bf16[64,512]{1,0:T(8,128)(2,1)S(1)}, u32[]{:S(2)}, u32[]{:S(2)}) collective-permute-start(bf16[64,512]{1,0:T(8,128)(2,1)S(1)} %get-tuple-element.40), channel_id=1, source_target_pairs={{0,2},{1,3},{2,0},{3,1},{4,6},{5,7},{6,4},{7,5},{8,10},{9,11},{10,... | collective-permute-start | bytes 196616 | tf_op jit(solution)/shard_map/ppermute | solution.py:276
  11.9 13.3 %collective-permute-start.6 = (bf16[64,512]{1,0:T(8,128)(2,1)S(1)}, bf16[64,512]{1,0:T(8,128)(2,1)S(1)}, u32[]{:S(2)}, u32[]{:S(2)}) collective-permute-start(bf16[64,512]{1,0:T(8,128)(2,1)S(1)} %get-tuple-element.41), channel_id=1, source_target_pairs={{0,4},{1,5},{2,6},{3,7},{4,0},{5,1},{6,2},{7,3},{8,12},{9,13},{10,... | collective-permute-start | bytes 196616 | tf_op jit(solution)/shard_map/ppermute | solution.py:276
  14.7 10.5 %collective-permute-start.7 = (bf16[64,512]{1,0:T(8,128)(2,1)S(1)}, bf16[64,512]{1,0:T(8,128)(2,1)S(1)}, u32[]{:S(2)}, u32[]{:S(2)}) collective-permute-start(bf16[64,512]{1,0:T(8,128)(2,1)S(1)} %get-tuple-element.42), channel_id=1, source_target_pairs={{0,6},{1,7},{2,4},{3,5},{4,2},{5,3},{6,0},{7,1},{8,14},{9,15},{10,... | collective-permute-start | bytes 196616 | tf_op jit(solution)/shard_map/ppermute | solution.py:276
  14.7 8.0 %copy-start.1 = (bf16[1,2,512,512]{3,2,1,0:T(8,128)(2,1)S(1)}, bf16[1,2,512,512]{3,2,1,0:T(8,128)(2,1)}, u32[]{:S(2)}) copy-start(bf16[1,2,512,512]{3,2,1,0:T(8,128)(2,1)} %param.14) | copy-start | bytes 3145732
  22.7 2.5 %copy-start.3 = (f32[1,2,64,512]{3,2,1,0:T(8,128)S(1)}, f32[1,2,64,512]{3,2,1,0:T(8,128)}, u32[]{:S(2)}) copy-start(f32[1,2,64,512]{3,2,1,0:T(8,128)} %param.9) | copy-start | bytes 786436
  27.3 34.2 %copy-start.5 = (f32[2,64,512]{2,1,0:T(8,128)S(1)}, f32[2,64,512]{2,1,0:T(8,128)}, u32[]{:S(2)}) copy-start(f32[2,64,512]{2,1,0:T(8,128)} %refs_7_.3) | copy-start | bytes 786436
  27.3 34.1 %copy-start.6 = (f32[1,2,64,512]{3,2,1,0:T(8,128)S(1)}, f32[1,2,64,512]{3,2,1,0:T(8,128)}, u32[]{:S(2)}) copy-start(f32[1,2,64,512]{3,2,1,0:T(8,128)} %param.10) | copy-start | bytes 786436
  27.3 34.1 %copy-start.7 = (f32[1,2,64,512]{3,2,1,0:T(8,128)S(1)}, f32[1,2,64,512]{3,2,1,0:T(8,128)}, u32[]{:S(2)}) copy-start(f32[1,2,64,512]{3,2,1,0:T(8,128)} %param.11) | copy-start | bytes 786436
  27.4 34.1 %copy-start.8 = (f32[2,64,512]{2,1,0:T(8,128)S(1)}, f32[2,64,512]{2,1,0:T(8,128)}, u32[]{:S(2)}) copy-start(f32[2,64,512]{2,1,0:T(8,128)} %refs_6_.1) | copy-start | bytes 786436
  27.4 10.3 %collective-permute-start.9 = (bf16[128,512]{1,0:T(8,128)(2,1)S(1)}, bf16[128,512]{1,0:T(8,128)(2,1)S(1)}, u32[]{:S(2)}, u32[]{:S(2)}) collective-permute-start(bf16[128,512]{1,0:T(8,128)(2,1)S(1)} %get-tuple-element.45), channel_id=1, source_target_pairs={{0,2},{1,3},{2,0},{3,1},{4,6},{5,7},{6,4},{7,5},{8,10},{9,11},{10,... | collective-permute-start | bytes 393224 | tf_op jit(solution)/shard_map/ppermute | solution.py:276
  28.3 18.9 %collective-permute-start.11 = (bf16[192,512]{1,0:T(8,128)(2,1)S(1)}, bf16[192,512]{1,0:T(8,128)(2,1)S(1)}, u32[]{:S(2)}, u32[]{:S(2)}) collective-permute-start(bf16[192,512]{1,0:T(8,128)(2,1)S(1)} %get-tuple-element.49), channel_id=1, source_target_pairs={{0,2},{1,3},{2,0},{3,1},{4,6},{5,7},{6,4},{7,5},{8,10},{9,11},{10,... | collective-permute-start | bytes 589832 | tf_op jit(solution)/shard_map/ppermute | solution.py:276
  29.5 17.8 %collective-permute-start.12 = (bf16[192,512]{1,0:T(8,128)(2,1)S(1)}, bf16[192,512]{1,0:T(8,128)(2,1)S(1)}, u32[]{:S(2)}, u32[]{:S(2)}) collective-permute-start(bf16[192,512]{1,0:T(8,128)(2,1)S(1)} %get-tuple-element.50), channel_id=1, source_target_pairs={{0,4},{1,5},{2,6},{3,7},{4,0},{5,1},{6,2},{7,3},{8,12},{9,13},{10,... | collective-permute-start | bytes 589832 | tf_op jit(solution)/shard_map/ppermute | solution.py:276
  31.9 16.3 %collective-permute-start.13 = (bf16[192,512]{1,0:T(8,128)(2,1)S(1)}, bf16[192,512]{1,0:T(8,128)(2,1)S(1)}, u32[]{:S(2)}, u32[]{:S(2)}) collective-permute-start(bf16[192,512]{1,0:T(8,128)(2,1)S(1)} %get-tuple-element.51), channel_id=1, source_target_pairs={{0,6},{1,7},{2,4},{3,5},{4,2},{5,3},{6,0},{7,1},{8,14},{9,15},{10,... | collective-permute-start | bytes 589832 | tf_op jit(solution)/shard_map/ppermute | solution.py:276
  33.3 15.7 %collective-permute-start.14 = (f32[2,64,512]{2,1,0:T(8,128)S(1)}, f32[2,64,512]{2,1,0:T(8,128)S(1)}, u32[]{:S(2)}, u32[]{:S(2)}) collective-permute-start(f32[2,64,512]{2,1,0:T(8,128)S(1)} %get-tuple-element.53.refs_0_), channel_id=1, source_target_pairs={{0,8},{8,0},{16,24},{24,16},{1,9},{9,1},{17,25},{25,17},{2,10},{10... | collective-permute-start | bytes 786440 | tf_op jit(solution)/shard_map/ppermute | solution.py:276
  37.7 9.5 %collective-permute-start.8 = (bf16[128,512]{1,0:T(8,128)(2,1)S(1)}, bf16[128,512]{1,0:T(8,128)(2,1)S(1)}, u32[]{:S(2)}, u32[]{:S(2)}) collective-permute-start(bf16[128,512]{1,0:T(8,128)(2,1)S(1)} %get-tuple-element.44), channel_id=1, source_target_pairs={{0,2},{1,3},{2,0},{3,1},{4,6},{5,7},{6,4},{7,5},{8,10},{9,11},{10,... | collective-permute-start | bytes 393224 | tf_op jit(solution)/shard_map/ppermute | solution.py:276
  48.9 6.2 %collective-permute-start.17 = (bf16[256,512]{1,0:T(8,128)(2,1)S(1)}, bf16[256,512]{1,0:T(8,128)(2,1)S(1)}, u32[]{:S(2)}, u32[]{:S(2)}) collective-permute-start(bf16[256,512]{1,0:T(8,128)(2,1)S(1)} %get-tuple-element.55.refs_4_), channel_id=1, source_target_pairs={{0,1},{1,0},{2,3},{3,2},{4,5},{5,4},{6,7},{7,6},{8,9},{9,8},{10,11... | collective-permute-start | bytes 786440 | tf_op jit(solution)/shard_map/ppermute | solution.py:276
  49.0 11.2 %collective-permute-start.15 = (f32[2,64,512]{2,1,0:T(8,128)S(1)}, f32[2,64,512]{2,1,0:T(8,128)S(1)}, u32[]{:S(2)}, u32[]{:S(2)}) collective-permute-start(f32[2,64,512]{2,1,0:T(8,128)S(1)} %add_reps.2.refs_0_), channel_id=1, source_target_pairs={{0,16},{8,24},{16,0},{24,8},{1,17},{9,25},{17,1},{25,9},{2,18},{10... | collective-permute-start | bytes 786440 | tf_op jit(solution)/shard_map/ppermute | solution.py:276
  50.7 10.1 %collective-permute-start.10 = (bf16[128,512]{1,0:T(8,128)(2,1)S(1)}, bf16[128,512]{1,0:T(8,128)(2,1)S(1)}, u32[]{:S(2)}, u32[]{:S(2)}) collective-permute-start(bf16[128,512]{1,0:T(8,128)(2,1)S(1)} %get-tuple-element.47), channel_id=1, source_target_pairs={{0,4},{1,5},{2,6},{3,7},{4,0},{5,1},{6,2},{7,3},{8,12},{9,13},{10,... | collective-permute-start | bytes 393224 | tf_op jit(solution)/shard_map/ppermute | solution.py:276
  53.9 1.2 %collective-permute-start.16 = (f32[8,128]{1,0:T(8,128)S(1)}, f32[8,128]{1,0:T(8,128)S(1)}, u32[]{:S(2)}, u32[]{:S(2)}) collective-permute-start(f32[8,128]{1,0:T(8,128)S(1)} %get-tuple-element.54.refs_0_), channel_id=1, source_target_pairs={{0,1},{1,0},{2,3},{3,2},{4,5},{5,4},{6,7},{7,6},{8,9},{9,8},{10,11... | collective-permute-start | bytes 12296 | tf_op jit(solution)/shard_map/ppermute | solution.py:276
  55.1 5.7 %collective-permute-start.18 = (f32[8,128]{1,0:T(8,128)S(1)}, f32[8,128]{1,0:T(8,128)S(1)}, u32[]{:S(2)}, u32[]{:S(2)}) collective-permute-start(f32[8,128]{1,0:T(8,128)S(1)} %add_cores.2.refs_9_), channel_id=1, source_target_pairs={{0,2},{1,3},{2,0},{3,1},{4,6},{5,7},{6,4},{7,5},{8,10},{9,11},{10,... | collective-permute-start | bytes 12296 | tf_op jit(solution)/shard_map/ppermute | solution.py:276
  55.5 5.2 %collective-permute-start.19 = (f32[8,128]{1,0:T(8,128)S(1)}, f32[8,128]{1,0:T(8,128)S(1)}, u32[]{:S(2)}, u32[]{:S(2)}) collective-permute-start(f32[8,128]{1,0:T(8,128)S(1)} %add_cores.2.refs_9_), channel_id=1, source_target_pairs={{0,4},{1,5},{2,6},{3,7},{4,0},{5,1},{6,2},{7,3},{8,12},{9,13},{10,... | collective-permute-start | bytes 12296 | tf_op jit(solution)/shard_map/ppermute | solution.py:276
  56.1 5.4 %collective-permute-start.20 = (f32[8,128]{1,0:T(8,128)S(1)}, f32[8,128]{1,0:T(8,128)S(1)}, u32[]{:S(2)}, u32[]{:S(2)}) collective-permute-start(f32[8,128]{1,0:T(8,128)S(1)} %add_cores.2.refs_9_), channel_id=1, source_target_pairs={{0,6},{1,7},{2,4},{3,5},{4,2},{5,3},{6,0},{7,1},{8,14},{9,15},{10,... | collective-permute-start | bytes 12296 | tf_op jit(solution)/shard_map/ppermute | solution.py:276
  62.6 14.5 %collective-permute-start.21 = (bf16[64,512]{1,0:T(8,128)(2,1)S(1)}, bf16[64,512]{1,0:T(8,128)(2,1)S(1)}, u32[]{:S(2)}, u32[]{:S(2)}) collective-permute-start(bf16[64,512]{1,0:T(8,128)(2,1)S(1)} %get-tuple-element.62.refs_9_), channel_id=1, source_target_pairs={{0,8},{8,0},{16,24},{24,16},{1,9},{9,1},{17,25},{25,17},{2,10},{10... | collective-permute-start | bytes 196616 | tf_op jit(solution)/shard_map/ppermute | solution.py:276
  64.1 12.9 %collective-permute-start.22 = (bf16[64,512]{1,0:T(8,128)(2,1)S(1)}, bf16[64,512]{1,0:T(8,128)(2,1)S(1)}, u32[]{:S(2)}, u32[]{:S(2)}) collective-permute-start(bf16[64,512]{1,0:T(8,128)(2,1)S(1)} %get-tuple-element.62.refs_9_), channel_id=1, source_target_pairs={{0,16},{8,24},{16,0},{24,8},{1,17},{9,25},{17,1},{25,9},{2,18},{10... | collective-permute-start | bytes 196616 | tf_op jit(solution)/shard_map/ppermute | solution.py:276
  64.6 12.4 %collective-permute-start.23 = (bf16[64,512]{1,0:T(8,128)(2,1)S(1)}, bf16[64,512]{1,0:T(8,128)(2,1)S(1)}, u32[]{:S(2)}, u32[]{:S(2)}) collective-permute-start(bf16[64,512]{1,0:T(8,128)(2,1)S(1)} %get-tuple-element.62.refs_9_), channel_id=1, source_target_pairs={{0,24},{8,16},{16,8},{24,0},{1,25},{9,17},{17,9},{25,1},{2,26},{10... | collective-permute-start | bytes 196616 | tf_op jit(solution)/shard_map/ppermute | solution.py:276
  66.5 1.2 %collective-permute-start.24 = (f32[8,128]{1,0:T(8,128)S(1)}, f32[8,128]{1,0:T(8,128)S(1)}, u32[]{:S(2)}, u32[]{:S(2)}) collective-permute-start(f32[8,128]{1,0:T(8,128)S(1)} %get-tuple-element.63.refs_0_), channel_id=1, source_target_pairs={{0,1},{1,0},{2,3},{3,2},{4,5},{5,4},{6,7},{7,6},{8,9},{9,8},{10,11... | collective-permute-start | bytes 12296 | tf_op jit(solution)/shard_map/ppermute | solution.py:276
  67.7 3.9 %collective-permute-start.25 = (f32[8,128]{1,0:T(8,128)S(1)}, f32[8,128]{1,0:T(8,128)S(1)}, u32[]{:S(2)}, u32[]{:S(2)}) collective-permute-start(f32[8,128]{1,0:T(8,128)S(1)} %add_cores.3.refs_13_), channel_id=1, source_target_pairs={{0,2},{1,3},{2,0},{3,1},{4,6},{5,7},{6,4},{7,5},{8,10},{9,11},{10,... | collective-permute-start | bytes 12296 | tf_op jit(solution)/shard_map/ppermute | solution.py:276
  67.8 6.8 %collective-permute-start.26 = (f32[8,128]{1,0:T(8,128)S(1)}, f32[8,128]{1,0:T(8,128)S(1)}, u32[]{:S(2)}, u32[]{:S(2)}) collective-permute-start(f32[8,128]{1,0:T(8,128)S(1)} %add_cores.3.refs_13_), channel_id=1, source_target_pairs={{0,4},{1,5},{2,6},{3,7},{4,0},{5,1},{6,2},{7,3},{8,12},{9,13},{10,... | collective-permute-start | bytes 12296 | tf_op jit(solution)/shard_map/ppermute | solution.py:276
  71.6 5.4 %collective-permute-start.27 = (f32[8,128]{1,0:T(8,128)S(1)}, f32[8,128]{1,0:T(8,128)S(1)}, u32[]{:S(2)}, u32[]{:S(2)}) collective-permute-start(f32[8,128]{1,0:T(8,128)S(1)} %add_cores.3.refs_13_), channel_id=1, source_target_pairs={{0,6},{1,7},{2,4},{3,5},{4,2},{5,3},{6,0},{7,1},{8,14},{9,15},{10,... | collective-permute-start | bytes 12296 | tf_op jit(solution)/shard_map/ppermute | solution.py:276

commit v4 on v3

--- a/solution.py
+++ b/solution.py
@@ -67,17 +67,25 @@
 
 def split_kernel(rows, side_ref, own_ref, sib_ref, *outs):
     core = side_ref[0]
+    toks, width = own_ref.shape[2], own_ref.shape[4]
+    size = math.gcd(toks, 256)
+    row = lax.broadcasted_iota(jnp.int32, (size, 2 * size), 0)
+    column = lax.broadcasted_iota(jnp.int32, (size, 2 * size), 1)
+    takes = [(column == 2 * row + frag).astype(BF16) for frag in range(2)]
     for step in range(2):
         for goal_ref, out_ref in zip((own_ref, sib_ref), outs):
-            first, second = (goal_ref[0, step, :, frag, :].astype(F32) for frag in range(2))
-            for chip in range(out_ref.shape[1]):
-                for which in range(2):
-
-                    @pl.when(core == which)
-                    def _():
-                        at = (2 * chip + which) * rows
-                        pair = [first[:, at : at + rows], second[:, at : at + rows]]
-                        out_ref[step, chip] = jnp.concatenate(pair, 1).astype(BF16)
+            for start in range(0, toks, size):
+                part = pl.ds(start, size)
+                goal = goal_ref[0, step, part].reshape(2 * size, width)
+                first, second = (jnp.dot(take, goal, preferred_element_type=F32) for take in takes)
+                for chip in range(out_ref.shape[1]):
+                    for which in range(2):
+
+                        @pl.when(core == which)
+                        def _():
+                            at = (2 * chip + which) * rows
+                            pair = [first[:, at : at + rows], second[:, at : at + rows]]
+                            out_ref[step, chip, part] = jnp.concatenate(pair, 1).astype(BF16)
 
 
 def chunk_grad(scale, grad_scale, step, group, place_ref, w_refs, token_refs, goal_refs):
@@ -104,30 +112,30 @@
             ref[...] = value
 
 
-def far_kernel(scales, near, far, place_ref, *refs):
-    size = len(far)
-    chips = len(near) + size
+def far_kernel(scales, near, far, place_ref, first_ref, *refs):
+    size, ready = len(far), len(near)
+    chips = ready + size
     w_refs, token_refs, goal_refs = refs[:size], refs[size : size + 2], refs[size + 2 : size + 4]
-    near_refs = refs[size + 4 : size + 4 + len(near)]
-    strip_refs = refs[size + 4 + len(near) : size + 4 + len(near) + chips]
-    weights_ref, *outs, copy_ref = refs[size + 4 + len(near) + chips :]
-    made = dict(zip(near, (ref[...] for ref in near_refs)))
+    near_refs, refs = refs[size + 4 : size + 4 + 2 * ready], refs[size + 4 + 2 * ready :]
+    strip_refs, (weights_ref, *outs, keep_ref, send_ref, copy_ref) = refs[:chips], refs[chips:]
+    made = dict(zip(near, (ref[...] for ref in near_refs[:ready])))
     made.update(zip(far, chunk_grad(*scales, 0, far, place_ref, w_refs, token_refs, goal_refs)))
     strip = tree_sum(ref[...].astype(F32) for ref in strip_refs).astype(BF16)
-    for k, ref in enumerate(outs[:chips]):
+    for k, ref in enumerate(outs):
         rows = made[k].shape[0]
         ref[pl.ds(0, rows), :] = made[k]
         ref[pl.ds(rows, strip.shape[0]), :] = strip
-    made = chunk_grad(*scales, 1, far, place_ref, w_refs, token_refs, goal_refs)
-    for ref, value in zip(outs[chips:], made):
-        ref[...] = value
-    copy_ref[...] = weights_ref[...]
-
-
-def halve_kernel(*refs):
-    count = len(refs) // 3
-    for keep_ref, got_ref, out_ref in zip(refs[:count], refs[count:], refs[2 * count :]):
-        out_ref[...] = (keep_ref[...].astype(F32) + got_ref[...].astype(F32)).astype(BF16)
+    made = dict(zip(near, (ref[...] for ref in near_refs[ready:])))
+    made.update(zip(far, chunk_grad(*scales, 1, far, place_ref, w_refs, token_refs, goal_refs)))
+    for k in range(chips):
+        (send_ref if k % 2 else keep_ref)[k // 2] = made[k]
+    copy_ref[...] = jnp.where(first_ref[0] == 0, weights_ref[0], weights_ref[1])
+
+
+def halve_kernel(keep_ref, got_ref, next_ref, send_ref):
+    for k in range(keep_ref.shape[0]):
+        total = (keep_ref[k].astype(F32) + got_ref[k].astype(F32)).astype(BF16)
+        (send_ref if k % 2 else next_ref)[k // 2] = total
 
 
 def gram_kernel(step, side_ref, place_ref, xo_ref, xs_ref, *refs):
@@ -141,7 +149,7 @@
 
 
 def add_kernel(*refs):
-    refs[-1][...] = tree_sum(ref[...] for ref in refs[:-1])
+    refs[-1][...] = tree_sum(ref[...].astype(F32) for ref in refs[:-1]).astype(refs[-1].dtype)
 
 
 def sum_kernel(place_ref, *refs):
@@ -193,7 +201,7 @@
     moment_one = beta_one * moment_one + (1.0 - beta_one) * clipped
     moment_two = beta_two * moment_two + (1.0 - beta_two) * clipped * clipped
     update = moment_one / one / (jnp.sqrt(moment_two / two) + adam_eps)
-    return moment_one, moment_two, update, weights - inner_rate * (update + decay_rate * weights)
+    return moment_one, moment_two, weights - inner_rate * (update + decay_rate * weights)
 
 
 def outer_step(theta, speed, delta):
@@ -211,39 +219,36 @@
     sends = []
     for frag in range(2):
         part = pl.ds(frag * rows, rows)
-        m, v, update, after = adam(
+        m, v, after = adam(
             grad_ref[part, :], norms, correct_ref[0], correct_ref[1], m_ref[frag], v_ref[frag], w_ref[frag]
         )
         m_out[frag] = m
         v_out[frag] = v
-        sends.append(update)
+        sends.append(after)
         old = outer_ref[frag]
-        theta = outer_step(old, vel_ref[frag], old - total_ref[frag] * (1.0 / replicas))
+        theta = outer_step(old, vel_ref[frag], old - total_ref[...] * (1.0 / replicas))
         now = first == frag
         theta_out[frag] = jnp.where(now, theta, old)
         after = jnp.where(now, mixing * theta + (1.0 - mixing) * after, after)
         w_out[frag] = after
         dw_out[part, :] = after.astype(BF16).astype(F32) - w_ref[frag].astype(BF16).astype(F32)
-    send_out[...] = jnp.where(first == 0, sends[1], sends[0]).astype(BF16)
+    send_out[...] = jnp.where(first == 0, sends[1], sends[0])
 
 
 def last_kernel(
-    replicas, count, first_ref, correct_ref, grad_ref, m_ref, v_ref, w_ref, outer_ref, vel_ref, total_ref, *refs
+    replicas, count, first_ref, correct_ref, grad_ref, m_ref, v_ref, w_ref, outer_ref, vel_ref, moved_ref, *refs
 ):
-    updates = refs[:replicas]
-    norms = refs[replicas : replicas + count]
-    outer_out, inner_out = refs[replicas + count :]
+    norms = refs[:count]
+    outer_out, inner_out = refs[count:]
     rows = grad_ref.shape[0] // 2
     first = first_ref[0]
-    moved = tree_sum(ref[...].astype(F32) for ref in updates)
     for frag in range(2):
         part = pl.ds(frag * rows, rows)
         after = adam(
             grad_ref[part, :], norms, correct_ref[2], correct_ref[3], m_ref[frag], v_ref[frag], w_ref[frag]
-        )[3]
+        )[2]
         old = outer_ref[frag]
-        mean = ((1.0 - inner_rate * decay_rate) * total_ref[frag] - inner_rate * moved) * (1.0 / replicas)
-        theta = outer_step(old, vel_ref[frag], old - mean)
+        theta = outer_step(old, vel_ref[frag], old - moved_ref[...] * (1.0 / replicas))
         now = first != frag
         outer_out[frag] = jnp.where(now, theta, old)
         inner_out[frag] = jnp.where(now, mixing * theta + (1.0 - mixing) * after, after)
@@ -277,12 +282,12 @@
 
     sibling = lambda x: swap(x, "shard", shards, 1)
     across = lambda x, by: swap(x, "shard", shards, 2 * by)
-    over_rep = lambda x, by: x if by == 0 else swap(x, "rep", replicas, by)
 
     shape = jax.ShapeDtypeStruct
     block = shape((2 * rows, width), BF16)
     tile = shape((8, 128), F32)
     state = shape((2, rows, width), F32)
+    row_block = shape((rows, width), F32)
     flat = shape((2 * rows, width), F32)
     side = jnp.reshape(core, (1,)).astype(jnp.int32)
     place = jnp.stack([chip ^ k for k in range(chips)]).astype(jnp.int32)
@@ -328,30 +333,25 @@
         [held[k] for k in near] + [own_x, sib_x, own_t, sib_t],
         "near_grad",
     )
-    joint = call(
+    pairs = shape((chips // 2, 2 * rows, width), BF16)
+    *joint, keep, send, sums = call(
         functools.partial(far_kernel, scales, near, far),
-        [shape((2 * rows + width // shards, width), BF16)] * chips + [block] * len(far) + [state],
-        [place],
-        [held[k] for k in far] + [own_x, sib_x, own_t, sib_t, *made[: len(near)], *spread(strips), weights],
+        [shape((2 * rows + width // shards, width), BF16)] * chips + [pairs, pairs, row_block],
+        [place, first_fragment],
+        [held[k] for k in far] + [own_x, sib_x, own_t, sib_t, *made, *spread(strips), weights],
         "far_grad",
     )
-    pieces_one = spread(joint[:chips])
-    made = [*made[len(near) :], *joint[chips:-1]]
-    early = joint[-1]
-    keep, got = made[0::2], [across(x, 1) for x in made[1::2]]
-    ready = got
-    bit = 2
-    while bit < chips:
-        made = call(halve_kernel, [block] * len(keep), [], [*keep, *got], "halve")
-        keep, got = made[0::2], [across(x, bit) for x in made[1::2]]
-        bit *= 2
-    pieces_two = [keep[0], got[0]]
-
-    sums = early
-    by = 1
-    while by < replicas:
-        (sums,) = call(add_kernel, [state], [], [sums, swap(sums, "rep", replicas, by)], "add_reps")
-        by *= 2
+    got = across(send, 1)
+    pieces_one = spread(joint)
+
+    def over_rep(x, name, after):
+        by = 1
+        while by < replicas:
+            (x,) = call(add_kernel, [row_block], [], [x, swap(x, "rep", replicas, by)], name, after)
+            by *= 2
+        return x
+
+    sums = over_rep(sums, "add_reps", [])
 
     grad, squares, own_g = call(
         sum_kernel,
@@ -359,10 +359,17 @@
         [place],
         pieces_one,
         "sum_pieces",
-        ready,
+        [sums, got],
     )
     sib_g = sibling(own_g)
     norms = norm_parts(squares, [sib_g])
+    bit = 2
+    while bit < chips:
+        half = shape((keep.shape[0] // 2, 2 * rows, width), BF16)
+        keep, send = call(halve_kernel, [half, half], [], [keep, got], "halve", norms[:1])
+        got = across(send, bit)
+        bit *= 2
+    pieces_two = [keep[0], got[0]]
 
     count = step_count[0].astype(F32)
     correct = jnp.stack(
@@ -370,14 +377,11 @@
     )
     m, v, middle, change, outer, moved = call(
         functools.partial(first_kernel, replicas, chips),
-        [state, state, state, flat, state, shape((rows, width), BF16)],
+        [state, state, state, flat, state, row_block],
         [first_fragment, correct],
         [grad, first_moment[0], second_moment[0], weights, outer_weights, outer_velocity, sums, *norms],
         "first_update",
-        pieces_two[1:],
-    )
-    updates = [over_rep(moved, k) for k in range(replicas)]
-
+    )
     grad, squares = call(
         functools.partial(correct_kernel, len(pieces_two), scale * grad_scale),
         [flat, tile],
@@ -386,11 +390,12 @@
         "corrected",
     )
     norms = norm_parts(squares, [])
+    moved = over_rep(moved, "add_moves", norms[:1])
     new_outer, new_inner = call(
         functools.partial(last_kernel, replicas, chips),
         [state, state],
         [first_fragment, correct],
-        [grad, m, v, middle, outer, outer_velocity, sums, *updates, *norms],
+        [grad, m, v, middle, outer, outer_velocity, moved, *norms],
         "last_update",
     )
     return (new_outer, new_inner[None])

time: 79.1 us -> 76.8 us (0.971)
  starting transfers between devices: 38 us -> 31.8 us
  waiting for transfers between devices: 18.6 us -> 24.2 us
  Pallas kernels: 17.6 us -> 15.9 us
    ppermute x28 -> x26, starting transfers between devices: 38 us -> 31.8 us  [swap(): return lax.ppermute(x, axis, [(i, i ^ by) for i in range(size)])]
    ppermute x28 -> x26, waiting for transfers between devices: 18.6 us -> 24.2 us  [swap(): return lax.ppermute(x, axis, [(i, i ^ by) for i in range(size)])]
    pallas_call x14 -> x16, Pallas kernels: 17.6 us -> 15.9 us  [call(): pl.pallas_call(run, in_specs=[pl.BlockSpec(memory_space=pltpu.SMEM)] * le...]
  transfers between devices with their start and end apart: 28 -> 26, of which waited for: 8 -> 12; matrix products, arithmetic and copies ran while one was open for 0% -> 0% of each run, Pallas kernels for 16% -> 15%
where the time goes in v4:
time: 76.8 us; the launch traced here: 76.6 us
  starting transfers between devices  31.8 us (41%)
  waiting for transfers between devices  24.2 us (32%)
  Pallas kernels  15.9 us (21%)
  between operations  2.32 us (3%)
  local copies, waits for them, and re-layouts  2.22 us (3%)
    ppermute x26, starting transfers between devices, swap(): return lax.ppermute(x, axis, [(i, i ^ by) for i in range(size)])  31.8 us
    ppermute x26, waiting for transfers between devices, swap(): return lax.ppermute(x, axis, [(i, i ^ by) for i in range(size)])  24.2 us
    pallas_call x16, Pallas kernels, call(): pl.pallas_call(run, in_specs=[pl.BlockSpec(memory_space=pltpu.SMEM)] * le...  15.9 us
    unnamed x18, local copies, waits for them, and re-layouts  2.22 us
  transfers between devices with their start and end apart: 26, of which 12 were waited for; matrix products, arithmetic and copies ran while one was open for 0% of the time, Pallas kernels for 15%

profile of v4, /device:TPU:0, one launch (start us, length us, event | category | flops | bytes accessed | tf_op | source)
XLA Modules:
  0.0 76.6 jit_solution(2734991975344097688)
XLA Ops:
  0.6 0.5 collective-permute-start.3
  1.1 0.1 collective-permute-start.2
  1.2 0.9 %copy-done.2 = f32[1,2,64,512]{3,2,1,0:T(8,128)S(1)} copy-done((f32[1,2,64,512]{3,2,1,0:T(8,128)S(1)}, f32[1,2,64,512]{3,2,1,0:T(8,128)}, u32[]{:S(2)}) %copy-start.2) | copy-done | bytes 262168
  2.2 3.1 %collective-permute-start.4 = (bf16[128,512]{1,0:T(8,128)(2,1)S(1)}, bf16[128,512]{1,0:T(8,128)(2,1)}, u32[]{:S(2)}, u32[]{:S(2)}) collective-permute-start(bf16[128,512]{1,0:T(8,128)(2,1)S(1)} %lower.1.refs_4_.refs_1_), channel_id=1, source_target_pairs={{0,2},{1,3},{2,0},{3,1},{4,6},{5,7},{6,4},{7,5},{8,10},{9,11},{10,... | collective-permute-start | bytes 393224 | tf_op jit(solution)/shard_map/ppermute | solution.py:281
  5.3 2.6 %collective-permute-start = (bf16[128,512]{1,0:T(8,128)(2,1)S(1)}, bf16[128,512]{1,0:T(8,128)(2,1)S(1)}, u32[]{:S(2)}, u32[]{:S(2)}) collective-permute-start(bf16[128,512]{1,0:T(8,128)(2,1)S(1)} %lower.1.refs_4_.refs_1_), channel_id=1, source_target_pairs={{0,4},{1,5},{2,6},{3,7},{4,0},{5,1},{6,2},{7,3},{8,12},{9,13},{10,... | collective-permute-start | bytes 393224 | tf_op jit(solution)/shard_map/ppermute | solution.py:281
  7.9 0.1 pad_add_fusion.refs_1_.refs_0_
  7.9 1.2 %copy-done = bf16[1,2,512,512]{3,2,1,0:T(8,128)(2,1)S(1)} copy-done((bf16[1,2,512,512]{3,2,1,0:T(8,128)(2,1)S(1)}, bf16[1,2,512,512]{3,2,1,0:T(8,128)(2,1)}, u32[]{:S(2)}) %copy-start) | copy-done | bytes 1048600
  9.2 1.0 %gram.1 = (bf16[64,512]{1,0:T(8,128)(2,1)S(1)}, bf16[64,512]{1,0:T(8,128)(2,1)S(1)}, bf16[64,512]{1,0:T(8,128)(2,1)S(1)}, bf16[64,512]{1,0:T(8,128)(2,1)S(1)}) custom-call(s32[1]{0:T(128)} %bitcast.refs_0_, s32[4]{0:T(128)S(1)} %pad_add_fusion.refs_1_.refs_0_, bf16[2,512,512]{2,1,0:T(8,128)(2,1)S(1)} %bitcast.13, ...), custom_call_target="tpu_custom_call" | custom-call | bytes 1024 | tf_op jit(solution)/shard_map/gram/pallas_call | solution.py:48
  10.2 1.7 %collective-permute-start.5 = (bf16[64,512]{1,0:T(8,128)(2,1)S(1)}, bf16[64,512]{1,0:T(8,128)(2,1)S(1)}, u32[]{:S(2)}, u32[]{:S(2)}) collective-permute-start(bf16[64,512]{1,0:T(8,128)(2,1)S(1)} %get-tuple-element.41), channel_id=1, source_target_pairs={{0,2},{1,3},{2,0},{3,1},{4,6},{5,7},{6,4},{7,5},{8,10},{9,11},{10,... | collective-permute-start | bytes 196616 | tf_op jit(solution)/shard_map/ppermute | solution.py:281
  11.9 2.7 %collective-permute-start.6 = (bf16[64,512]{1,0:T(8,128)(2,1)S(1)}, bf16[64,512]{1,0:T(8,128)(2,1)S(1)}, u32[]{:S(2)}, u32[]{:S(2)}) collective-permute-start(bf16[64,512]{1,0:T(8,128)(2,1)S(1)} %get-tuple-element.42), channel_id=1, source_target_pairs={{0,4},{1,5},{2,6},{3,7},{4,0},{5,1},{6,2},{7,3},{8,12},{9,13},{10,... | collective-permute-start | bytes 196616 | tf_op jit(solution)/shard_map/ppermute | solution.py:281
  15.3 6.3 %split.1 = (bf16[2,4,512,128]{3,2,1,0:T(8,128)(2,1)S(1)}, bf16[2,4,512,128]{3,2,1,0:T(8,128)(2,1)S(1)}) custom-call(s32[1]{0:T(128)} %bitcast.refs_0_, bf16[1,2,512,2,512]{4,3,2,1,0:T(2,128)(2,1)S(1)} %copy-done.4, bf16[1,2,512,2,512]{4,3,2,1,0:T(2,128)(2,1)S(1)} %collective-permute-done.3.refs_2_, bf16[64,512]{1,0:T(8,128)(2,1)S(1)} %get-tuple-element.34.refs_3_.refs_12_), custom_call_target="tpu_custom_call" | custom-call | bytes 1024 | tf_op jit(solution)/shard_map/split/pallas_call | solution.py:48
  21.7 2.5 %near_grad.1 = (bf16[128,512]{1,0:T(8,128)(2,1)S(1)}, bf16[128,512]{1,0:T(8,128)(2,1)S(1)}, bf16[128,512]{1,0:T(8,128)(2,1)S(1)}, bf16[128,512]{1,0:T(8,128)(2,1)S(1)}) custom-call(s32[4]{0:T(128)S(1)} %pad_add_fusion.refs_1_.refs_0_, bf16[128,512]{1,0:T(8,128)(2,1)S(1)} %lower.1.refs_4_.refs_1_, bf16[128,512]{1,0:T(8,128)(2,1)} %collective-permute-done.4.refs_2_, ...), custom_call_target="tpu_custom_call" | custom-call | bytes 1024 | tf_op jit(solution)/shard_map/near_grad/pallas_call | solution.py:48
  24.2 0.6 collective-permute-done.6.refs_14_
  24.8 2.1 %far_grad.1 = (bf16[192,512]{1,0:T(8,128)(2,1)S(1)}, bf16[192,512]{1,0:T(8,128)(2,1)S(1)}, bf16[192,512]{1,0:T(8,128)(2,1)S(1)}, bf16[192,512]{1,0:T(8,128)(2,1)...) custom-call(s32[4]{0:T(128)S(1)} %pad_add_fusion.refs_1_.refs_0_, ...), custom_call_target="tpu_custom_call" | custom-call | bytes 1024 | tf_op jit(solution)/shard_map/far_grad/pallas_call | solution.py:48
  27.0 1.6 %collective-permute-start.12 = (f32[64,512]{1,0:T(8,128)S(1)}, f32[64,512]{1,0:T(8,128)S(1)}, u32[]{:S(2)}, u32[]{:S(2)}) collective-permute-start(f32[64,512]{1,0:T(8,128)S(1)} %get-tuple-element.50.refs_0_), channel_id=1, source_target_pairs={{0,8},{8,0},{16,24},{24,16},{1,9},{9,1},{17,25},{25,17},{2,10},{10... | collective-permute-start | bytes 393224 | tf_op jit(solution)/shard_map/ppermute | solution.py:281
  28.5 1.3 %collective-permute-start.8 = (bf16[2,128,512]{2,1,0:T(8,128)(2,1)S(1)}, bf16[2,128,512]{2,1,0:T(8,128)(2,1)S(1)}, u32[]{:S(2)}, u32[]{:S(2)}) collective-permute-start(bf16[2,128,512]{2,1,0:T(8,128)(2,1)S(1)} %get-tuple-element.45), channel_id=1, source_target_pairs={{0,2},{1,3},{2,0},{3,1},{4,6},{5,7},{6,4},{7,5},{8,10},{9,11},{10,... | collective-permute-start | bytes 786440 | tf_op jit(solution)/shard_map/ppermute | solution.py:281
  29.8 2.6 %collective-permute-start.10 = (bf16[192,512]{1,0:T(8,128)(2,1)S(1)}, bf16[192,512]{1,0:T(8,128)(2,1)S(1)}, u32[]{:S(2)}, u32[]{:S(2)}) collective-permute-start(bf16[192,512]{1,0:T(8,128)(2,1)S(1)} %get-tuple-element.48), channel_id=1, source_target_pairs={{0,4},{1,5},{2,6},{3,7},{4,0},{5,1},{6,2},{7,3},{8,12},{9,13},{10,... | collective-permute-start | bytes 589832 | tf_op jit(solution)/shard_map/ppermute | solution.py:281
  32.4 0.6 collective-permute-start.11
  32.9 0.4 collective-permute-start.9
  33.3 1.6 %collective-permute-start.13 = (f32[64,512]{1,0:T(8,128)S(1)}, f32[64,512]{1,0:T(8,128)S(1)}, u32[]{:S(2)}, u32[]{:S(2)}) collective-permute-start(f32[64,512]{1,0:T(8,128)S(1)} %add_reps.2.refs_0_), channel_id=1, source_target_pairs={{0,16},{8,24},{16,0},{24,8},{1,17},{9,25},{17,1},{25,9},{2,18},{10... | collective-permute-start | bytes 393224 | tf_op jit(solution)/shard_map/ppermute | solution.py:281
  34.9 3.4 %collective-permute-done.13.refs_1_ = f32[64,512]{1,0:T(8,128)S(1)} collective-permute-done((f32[64,512]{1,0:T(8,128)S(1)}, f32[64,512]{1,0:T(8,128)S(1)}, u32[]{:S(2)}, u32[]{:S(2)}) %collective-permute-start.13) | collective-permute-done | bytes 131104 | tf_op jit(solution)/shard_map/ppermute | solution.py:281
  38.4 7.0 %collective-permute-done.10.refs_3_ = bf16[192,512]{1,0:T(8,128)(2,1)S(1)} collective-permute-done((bf16[192,512]{1,0:T(8,128)(2,1)S(1)}, bf16[192,512]{1,0:T(8,128)(2,1)S(1)}, u32[]{:S(2)}, u32[]{:S(2)}) %collective-permute-start.10) | collective-permute-done | bytes 196640 | tf_op jit(solution)/shard_map/ppermute | solution.py:281
  45.4 2.4 %collective-permute-done.11.refs_4_ = bf16[192,512]{1,0:T(8,128)(2,1)S(1)} collective-permute-done((bf16[192,512]{1,0:T(8,128)(2,1)S(1)}, bf16[192,512]{1,0:T(8,128)(2,1)S(1)}, u32[]{:S(2)}, u32[]{:S(2)}) %collective-permute-start.11) | collective-permute-done | bytes 196640 | tf_op jit(solution)/shard_map/ppermute | solution.py:281
  47.8 0.2 collective-permute-done.9.refs_2_
  48.0 0.6 sum_pieces.1
  48.6 0.1 collective-permute-start.15
  48.7 0.5 collective-permute-start.14
  50.0 0.2 collective-permute-done.14.refs_1_
  50.3 1.3 %collective-permute-start.17 = (f32[8,128]{1,0:T(8,128)S(1)}, f32[8,128]{1,0:T(8,128)S(1)}, u32[]{:S(2)}, u32[]{:S(2)}) collective-permute-start(f32[8,128]{1,0:T(8,128)S(1)} %add_cores.2.refs_2_.refs_9_), channel_id=1, source_target_pairs={{0,2},{1,3},{2,0},{3,1},{4,6},{5,7},{6,4},{7,5},{8,10},{9,11},{10,... | collective-permute-start | bytes 12296 | tf_op jit(solution)/shard_map/ppermute | solution.py:281
  51.6 2.8 %collective-permute-start.18 = (f32[8,128]{1,0:T(8,128)S(1)}, f32[8,128]{1,0:T(8,128)S(1)}, u32[]{:S(2)}, u32[]{:S(2)}) collective-permute-start(f32[8,128]{1,0:T(8,128)S(1)} %add_cores.2.refs_2_.refs_9_), channel_id=1, source_target_pairs={{0,4},{1,5},{2,6},{3,7},{4,0},{5,1},{6,2},{7,3},{8,12},{9,13},{10,... | collective-permute-start | bytes 12296 | tf_op jit(solution)/shard_map/ppermute | solution.py:281
  54.4 0.3 collective-permute-start.19
  54.6 0.1 halve.1
  54.7 1.6 %collective-permute-start.16 = (bf16[1,128,512]{2,1,0:T(8,128)(2,1)S(1)}, bf16[1,128,512]{2,1,0:T(8,128)(2,1)S(1)}, u32[]{:S(2)}, u32[]{:S(2)}) collective-permute-start(bf16[1,128,512]{2,1,0:T(8,128)(2,1)S(1)} %get-tuple-element.54), channel_id=1, source_target_pairs={{0,4},{1,5},{2,6},{3,7},{4,0},{5,1},{6,2},{7,3},{8,12},{9,13},{10,... | collective-permute-start | bytes 393224 | tf_op jit(solution)/shard_map/ppermute | solution.py:281
  56.3 0.1 pad_maximum_fusion.refs_1_
  56.4 3.5 %collective-permute-done.19.refs_12_ = f32[8,128]{1,0:T(8,128)S(1)} collective-permute-done((f32[8,128]{1,0:T(8,128)S(1)}, f32[8,128]{1,0:T(8,128)S(1)}, u32[]{:S(2)}, u32[]{:S(2)}) %collective-permute-start.19) | collective-permute-done | bytes 4128 | tf_op jit(solution)/shard_map/ppermute | solution.py:281
  59.9 1.1 %first_update.1 = (f32[2,64,512]{2,1,0:T(8,128)S(1)}, f32[2,64,512]{2,1,0:T(8,128)S(1)}, f32[2,64,512]{2,1,0:T(8,128)S(1)}, f32[128,512]{1,0:T(8,128)S(1)}, f32[...) custom-call(s32[1]{0:T(128)S(6)} %copy.12.refs_1_.refs_0_, f32[4]{0:T(128)S(1)} %pad_maximum_fusion.refs_1_, ...), custom_call_target="tpu_custom_call" | custom-call | bytes 1024 | tf_op jit(solution)/shard_map/first_update/pallas_call | solution.py:48
  61.0 0.6 collective-permute-start.20
  61.6 1.8 %collective-permute-done.16 = bf16[1,128,512]{2,1,0:T(8,128)(2,1)S(1)} collective-permute-done((bf16[1,128,512]{2,1,0:T(8,128)(2,1)S(1)}, bf16[1,128,512]{2,1,0:T(8,128)(2,1)S(1)}, u32[]{:S(2)}, u32[]{:S(2)}) %collective-permute-start.16) | collective-permute-done | bytes 131104 | tf_op jit(solution)/shard_map/ppermute | solution.py:281
  63.3 0.3 corrected.1
  63.7 0.1 collective-permute-start.21
  63.8 1.2 %collective-permute-done.21.refs_1_ = f32[8,128]{1,0:T(8,128)S(1)} collective-permute-done((f32[8,128]{1,0:T(8,128)S(1)}, f32[8,128]{1,0:T(8,128)S(1)}, u32[]{:S(2)}, u32[]{:S(2)}) %collective-permute-start.21) | collective-permute-done | bytes 4128 | tf_op jit(solution)/shard_map/ppermute | solution.py:281
  64.9 1.1 %collective-permute-done.20.refs_1_ = f32[64,512]{1,0:T(8,128)S(1)} collective-permute-done((f32[64,512]{1,0:T(8,128)S(1)}, f32[64,512]{1,0:T(8,128)S(1)}, u32[]{:S(2)}, u32[]{:S(2)}) %collective-permute-start.20) | collective-permute-done | bytes 131104 | tf_op jit(solution)/shard_map/ppermute | solution.py:281
  66.0 1.6 %collective-permute-start.22 = (f32[64,512]{1,0:T(8,128)S(1)}, f32[64,512]{1,0:T(8,128)S(1)}, u32[]{:S(2)}, u32[]{:S(2)}) collective-permute-start(f32[64,512]{1,0:T(8,128)S(1)} %add_moves.2.refs_0_), channel_id=1, source_target_pairs={{0,16},{8,24},{16,0},{24,8},{1,17},{9,25},{17,1},{25,9},{2,18},{10... | collective-permute-start | bytes 393224 | tf_op jit(solution)/shard_map/ppermute | solution.py:281
  67.6 1.8 %collective-permute-start.24 = (f32[8,128]{1,0:T(8,128)S(1)}, f32[8,128]{1,0:T(8,128)S(1)}, u32[]{:S(2)}, u32[]{:S(2)}) collective-permute-start(f32[8,128]{1,0:T(8,128)S(1)} %add_cores.3.refs_2_.refs_9_), channel_id=1, source_target_pairs={{0,4},{1,5},{2,6},{3,7},{4,0},{5,1},{6,2},{7,3},{8,12},{9,13},{10,... | collective-permute-start | bytes 12296 | tf_op jit(solution)/shard_map/ppermute | solution.py:281
  69.4 2.6 %collective-permute-start.25 = (f32[8,128]{1,0:T(8,128)S(1)}, f32[8,128]{1,0:T(8,128)S(1)}, u32[]{:S(2)}, u32[]{:S(2)}) collective-permute-start(f32[8,128]{1,0:T(8,128)S(1)} %add_cores.3.refs_2_.refs_9_), channel_id=1, source_target_pairs={{0,6},{1,7},{2,4},{3,5},{4,2},{5,3},{6,0},{7,1},{8,14},{9,15},{10,... | collective-permute-start | bytes 12296 | tf_op jit(solution)/shard_map/ppermute | solution.py:281
  72.0 0.1 collective-permute-done.24.refs_11_
  72.1 2.7 %collective-permute-done.25.refs_12_ = f32[8,128]{1,0:T(8,128)S(1)} collective-permute-done((f32[8,128]{1,0:T(8,128)S(1)}, f32[8,128]{1,0:T(8,128)S(1)}, u32[]{:S(2)}, u32[]{:S(2)}) %collective-permute-start.25) | collective-permute-done | bytes 4128 | tf_op jit(solution)/shard_map/ppermute | solution.py:281
  74.8 1.8 %last_update.1 = (f32[2,64,512]{2,1,0:T(8,128)}, f32[2,64,512]{2,1,0:T(8,128)}) custom-call(s32[1]{0:T(128)S(6)} %copy.12.refs_1_.refs_0_, f32[4]{0:T(128)S(1)} %pad_maximum_fusion.refs_1_, f32[128,512]{1,0:T(8,128)S(1)} %get-tuple-element.57.refs_2_, f32[2,64,512]{2,1,0:T(8,128)S(1)} %get-tuple-element.58.refs_3_, ...), custom_call_target="tpu_custom_call" | custom-call | bytes 1024 | tf_op jit(solution)/shard_map/last_update/pallas_call | solution.py:48
  (40 shorter events, 0.2 us)
Async XLA Ops:
  0.6 14.0 %collective-permute-start.3 = (bf16[1,2,512,2,512]{4,3,2,1,0:T(2,128)(2,1)}, bf16[1,2,512,2,512]{4,3,2,1,0:T(2,128)(2,1)S(1)}, u32[]{:S(2)}, u32[]{:S(2)}) collective-permute-start(bf16[1,2,512,2,512]{4,3,2,1,0:T(2,128)(2,1)} %refs_1_.2), channel_id=1, source_target_pairs={{0,1},{1,0},{2,3},{3,2},{4,5},{5,4},{6,7},{7,6},{8,9},{9,8},{10,11... | collective-permute-start | bytes 6291464 | tf_op jit(solution)/shard_map/ppermute | solution.py:281
  1.1 6.8 %collective-permute-start.2 = (bf16[2,512,512]{2,1,0:T(8,128)(2,1)}, bf16[2,512,512]{2,1,0:T(8,128)(2,1)S(1)}, u32[]{:S(2)}, u32[]{:S(2)}) collective-permute-start(bf16[2,512,512]{2,1,0:T(8,128)(2,1)} %bitcast.12), channel_id=1, source_target_pairs={{0,1},{1,0},{2,3},{3,2},{4,5},{5,4},{6,7},{7,6},{8,9},{9,8},{10,11... | collective-permute-start | bytes 3145736 | tf_op jit(solution)/shard_map/ppermute | solution.py:281
  1.2 0.9 %copy-start.2 = (f32[1,2,64,512]{3,2,1,0:T(8,128)S(1)}, f32[1,2,64,512]{3,2,1,0:T(8,128)}, u32[]{:S(2)}) copy-start(f32[1,2,64,512]{3,2,1,0:T(8,128)} %param.9) | copy-start | bytes 786436
  2.2 9.7 %collective-permute-start.4 = (bf16[128,512]{1,0:T(8,128)(2,1)S(1)}, bf16[128,512]{1,0:T(8,128)(2,1)}, u32[]{:S(2)}, u32[]{:S(2)}) collective-permute-start(bf16[128,512]{1,0:T(8,128)(2,1)S(1)} %lower.1.refs_4_.refs_1_), channel_id=1, source_target_pairs={{0,2},{1,3},{2,0},{3,1},{4,6},{5,7},{6,4},{7,5},{8,10},{9,11},{10,... | collective-permute-start | bytes 393224 | tf_op jit(solution)/shard_map/ppermute | solution.py:281
  5.3 18.9 %collective-permute-start = (bf16[128,512]{1,0:T(8,128)(2,1)S(1)}, bf16[128,512]{1,0:T(8,128)(2,1)S(1)}, u32[]{:S(2)}, u32[]{:S(2)}) collective-permute-start(bf16[128,512]{1,0:T(8,128)(2,1)S(1)} %lower.1.refs_4_.refs_1_), channel_id=1, source_target_pairs={{0,4},{1,5},{2,6},{3,7},{4,0},{5,1},{6,2},{7,3},{8,12},{9,13},{10,... | collective-permute-start | bytes 393224 | tf_op jit(solution)/shard_map/ppermute | solution.py:281
  7.9 16.3 %collective-permute-start.1 = (bf16[128,512]{1,0:T(8,128)(2,1)S(1)}, bf16[128,512]{1,0:T(8,128)(2,1)S(1)}, u32[]{:S(2)}, u32[]{:S(2)}) collective-permute-start(bf16[128,512]{1,0:T(8,128)(2,1)S(1)} %lower.1.refs_4_.refs_1_), channel_id=1, source_target_pairs={{0,6},{1,7},{2,4},{3,5},{4,2},{5,3},{6,0},{7,1},{8,14},{9,15},{10,... | collective-permute-start | bytes 393224 | tf_op jit(solution)/shard_map/ppermute | solution.py:281
  7.9 1.2 %copy-start = (bf16[1,2,512,512]{3,2,1,0:T(8,128)(2,1)S(1)}, bf16[1,2,512,512]{3,2,1,0:T(8,128)(2,1)}, u32[]{:S(2)}) copy-start(bf16[1,2,512,512]{3,2,1,0:T(8,128)(2,1)} %param.14) | copy-start | bytes 3145732
  9.2 6.1 %copy-start.4 = (bf16[1,2,512,2,512]{4,3,2,1,0:T(2,128)(2,1)S(1)}, bf16[1,2,512,2,512]{4,3,2,1,0:T(2,128)(2,1)}, u32[]{:S(2)}) copy-start(bf16[1,2,512,2,512]{4,3,2,1,0:T(2,128)(2,1)} %refs_1_.2) | copy-start | bytes 6291460
  10.2 14.0 %collective-permute-start.5 = (bf16[64,512]{1,0:T(8,128)(2,1)S(1)}, bf16[64,512]{1,0:T(8,128)(2,1)S(1)}, u32[]{:S(2)}, u32[]{:S(2)}) collective-permute-start(bf16[64,512]{1,0:T(8,128)(2,1)S(1)} %get-tuple-element.41), channel_id=1, source_target_pairs={{0,2},{1,3},{2,0},{3,1},{4,6},{5,7},{6,4},{7,5},{8,10},{9,11},{10,... | collective-permute-start | bytes 196616 | tf_op jit(solution)/shard_map/ppermute | solution.py:281
  11.9 12.9 %collective-permute-start.6 = (bf16[64,512]{1,0:T(8,128)(2,1)S(1)}, bf16[64,512]{1,0:T(8,128)(2,1)S(1)}, u32[]{:S(2)}, u32[]{:S(2)}) collective-permute-start(bf16[64,512]{1,0:T(8,128)(2,1)S(1)} %get-tuple-element.42), channel_id=1, source_target_pairs={{0,4},{1,5},{2,6},{3,7},{4,0},{5,1},{6,2},{7,3},{8,12},{9,13},{10,... | collective-permute-start | bytes 196616 | tf_op jit(solution)/shard_map/ppermute | solution.py:281
  14.7 10.1 %collective-permute-start.7 = (bf16[64,512]{1,0:T(8,128)(2,1)S(1)}, bf16[64,512]{1,0:T(8,128)(2,1)S(1)}, u32[]{:S(2)}, u32[]{:S(2)}) collective-permute-start(bf16[64,512]{1,0:T(8,128)(2,1)S(1)} %get-tuple-element.43), channel_id=1, source_target_pairs={{0,6},{1,7},{2,4},{3,5},{4,2},{5,3},{6,0},{7,1},{8,14},{9,15},{10,... | collective-permute-start | bytes 196616 | tf_op jit(solution)/shard_map/ppermute | solution.py:281
  15.3 6.3 %copy-start.1 = (bf16[1,2,512,512]{3,2,1,0:T(8,128)(2,1)S(1)}, bf16[1,2,512,512]{3,2,1,0:T(8,128)(2,1)}, u32[]{:S(2)}) copy-start(bf16[1,2,512,512]{3,2,1,0:T(8,128)(2,1)} %param.14) | copy-start | bytes 3145732
  21.7 3.1 %copy-start.3 = (f32[1,2,64,512]{3,2,1,0:T(8,128)S(1)}, f32[1,2,64,512]{3,2,1,0:T(8,128)}, u32[]{:S(2)}) copy-start(f32[1,2,64,512]{3,2,1,0:T(8,128)} %param.9) | copy-start | bytes 786436
  26.9 32.9 %copy-start.5 = (f32[2,64,512]{2,1,0:T(8,128)S(1)}, f32[2,64,512]{2,1,0:T(8,128)}, u32[]{:S(2)}) copy-start(f32[2,64,512]{2,1,0:T(8,128)} %refs_7_.3) | copy-start | bytes 786436
  26.9 32.9 %copy-start.6 = (f32[1,2,64,512]{3,2,1,0:T(8,128)S(1)}, f32[1,2,64,512]{3,2,1,0:T(8,128)}, u32[]{:S(2)}) copy-start(f32[1,2,64,512]{3,2,1,0:T(8,128)} %param.10) | copy-start | bytes 786436
  27.0 32.9 %copy-start.7 = (f32[1,2,64,512]{3,2,1,0:T(8,128)S(1)}, f32[1,2,64,512]{3,2,1,0:T(8,128)}, u32[]{:S(2)}) copy-start(f32[1,2,64,512]{3,2,1,0:T(8,128)} %param.11) | copy-start | bytes 786436
  27.0 32.9 %copy-start.8 = (f32[2,64,512]{2,1,0:T(8,128)S(1)}, f32[2,64,512]{2,1,0:T(8,128)}, u32[]{:S(2)}) copy-start(f32[2,64,512]{2,1,0:T(8,128)} %refs_6_.1) | copy-start | bytes 786436
  27.0 6.3 %collective-permute-start.12 = (f32[64,512]{1,0:T(8,128)S(1)}, f32[64,512]{1,0:T(8,128)S(1)}, u32[]{:S(2)}, u32[]{:S(2)}) collective-permute-start(f32[64,512]{1,0:T(8,128)S(1)} %get-tuple-element.50.refs_0_), channel_id=1, source_target_pairs={{0,8},{8,0},{16,24},{24,16},{1,9},{9,1},{17,25},{25,17},{2,10},{10... | collective-permute-start | bytes 393224 | tf_op jit(solution)/shard_map/ppermute | solution.py:281
  28.5 19.5 %collective-permute-start.8 = (bf16[2,128,512]{2,1,0:T(8,128)(2,1)S(1)}, bf16[2,128,512]{2,1,0:T(8,128)(2,1)S(1)}, u32[]{:S(2)}, u32[]{:S(2)}) collective-permute-start(bf16[2,128,512]{2,1,0:T(8,128)(2,1)S(1)} %get-tuple-element.45), channel_id=1, source_target_pairs={{0,2},{1,3},{2,0},{3,1},{4,6},{5,7},{6,4},{7,5},{8,10},{9,11},{10,... | collective-permute-start | bytes 786440 | tf_op jit(solution)/shard_map/ppermute | solution.py:281
  29.8 15.6 %collective-permute-start.10 = (bf16[192,512]{1,0:T(8,128)(2,1)S(1)}, bf16[192,512]{1,0:T(8,128)(2,1)S(1)}, u32[]{:S(2)}, u32[]{:S(2)}) collective-permute-start(bf16[192,512]{1,0:T(8,128)(2,1)S(1)} %get-tuple-element.48), channel_id=1, source_target_pairs={{0,4},{1,5},{2,6},{3,7},{4,0},{5,1},{6,2},{7,3},{8,12},{9,13},{10,... | collective-permute-start | bytes 589832 | tf_op jit(solution)/shard_map/ppermute | solution.py:281
  32.4 15.4 %collective-permute-start.11 = (bf16[192,512]{1,0:T(8,128)(2,1)S(1)}, bf16[192,512]{1,0:T(8,128)(2,1)S(1)}, u32[]{:S(2)}, u32[]{:S(2)}) collective-permute-start(bf16[192,512]{1,0:T(8,128)(2,1)S(1)} %get-tuple-element.49), channel_id=1, source_target_pairs={{0,6},{1,7},{2,4},{3,5},{4,2},{5,3},{6,0},{7,1},{8,14},{9,15},{10,... | collective-permute-start | bytes 589832 | tf_op jit(solution)/shard_map/ppermute | solution.py:281
  32.9 15.1 %collective-permute-start.9 = (bf16[192,512]{1,0:T(8,128)(2,1)S(1)}, bf16[192,512]{1,0:T(8,128)(2,1)S(1)}, u32[]{:S(2)}, u32[]{:S(2)}) collective-permute-start(bf16[192,512]{1,0:T(8,128)(2,1)S(1)} %get-tuple-element.47), channel_id=1, source_target_pairs={{0,2},{1,3},{2,0},{3,1},{4,6},{5,7},{6,4},{7,5},{8,10},{9,11},{10,... | collective-permute-start | bytes 589832 | tf_op jit(solution)/shard_map/ppermute | solution.py:281
  33.3 5.0 %collective-permute-start.13 = (f32[64,512]{1,0:T(8,128)S(1)}, f32[64,512]{1,0:T(8,128)S(1)}, u32[]{:S(2)}, u32[]{:S(2)}) collective-permute-start(f32[64,512]{1,0:T(8,128)S(1)} %add_reps.2.refs_0_), channel_id=1, source_target_pairs={{0,16},{8,24},{16,0},{24,8},{1,17},{9,25},{17,1},{25,9},{2,18},{10... | collective-permute-start | bytes 393224 | tf_op jit(solution)/shard_map/ppermute | solution.py:281
  48.6 1.6 %collective-permute-start.15 = (bf16[256,512]{1,0:T(8,128)(2,1)S(1)}, bf16[256,512]{1,0:T(8,128)(2,1)S(1)}, u32[]{:S(2)}, u32[]{:S(2)}) collective-permute-start(bf16[256,512]{1,0:T(8,128)(2,1)S(1)} %get-tuple-element.52.refs_4_), channel_id=1, source_target_pairs={{0,1},{1,0},{2,3},{3,2},{4,5},{5,4},{6,7},{7,6},{8,9},{9,8},{10,11... | collective-permute-start | bytes 786440 | tf_op jit(solution)/shard_map/ppermute | solution.py:281
  48.7 1.5 %collective-permute-start.14 = (f32[8,128]{1,0:T(8,128)S(1)}, f32[8,128]{1,0:T(8,128)S(1)}, u32[]{:S(2)}, u32[]{:S(2)}) collective-permute-start(f32[8,128]{1,0:T(8,128)S(1)} %get-tuple-element.51.refs_0_), channel_id=1, source_target_pairs={{0,1},{1,0},{2,3},{3,2},{4,5},{5,4},{6,7},{7,6},{8,9},{9,8},{10,11... | collective-permute-start | bytes 12296 | tf_op jit(solution)/shard_map/ppermute | solution.py:281
  50.3 6.1 %collective-permute-start.17 = (f32[8,128]{1,0:T(8,128)S(1)}, f32[8,128]{1,0:T(8,128)S(1)}, u32[]{:S(2)}, u32[]{:S(2)}) collective-permute-start(f32[8,128]{1,0:T(8,128)S(1)} %add_cores.2.refs_2_.refs_9_), channel_id=1, source_target_pairs={{0,2},{1,3},{2,0},{3,1},{4,6},{5,7},{6,4},{7,5},{8,10},{9,11},{10,... | collective-permute-start | bytes 12296 | tf_op jit(solution)/shard_map/ppermute | solution.py:281
  51.6 4.8 %collective-permute-start.18 = (f32[8,128]{1,0:T(8,128)S(1)}, f32[8,128]{1,0:T(8,128)S(1)}, u32[]{:S(2)}, u32[]{:S(2)}) collective-permute-start(f32[8,128]{1,0:T(8,128)S(1)} %add_cores.2.refs_2_.refs_9_), channel_id=1, source_target_pairs={{0,4},{1,5},{2,6},{3,7},{4,0},{5,1},{6,2},{7,3},{8,12},{9,13},{10,... | collective-permute-start | bytes 12296 | tf_op jit(solution)/shard_map/ppermute | solution.py:281
  54.4 5.5 %collective-permute-start.19 = (f32[8,128]{1,0:T(8,128)S(1)}, f32[8,128]{1,0:T(8,128)S(1)}, u32[]{:S(2)}, u32[]{:S(2)}) collective-permute-start(f32[8,128]{1,0:T(8,128)S(1)} %add_cores.2.refs_2_.refs_9_), channel_id=1, source_target_pairs={{0,6},{1,7},{2,4},{3,5},{4,2},{5,3},{6,0},{7,1},{8,14},{9,15},{10,... | collective-permute-start | bytes 12296 | tf_op jit(solution)/shard_map/ppermute | solution.py:281
  54.7 8.6 %collective-permute-start.16 = (bf16[1,128,512]{2,1,0:T(8,128)(2,1)S(1)}, bf16[1,128,512]{2,1,0:T(8,128)(2,1)S(1)}, u32[]{:S(2)}, u32[]{:S(2)}) collective-permute-start(bf16[1,128,512]{2,1,0:T(8,128)(2,1)S(1)} %get-tuple-element.54), channel_id=1, source_target_pairs={{0,4},{1,5},{2,6},{3,7},{4,0},{5,1},{6,2},{7,3},{8,12},{9,13},{10,... | collective-permute-start | bytes 393224 | tf_op jit(solution)/shard_map/ppermute | solution.py:281
  61.0 5.0 %collective-permute-start.20 = (f32[64,512]{1,0:T(8,128)S(1)}, f32[64,512]{1,0:T(8,128)S(1)}, u32[]{:S(2)}, u32[]{:S(2)}) collective-permute-start(f32[64,512]{1,0:T(8,128)S(1)} %get-tuple-element.62.refs_0_), channel_id=1, source_target_pairs={{0,8},{8,0},{16,24},{24,16},{1,9},{9,1},{17,25},{25,17},{2,10},{10... | collective-permute-start | bytes 393224 | tf_op jit(solution)/shard_map/ppermute | solution.py:281
  63.7 1.2 %collective-permute-start.21 = (f32[8,128]{1,0:T(8,128)S(1)}, f32[8,128]{1,0:T(8,128)S(1)}, u32[]{:S(2)}, u32[]{:S(2)}) collective-permute-start(f32[8,128]{1,0:T(8,128)S(1)} %get-tuple-element.63.refs_0_), channel_id=1, source_target_pairs={{0,1},{1,0},{2,3},{3,2},{4,5},{5,4},{6,7},{7,6},{8,9},{9,8},{10,11... | collective-permute-start | bytes 12296 | tf_op jit(solution)/shard_map/ppermute | solution.py:281
  66.0 5.9 %collective-permute-start.22 = (f32[64,512]{1,0:T(8,128)S(1)}, f32[64,512]{1,0:T(8,128)S(1)}, u32[]{:S(2)}, u32[]{:S(2)}) collective-permute-start(f32[64,512]{1,0:T(8,128)S(1)} %add_moves.2.refs_0_), channel_id=1, source_target_pairs={{0,16},{8,24},{16,0},{24,8},{1,17},{9,25},{17,1},{25,9},{2,18},{10... | collective-permute-start | bytes 393224 | tf_op jit(solution)/shard_map/ppermute | solution.py:281
  67.6 4.4 %collective-permute-start.23 = (f32[8,128]{1,0:T(8,128)S(1)}, f32[8,128]{1,0:T(8,128)S(1)}, u32[]{:S(2)}, u32[]{:S(2)}) collective-permute-start(f32[8,128]{1,0:T(8,128)S(1)} %add_cores.3.refs_2_.refs_9_), channel_id=1, source_target_pairs={{0,2},{1,3},{2,0},{3,1},{4,6},{5,7},{6,4},{7,5},{8,10},{9,11},{10,... | collective-permute-start | bytes 12296 | tf_op jit(solution)/shard_map/ppermute | solution.py:281
  67.6 4.5 %collective-permute-start.24 = (f32[8,128]{1,0:T(8,128)S(1)}, f32[8,128]{1,0:T(8,128)S(1)}, u32[]{:S(2)}, u32[]{:S(2)}) collective-permute-start(f32[8,128]{1,0:T(8,128)S(1)} %add_cores.3.refs_2_.refs_9_), channel_id=1, source_target_pairs={{0,4},{1,5},{2,6},{3,7},{4,0},{5,1},{6,2},{7,3},{8,12},{9,13},{10,... | collective-permute-start | bytes 12296 | tf_op jit(solution)/shard_map/ppermute | solution.py:281
  69.4 5.4 %collective-permute-start.25 = (f32[8,128]{1,0:T(8,128)S(1)}, f32[8,128]{1,0:T(8,128)S(1)}, u32[]{:S(2)}, u32[]{:S(2)}) collective-permute-start(f32[8,128]{1,0:T(8,128)S(1)} %add_cores.3.refs_2_.refs_9_), channel_id=1, source_target_pairs={{0,6},{1,7},{2,4},{3,5},{4,2},{5,3},{6,0},{7,1},{8,14},{9,15},{10,... | collective-permute-start | bytes 12296 | tf_op jit(solution)/shard_map/ppermute | solution.py:281

commit v5 on v4

--- a/solution.py
+++ b/solution.py
@@ -359,10 +359,10 @@
         [place],
         pieces_one,
         "sum_pieces",
-        [sums, got],
+        [sums],
     )
     sib_g = sibling(own_g)
-    norms = norm_parts(squares, [sib_g])
+    norms = norm_parts(squares, [sib_g, got])
     bit = 2
     while bit < chips:
         half = shape((keep.shape[0] // 2, 2 * rows, width), BF16)

time: 76.8 us -> 76 us (0.990)
  waiting for transfers between devices: 24.2 us -> 23.2 us
    ppermute x26, waiting for transfers between devices: 24.2 us -> 23.2 us  [swap(): return lax.ppermute(x, axis, [(i, i ^ by) for i in range(size)])]
  transfers between devices with their start and end apart: 26 -> 26, of which waited for: 12 -> 11; matrix products, arithmetic and copies ran while one was open for 0% -> 0% of each run, Pallas kernels for 15% -> 16%
where the time goes in v5:
time: 76 us; the launch traced here: 75.8 us
  starting transfers between devices  31.9 us (42%)
  waiting for transfers between devices  23.2 us (31%)
  Pallas kernels  15.9 us (21%)
  between operations  2.33 us (3%)
  local copies, waits for them, and re-layouts  2.22 us (3%)
    ppermute x26, starting transfers between devices, swap(): return lax.ppermute(x, axis, [(i, i ^ by) for i in range(size)])  31.9 us
    ppermute x26, waiting for transfers between devices, swap(): return lax.ppermute(x, axis, [(i, i ^ by) for i in range(size)])  23.2 us
    pallas_call x16, Pallas kernels, call(): pl.pallas_call(run, in_specs=[pl.BlockSpec(memory_space=pltpu.SMEM)] * le...  15.9 us
    unnamed x18, local copies, waits for them, and re-layouts  2.22 us
  transfers between devices with their start and end apart: 26, of which 11 were waited for; matrix products, arithmetic and copies ran while one was open for 0% of the time, Pallas kernels for 16%

profile of v5, /device:TPU:0, one launch (start us, length us, event | category | flops | bytes accessed | tf_op | source)
XLA Modules:
  0.0 75.8 jit_solution(14101976689656683763)
XLA Ops:
  0.6 0.5 collective-permute-start.3
  1.1 0.1 collective-permute-start.2
  1.2 0.9 %copy-done.2 = f32[1,2,64,512]{3,2,1,0:T(8,128)S(1)} copy-done((f32[1,2,64,512]{3,2,1,0:T(8,128)S(1)}, f32[1,2,64,512]{3,2,1,0:T(8,128)}, u32[]{:S(2)}) %copy-start.2) | copy-done | bytes 262168
  2.2 3.1 %collective-permute-start.4 = (bf16[128,512]{1,0:T(8,128)(2,1)S(1)}, bf16[128,512]{1,0:T(8,128)(2,1)}, u32[]{:S(2)}, u32[]{:S(2)}) collective-permute-start(bf16[128,512]{1,0:T(8,128)(2,1)S(1)} %lower.1.refs_4_.refs_1_), channel_id=1, source_target_pairs={{0,2},{1,3},{2,0},{3,1},{4,6},{5,7},{6,4},{7,5},{8,10},{9,11},{10,... | collective-permute-start | bytes 393224 | tf_op jit(solution)/shard_map/ppermute | solution.py:281
  5.3 2.6 %collective-permute-start = (bf16[128,512]{1,0:T(8,128)(2,1)S(1)}, bf16[128,512]{1,0:T(8,128)(2,1)S(1)}, u32[]{:S(2)}, u32[]{:S(2)}) collective-permute-start(bf16[128,512]{1,0:T(8,128)(2,1)S(1)} %lower.1.refs_4_.refs_1_), channel_id=1, source_target_pairs={{0,4},{1,5},{2,6},{3,7},{4,0},{5,1},{6,2},{7,3},{8,12},{9,13},{10,... | collective-permute-start | bytes 393224 | tf_op jit(solution)/shard_map/ppermute | solution.py:281
  7.9 0.1 pad_add_fusion.refs_1_.refs_0_
  7.9 1.2 %copy-done = bf16[1,2,512,512]{3,2,1,0:T(8,128)(2,1)S(1)} copy-done((bf16[1,2,512,512]{3,2,1,0:T(8,128)(2,1)S(1)}, bf16[1,2,512,512]{3,2,1,0:T(8,128)(2,1)}, u32[]{:S(2)}) %copy-start) | copy-done | bytes 1048600
  9.2 1.0 %gram.1 = (bf16[64,512]{1,0:T(8,128)(2,1)S(1)}, bf16[64,512]{1,0:T(8,128)(2,1)S(1)}, bf16[64,512]{1,0:T(8,128)(2,1)S(1)}, bf16[64,512]{1,0:T(8,128)(2,1)S(1)}) custom-call(s32[1]{0:T(128)} %bitcast.refs_0_, s32[4]{0:T(128)S(1)} %pad_add_fusion.refs_1_.refs_0_, bf16[2,512,512]{2,1,0:T(8,128)(2,1)S(1)} %bitcast.13, ...), custom_call_target="tpu_custom_call" | custom-call | bytes 1024 | tf_op jit(solution)/shard_map/gram/pallas_call | solution.py:48
  10.2 1.7 %collective-permute-start.5 = (bf16[64,512]{1,0:T(8,128)(2,1)S(1)}, bf16[64,512]{1,0:T(8,128)(2,1)S(1)}, u32[]{:S(2)}, u32[]{:S(2)}) collective-permute-start(bf16[64,512]{1,0:T(8,128)(2,1)S(1)} %get-tuple-element.41), channel_id=1, source_target_pairs={{0,2},{1,3},{2,0},{3,1},{4,6},{5,7},{6,4},{7,5},{8,10},{9,11},{10,... | collective-permute-start | bytes 196616 | tf_op jit(solution)/shard_map/ppermute | solution.py:281
  11.9 2.7 %collective-permute-start.6 = (bf16[64,512]{1,0:T(8,128)(2,1)S(1)}, bf16[64,512]{1,0:T(8,128)(2,1)S(1)}, u32[]{:S(2)}, u32[]{:S(2)}) collective-permute-start(bf16[64,512]{1,0:T(8,128)(2,1)S(1)} %get-tuple-element.42), channel_id=1, source_target_pairs={{0,4},{1,5},{2,6},{3,7},{4,0},{5,1},{6,2},{7,3},{8,12},{9,13},{10,... | collective-permute-start | bytes 196616 | tf_op jit(solution)/shard_map/ppermute | solution.py:281
  15.3 0.0 copy-start.1
  15.3 6.3 %split.1 = (bf16[2,4,512,128]{3,2,1,0:T(8,128)(2,1)S(1)}, bf16[2,4,512,128]{3,2,1,0:T(8,128)(2,1)S(1)}) custom-call(s32[1]{0:T(128)} %bitcast.refs_0_, bf16[1,2,512,2,512]{4,3,2,1,0:T(2,128)(2,1)S(1)} %copy-done.4, bf16[1,2,512,2,512]{4,3,2,1,0:T(2,128)(2,1)S(1)} %collective-permute-done.3.refs_2_, bf16[64,512]{1,0:T(8,128)(2,1)S(1)} %get-tuple-element.34.refs_3_.refs_12_), custom_call_target="tpu_custom_call" | custom-call | bytes 1024 | tf_op jit(solution)/shard_map/split/pallas_call | solution.py:48
  21.7 2.5 %near_grad.1 = (bf16[128,512]{1,0:T(8,128)(2,1)S(1)}, bf16[128,512]{1,0:T(8,128)(2,1)S(1)}, bf16[128,512]{1,0:T(8,128)(2,1)S(1)}, bf16[128,512]{1,0:T(8,128)(2,1)S(1)}) custom-call(s32[4]{0:T(128)S(1)} %pad_add_fusion.refs_1_.refs_0_, bf16[128,512]{1,0:T(8,128)(2,1)S(1)} %lower.1.refs_4_.refs_1_, bf16[128,512]{1,0:T(8,128)(2,1)} %collective-permute-done.4.refs_2_, ...), custom_call_target="tpu_custom_call" | custom-call | bytes 1024 | tf_op jit(solution)/shard_map/near_grad/pallas_call | solution.py:48
  24.2 0.6 collective-permute-done.6.refs_14_
  24.8 2.1 %far_grad.1 = (bf16[192,512]{1,0:T(8,128)(2,1)S(1)}, bf16[192,512]{1,0:T(8,128)(2,1)S(1)}, bf16[192,512]{1,0:T(8,128)(2,1)S(1)}, bf16[192,512]{1,0:T(8,128)(2,1)...) custom-call(s32[4]{0:T(128)S(1)} %pad_add_fusion.refs_1_.refs_0_, ...), custom_call_target="tpu_custom_call" | custom-call | bytes 1024 | tf_op jit(solution)/shard_map/far_grad/pallas_call | solution.py:48
  27.0 1.6 %collective-permute-start.12 = (f32[64,512]{1,0:T(8,128)S(1)}, f32[64,512]{1,0:T(8,128)S(1)}, u32[]{:S(2)}, u32[]{:S(2)}) collective-permute-start(f32[64,512]{1,0:T(8,128)S(1)} %get-tuple-element.50.refs_0_), channel_id=1, source_target_pairs={{0,8},{8,0},{16,24},{24,16},{1,9},{9,1},{17,25},{25,17},{2,10},{10... | collective-permute-start | bytes 393224 | tf_op jit(solution)/shard_map/ppermute | solution.py:281
  28.5 2.2 %collective-permute-start.10 = (bf16[192,512]{1,0:T(8,128)(2,1)S(1)}, bf16[192,512]{1,0:T(8,128)(2,1)S(1)}, u32[]{:S(2)}, u32[]{:S(2)}) collective-permute-start(bf16[192,512]{1,0:T(8,128)(2,1)S(1)} %get-tuple-element.48), channel_id=1, source_target_pairs={{0,4},{1,5},{2,6},{3,7},{4,0},{5,1},{6,2},{7,3},{8,12},{9,13},{10,... | collective-permute-start | bytes 589832 | tf_op jit(solution)/shard_map/ppermute | solution.py:281
  30.8 1.4 %collective-permute-start.11 = (bf16[192,512]{1,0:T(8,128)(2,1)S(1)}, bf16[192,512]{1,0:T(8,128)(2,1)S(1)}, u32[]{:S(2)}, u32[]{:S(2)}) collective-permute-start(bf16[192,512]{1,0:T(8,128)(2,1)S(1)} %get-tuple-element.49), channel_id=1, source_target_pairs={{0,6},{1,7},{2,4},{3,5},{4,2},{5,3},{6,0},{7,1},{8,14},{9,15},{10,... | collective-permute-start | bytes 589832 | tf_op jit(solution)/shard_map/ppermute | solution.py:281
  32.2 0.2 collective-permute-start.9
  32.4 1.6 %collective-permute-start.13 = (f32[64,512]{1,0:T(8,128)S(1)}, f32[64,512]{1,0:T(8,128)S(1)}, u32[]{:S(2)}, u32[]{:S(2)}) collective-permute-start(f32[64,512]{1,0:T(8,128)S(1)} %add_reps.2.refs_0_), channel_id=1, source_target_pairs={{0,16},{8,24},{16,0},{24,8},{1,17},{9,25},{17,1},{25,9},{2,18},{10... | collective-permute-start | bytes 393224 | tf_op jit(solution)/shard_map/ppermute | solution.py:281
  34.0 1.8 %collective-permute-start.8 = (bf16[2,128,512]{2,1,0:T(8,128)(2,1)S(1)}, bf16[2,128,512]{2,1,0:T(8,128)(2,1)S(1)}, u32[]{:S(2)}, u32[]{:S(2)}) collective-permute-start(bf16[2,128,512]{2,1,0:T(8,128)(2,1)S(1)} %get-tuple-element.45), channel_id=1, source_target_pairs={{0,2},{1,3},{2,0},{3,1},{4,6},{5,7},{6,4},{7,5},{8,10},{9,11},{10,... | collective-permute-start | bytes 786440 | tf_op jit(solution)/shard_map/ppermute | solution.py:281
  35.8 1.6 %collective-permute-done.13.refs_1_ = f32[64,512]{1,0:T(8,128)S(1)} collective-permute-done((f32[64,512]{1,0:T(8,128)S(1)}, f32[64,512]{1,0:T(8,128)S(1)}, u32[]{:S(2)}, u32[]{:S(2)}) %collective-permute-start.13) | collective-permute-done | bytes 131104 | tf_op jit(solution)/shard_map/ppermute | solution.py:281
  37.4 6.9 %collective-permute-done.10.refs_3_ = bf16[192,512]{1,0:T(8,128)(2,1)S(1)} collective-permute-done((bf16[192,512]{1,0:T(8,128)(2,1)S(1)}, bf16[192,512]{1,0:T(8,128)(2,1)S(1)}, u32[]{:S(2)}, u32[]{:S(2)}) %collective-permute-start.10) | collective-permute-done | bytes 196640 | tf_op jit(solution)/shard_map/ppermute | solution.py:281
  44.4 2.0 %collective-permute-done.9.refs_2_ = bf16[192,512]{1,0:T(8,128)(2,1)S(1)} collective-permute-done((bf16[192,512]{1,0:T(8,128)(2,1)S(1)}, bf16[192,512]{1,0:T(8,128)(2,1)S(1)}, u32[]{:S(2)}, u32[]{:S(2)}) %collective-permute-start.9) | collective-permute-done | bytes 196640 | tf_op jit(solution)/shard_map/ppermute | solution.py:281
  46.4 0.6 sum_pieces.1
  47.0 0.1 collective-permute-start.15
  47.1 0.5 collective-permute-start.14
  48.4 1.8 %collective-permute-done.8.refs_3_.refs_1_ = bf16[2,128,512]{2,1,0:T(8,128)(2,1)S(1)} collective-permute-done((bf16[2,128,512]{2,1,0:T(8,128)(2,1)S(1)}, bf16[2,128,512]{2,1,0:T(8,128)(2,1)S(1)}, u32[]{:S(2)}, u32[]{:S(2)}) %collective-permute-start.8) | collective-permute-done | bytes 262176 | tf_op jit(solution)/shard_map/ppermute | solution.py:281
  50.3 0.1 collective-permute-start.17
  50.4 3.5 %collective-permute-start.18 = (f32[8,128]{1,0:T(8,128)S(1)}, f32[8,128]{1,0:T(8,128)S(1)}, u32[]{:S(2)}, u32[]{:S(2)}) collective-permute-start(f32[8,128]{1,0:T(8,128)S(1)} %add_cores.2.refs_2_.refs_9_), channel_id=1, source_target_pairs={{0,4},{1,5},{2,6},{3,7},{4,0},{5,1},{6,2},{7,3},{8,12},{9,13},{10,... | collective-permute-start | bytes 12296 | tf_op jit(solution)/shard_map/ppermute | solution.py:281
  53.9 0.8 %collective-permute-start.19 = (f32[8,128]{1,0:T(8,128)S(1)}, f32[8,128]{1,0:T(8,128)S(1)}, u32[]{:S(2)}, u32[]{:S(2)}) collective-permute-start(f32[8,128]{1,0:T(8,128)S(1)} %add_cores.2.refs_2_.refs_9_), channel_id=1, source_target_pairs={{0,6},{1,7},{2,4},{3,5},{4,2},{5,3},{6,0},{7,1},{8,14},{9,15},{10,... | collective-permute-start | bytes 12296 | tf_op jit(solution)/shard_map/ppermute | solution.py:281
  54.7 0.1 halve.1
  54.8 0.8 %collective-permute-start.16 = (bf16[1,128,512]{2,1,0:T(8,128)(2,1)S(1)}, bf16[1,128,512]{2,1,0:T(8,128)(2,1)S(1)}, u32[]{:S(2)}, u32[]{:S(2)}) collective-permute-start(bf16[1,128,512]{2,1,0:T(8,128)(2,1)S(1)} %get-tuple-element.54), channel_id=1, source_target_pairs={{0,4},{1,5},{2,6},{3,7},{4,0},{5,1},{6,2},{7,3},{8,12},{9,13},{10,... | collective-permute-start | bytes 393224 | tf_op jit(solution)/shard_map/ppermute | solution.py:281
  55.6 0.1 pad_maximum_fusion.refs_1_
  55.6 3.7 %collective-permute-done.19.refs_12_ = f32[8,128]{1,0:T(8,128)S(1)} collective-permute-done((f32[8,128]{1,0:T(8,128)S(1)}, f32[8,128]{1,0:T(8,128)S(1)}, u32[]{:S(2)}, u32[]{:S(2)}) %collective-permute-start.19) | collective-permute-done | bytes 4128 | tf_op jit(solution)/shard_map/ppermute | solution.py:281
  59.4 1.1 %first_update.1 = (f32[2,64,512]{2,1,0:T(8,128)S(1)}, f32[2,64,512]{2,1,0:T(8,128)S(1)}, f32[2,64,512]{2,1,0:T(8,128)S(1)}, f32[128,512]{1,0:T(8,128)S(1)}, f32[...) custom-call(s32[1]{0:T(128)S(6)} %copy.12.refs_1_.refs_0_, f32[4]{0:T(128)S(1)} %pad_maximum_fusion.refs_1_, ...), custom_call_target="tpu_custom_call" | custom-call | bytes 1024 | tf_op jit(solution)/shard_map/first_update/pallas_call | solution.py:48
  60.5 0.6 collective-permute-start.20
  61.1 1.1 %collective-permute-done.16 = bf16[1,128,512]{2,1,0:T(8,128)(2,1)S(1)} collective-permute-done((bf16[1,128,512]{2,1,0:T(8,128)(2,1)S(1)}, bf16[1,128,512]{2,1,0:T(8,128)(2,1)S(1)}, u32[]{:S(2)}, u32[]{:S(2)}) %collective-permute-start.16) | collective-permute-done | bytes 131104 | tf_op jit(solution)/shard_map/ppermute | solution.py:281
  62.2 0.3 corrected.1
  62.5 0.1 collective-permute-start.21
  62.6 1.2 %collective-permute-done.21.refs_1_ = f32[8,128]{1,0:T(8,128)S(1)} collective-permute-done((f32[8,128]{1,0:T(8,128)S(1)}, f32[8,128]{1,0:T(8,128)S(1)}, u32[]{:S(2)}, u32[]{:S(2)}) %collective-permute-start.21) | collective-permute-done | bytes 4128 | tf_op jit(solution)/shard_map/ppermute | solution.py:281
  63.8 1.8 %collective-permute-done.20.refs_1_ = f32[64,512]{1,0:T(8,128)S(1)} collective-permute-done((f32[64,512]{1,0:T(8,128)S(1)}, f32[64,512]{1,0:T(8,128)S(1)}, u32[]{:S(2)}, u32[]{:S(2)}) %collective-permute-start.20) | collective-permute-done | bytes 131104 | tf_op jit(solution)/shard_map/ppermute | solution.py:281
  65.5 1.6 %collective-permute-start.22 = (f32[64,512]{1,0:T(8,128)S(1)}, f32[64,512]{1,0:T(8,128)S(1)}, u32[]{:S(2)}, u32[]{:S(2)}) collective-permute-start(f32[64,512]{1,0:T(8,128)S(1)} %add_moves.2.refs_0_), channel_id=1, source_target_pairs={{0,16},{8,24},{16,0},{24,8},{1,17},{9,25},{17,1},{25,9},{2,18},{10... | collective-permute-start | bytes 393224 | tf_op jit(solution)/shard_map/ppermute | solution.py:281
  67.1 1.4 %collective-permute-start.24 = (f32[8,128]{1,0:T(8,128)S(1)}, f32[8,128]{1,0:T(8,128)S(1)}, u32[]{:S(2)}, u32[]{:S(2)}) collective-permute-start(f32[8,128]{1,0:T(8,128)S(1)} %add_cores.3.refs_2_.refs_9_), channel_id=1, source_target_pairs={{0,4},{1,5},{2,6},{3,7},{4,0},{5,1},{6,2},{7,3},{8,12},{9,13},{10,... | collective-permute-start | bytes 12296 | tf_op jit(solution)/shard_map/ppermute | solution.py:281
  68.6 2.9 %collective-permute-start.25 = (f32[8,128]{1,0:T(8,128)S(1)}, f32[8,128]{1,0:T(8,128)S(1)}, u32[]{:S(2)}, u32[]{:S(2)}) collective-permute-start(f32[8,128]{1,0:T(8,128)S(1)} %add_cores.3.refs_2_.refs_9_), channel_id=1, source_target_pairs={{0,6},{1,7},{2,4},{3,5},{4,2},{5,3},{6,0},{7,1},{8,14},{9,15},{10,... | collective-permute-start | bytes 12296 | tf_op jit(solution)/shard_map/ppermute | solution.py:281
  71.6 0.1 collective-permute-done.24.refs_11_
  71.6 2.3 %collective-permute-done.25.refs_12_ = f32[8,128]{1,0:T(8,128)S(1)} collective-permute-done((f32[8,128]{1,0:T(8,128)S(1)}, f32[8,128]{1,0:T(8,128)S(1)}, u32[]{:S(2)}, u32[]{:S(2)}) %collective-permute-start.25) | collective-permute-done | bytes 4128 | tf_op jit(solution)/shard_map/ppermute | solution.py:281
  74.0 1.8 %last_update.1 = (f32[2,64,512]{2,1,0:T(8,128)}, f32[2,64,512]{2,1,0:T(8,128)}) custom-call(s32[1]{0:T(128)S(6)} %copy.12.refs_1_.refs_0_, f32[4]{0:T(128)S(1)} %pad_maximum_fusion.refs_1_, f32[128,512]{1,0:T(8,128)S(1)} %get-tuple-element.57.refs_2_, f32[2,64,512]{2,1,0:T(8,128)S(1)} %get-tuple-element.58.refs_3_, ...), custom_call_target="tpu_custom_call" | custom-call | bytes 1024 | tf_op jit(solution)/shard_map/last_update/pallas_call | solution.py:48
  (40 shorter events, 0.2 us)
Async XLA Ops:
  0.6 14.0 %collective-permute-start.3 = (bf16[1,2,512,2,512]{4,3,2,1,0:T(2,128)(2,1)}, bf16[1,2,512,2,512]{4,3,2,1,0:T(2,128)(2,1)S(1)}, u32[]{:S(2)}, u32[]{:S(2)}) collective-permute-start(bf16[1,2,512,2,512]{4,3,2,1,0:T(2,128)(2,1)} %refs_1_.2), channel_id=1, source_target_pairs={{0,1},{1,0},{2,3},{3,2},{4,5},{5,4},{6,7},{7,6},{8,9},{9,8},{10,11... | collective-permute-start | bytes 6291464 | tf_op jit(solution)/shard_map/ppermute | solution.py:281
  1.1 6.8 %collective-permute-start.2 = (bf16[2,512,512]{2,1,0:T(8,128)(2,1)}, bf16[2,512,512]{2,1,0:T(8,128)(2,1)S(1)}, u32[]{:S(2)}, u32[]{:S(2)}) collective-permute-start(bf16[2,512,512]{2,1,0:T(8,128)(2,1)} %bitcast.12), channel_id=1, source_target_pairs={{0,1},{1,0},{2,3},{3,2},{4,5},{5,4},{6,7},{7,6},{8,9},{9,8},{10,11... | collective-permute-start | bytes 3145736 | tf_op jit(solution)/shard_map/ppermute | solution.py:281
  1.2 0.9 %copy-start.2 = (f32[1,2,64,512]{3,2,1,0:T(8,128)S(1)}, f32[1,2,64,512]{3,2,1,0:T(8,128)}, u32[]{:S(2)}) copy-start(f32[1,2,64,512]{3,2,1,0:T(8,128)} %param.9) | copy-start | bytes 786436
  2.2 9.7 %collective-permute-start.4 = (bf16[128,512]{1,0:T(8,128)(2,1)S(1)}, bf16[128,512]{1,0:T(8,128)(2,1)}, u32[]{:S(2)}, u32[]{:S(2)}) collective-permute-start(bf16[128,512]{1,0:T(8,128)(2,1)S(1)} %lower.1.refs_4_.refs_1_), channel_id=1, source_target_pairs={{0,2},{1,3},{2,0},{3,1},{4,6},{5,7},{6,4},{7,5},{8,10},{9,11},{10,... | collective-permute-start | bytes 393224 | tf_op jit(solution)/shard_map/ppermute | solution.py:281
  5.3 18.9 %collective-permute-start = (bf16[128,512]{1,0:T(8,128)(2,1)S(1)}, bf16[128,512]{1,0:T(8,128)(2,1)S(1)}, u32[]{:S(2)}, u32[]{:S(2)}) collective-permute-start(bf16[128,512]{1,0:T(8,128)(2,1)S(1)} %lower.1.refs_4_.refs_1_), channel_id=1, source_target_pairs={{0,4},{1,5},{2,6},{3,7},{4,0},{5,1},{6,2},{7,3},{8,12},{9,13},{10,... | collective-permute-start | bytes 393224 | tf_op jit(solution)/shard_map/ppermute | solution.py:281
  7.9 16.3 %collective-permute-start.1 = (bf16[128,512]{1,0:T(8,128)(2,1)S(1)}, bf16[128,512]{1,0:T(8,128)(2,1)S(1)}, u32[]{:S(2)}, u32[]{:S(2)}) collective-permute-start(bf16[128,512]{1,0:T(8,128)(2,1)S(1)} %lower.1.refs_4_.refs_1_), channel_id=1, source_target_pairs={{0,6},{1,7},{2,4},{3,5},{4,2},{5,3},{6,0},{7,1},{8,14},{9,15},{10,... | collective-permute-start | bytes 393224 | tf_op jit(solution)/shard_map/ppermute | solution.py:281
  7.9 1.2 %copy-start = (bf16[1,2,512,512]{3,2,1,0:T(8,128)(2,1)S(1)}, bf16[1,2,512,512]{3,2,1,0:T(8,128)(2,1)}, u32[]{:S(2)}) copy-start(bf16[1,2,512,512]{3,2,1,0:T(8,128)(2,1)} %param.14) | copy-start | bytes 3145732
  9.2 6.1 %copy-start.4 = (bf16[1,2,512,2,512]{4,3,2,1,0:T(2,128)(2,1)S(1)}, bf16[1,2,512,2,512]{4,3,2,1,0:T(2,128)(2,1)}, u32[]{:S(2)}) copy-start(bf16[1,2,512,2,512]{4,3,2,1,0:T(2,128)(2,1)} %refs_1_.2) | copy-start | bytes 6291460
  10.2 14.0 %collective-permute-start.5 = (bf16[64,512]{1,0:T(8,128)(2,1)S(1)}, bf16[64,512]{1,0:T(8,128)(2,1)S(1)}, u32[]{:S(2)}, u32[]{:S(2)}) collective-permute-start(bf16[64,512]{1,0:T(8,128)(2,1)S(1)} %get-tuple-element.41), channel_id=1, source_target_pairs={{0,2},{1,3},{2,0},{3,1},{4,6},{5,7},{6,4},{7,5},{8,10},{9,11},{10,... | collective-permute-start | bytes 196616 | tf_op jit(solution)/shard_map/ppermute | solution.py:281
  11.9 12.9 %collective-permute-start.6 = (bf16[64,512]{1,0:T(8,128)(2,1)S(1)}, bf16[64,512]{1,0:T(8,128)(2,1)S(1)}, u32[]{:S(2)}, u32[]{:S(2)}) collective-permute-start(bf16[64,512]{1,0:T(8,128)(2,1)S(1)} %get-tuple-element.42), channel_id=1, source_target_pairs={{0,4},{1,5},{2,6},{3,7},{4,0},{5,1},{6,2},{7,3},{8,12},{9,13},{10,... | collective-permute-start | bytes 196616 | tf_op jit(solution)/shard_map/ppermute | solution.py:281
  14.7 10.1 %collective-permute-start.7 = (bf16[64,512]{1,0:T(8,128)(2,1)S(1)}, bf16[64,512]{1,0:T(8,128)(2,1)S(1)}, u32[]{:S(2)}, u32[]{:S(2)}) collective-permute-start(bf16[64,512]{1,0:T(8,128)(2,1)S(1)} %get-tuple-element.43), channel_id=1, source_target_pairs={{0,6},{1,7},{2,4},{3,5},{4,2},{5,3},{6,0},{7,1},{8,14},{9,15},{10,... | collective-permute-start | bytes 196616 | tf_op jit(solution)/shard_map/ppermute | solution.py:281
  15.3 6.3 %copy-start.1 = (bf16[1,2,512,512]{3,2,1,0:T(8,128)(2,1)S(1)}, bf16[1,2,512,512]{3,2,1,0:T(8,128)(2,1)}, u32[]{:S(2)}) copy-start(bf16[1,2,512,512]{3,2,1,0:T(8,128)(2,1)} %param.14) | copy-start | bytes 3145732
  21.7 3.1 %copy-start.3 = (f32[1,2,64,512]{3,2,1,0:T(8,128)S(1)}, f32[1,2,64,512]{3,2,1,0:T(8,128)}, u32[]{:S(2)}) copy-start(f32[1,2,64,512]{3,2,1,0:T(8,128)} %param.9) | copy-start | bytes 786436
  26.9 32.5 %copy-start.5 = (f32[2,64,512]{2,1,0:T(8,128)S(1)}, f32[2,64,512]{2,1,0:T(8,128)}, u32[]{:S(2)}) copy-start(f32[2,64,512]{2,1,0:T(8,128)} %refs_7_.3) | copy-start | bytes 786436
  26.9 32.4 %copy-start.6 = (f32[1,2,64,512]{3,2,1,0:T(8,128)S(1)}, f32[1,2,64,512]{3,2,1,0:T(8,128)}, u32[]{:S(2)}) copy-start(f32[1,2,64,512]{3,2,1,0:T(8,128)} %param.10) | copy-start | bytes 786436
  27.0 32.4 %copy-start.7 = (f32[1,2,64,512]{3,2,1,0:T(8,128)S(1)}, f32[1,2,64,512]{3,2,1,0:T(8,128)}, u32[]{:S(2)}) copy-start(f32[1,2,64,512]{3,2,1,0:T(8,128)} %param.11) | copy-start | bytes 786436
  27.0 32.4 %copy-start.8 = (f32[2,64,512]{2,1,0:T(8,128)S(1)}, f32[2,64,512]{2,1,0:T(8,128)}, u32[]{:S(2)}) copy-start(f32[2,64,512]{2,1,0:T(8,128)} %refs_6_.1) | copy-start | bytes 786436
  27.0 5.4 %collective-permute-start.12 = (f32[64,512]{1,0:T(8,128)S(1)}, f32[64,512]{1,0:T(8,128)S(1)}, u32[]{:S(2)}, u32[]{:S(2)}) collective-permute-start(f32[64,512]{1,0:T(8,128)S(1)} %get-tuple-element.50.refs_0_), channel_id=1, source_target_pairs={{0,8},{8,0},{16,24},{24,16},{1,9},{9,1},{17,25},{25,17},{2,10},{10... | collective-permute-start | bytes 393224 | tf_op jit(solution)/shard_map/ppermute | solution.py:281
  28.5 15.8 %collective-permute-start.10 = (bf16[192,512]{1,0:T(8,128)(2,1)S(1)}, bf16[192,512]{1,0:T(8,128)(2,1)S(1)}, u32[]{:S(2)}, u32[]{:S(2)}) collective-permute-start(bf16[192,512]{1,0:T(8,128)(2,1)S(1)} %get-tuple-element.48), channel_id=1, source_target_pairs={{0,4},{1,5},{2,6},{3,7},{4,0},{5,1},{6,2},{7,3},{8,12},{9,13},{10,... | collective-permute-start | bytes 589832 | tf_op jit(solution)/shard_map/ppermute | solution.py:281
  30.8 13.6 %collective-permute-start.11 = (bf16[192,512]{1,0:T(8,128)(2,1)S(1)}, bf16[192,512]{1,0:T(8,128)(2,1)S(1)}, u32[]{:S(2)}, u32[]{:S(2)}) collective-permute-start(bf16[192,512]{1,0:T(8,128)(2,1)S(1)} %get-tuple-element.49), channel_id=1, source_target_pairs={{0,6},{1,7},{2,4},{3,5},{4,2},{5,3},{6,0},{7,1},{8,14},{9,15},{10,... | collective-permute-start | bytes 589832 | tf_op jit(solution)/shard_map/ppermute | solution.py:281
  32.2 14.2 %collective-permute-start.9 = (bf16[192,512]{1,0:T(8,128)(2,1)S(1)}, bf16[192,512]{1,0:T(8,128)(2,1)S(1)}, u32[]{:S(2)}, u32[]{:S(2)}) collective-permute-start(bf16[192,512]{1,0:T(8,128)(2,1)S(1)} %get-tuple-element.47), channel_id=1, source_target_pairs={{0,2},{1,3},{2,0},{3,1},{4,6},{5,7},{6,4},{7,5},{8,10},{9,11},{10,... | collective-permute-start | bytes 589832 | tf_op jit(solution)/shard_map/ppermute | solution.py:281
  32.4 5.0 %collective-permute-start.13 = (f32[64,512]{1,0:T(8,128)S(1)}, f32[64,512]{1,0:T(8,128)S(1)}, u32[]{:S(2)}, u32[]{:S(2)}) collective-permute-start(f32[64,512]{1,0:T(8,128)S(1)} %add_reps.2.refs_0_), channel_id=1, source_target_pairs={{0,16},{8,24},{16,0},{24,8},{1,17},{9,25},{17,1},{25,9},{2,18},{10... | collective-permute-start | bytes 393224 | tf_op jit(solution)/shard_map/ppermute | solution.py:281
  34.0 16.3 %collective-permute-start.8 = (bf16[2,128,512]{2,1,0:T(8,128)(2,1)S(1)}, bf16[2,128,512]{2,1,0:T(8,128)(2,1)S(1)}, u32[]{:S(2)}, u32[]{:S(2)}) collective-permute-start(bf16[2,128,512]{2,1,0:T(8,128)(2,1)S(1)} %get-tuple-element.45), channel_id=1, source_target_pairs={{0,2},{1,3},{2,0},{3,1},{4,6},{5,7},{6,4},{7,5},{8,10},{9,11},{10,... | collective-permute-start | bytes 786440 | tf_op jit(solution)/shard_map/ppermute | solution.py:281
  47.0 3.2 %collective-permute-start.15 = (bf16[256,512]{1,0:T(8,128)(2,1)S(1)}, bf16[256,512]{1,0:T(8,128)(2,1)S(1)}, u32[]{:S(2)}, u32[]{:S(2)}) collective-permute-start(bf16[256,512]{1,0:T(8,128)(2,1)S(1)} %get-tuple-element.52.refs_4_), channel_id=1, source_target_pairs={{0,1},{1,0},{2,3},{3,2},{4,5},{5,4},{6,7},{7,6},{8,9},{9,8},{10,11... | collective-permute-start | bytes 786440 | tf_op jit(solution)/shard_map/ppermute | solution.py:281
  47.1 3.1 %collective-permute-start.14 = (f32[8,128]{1,0:T(8,128)S(1)}, f32[8,128]{1,0:T(8,128)S(1)}, u32[]{:S(2)}, u32[]{:S(2)}) collective-permute-start(f32[8,128]{1,0:T(8,128)S(1)} %get-tuple-element.51.refs_0_), channel_id=1, source_target_pairs={{0,1},{1,0},{2,3},{3,2},{4,5},{5,4},{6,7},{7,6},{8,9},{9,8},{10,11... | collective-permute-start | bytes 12296 | tf_op jit(solution)/shard_map/ppermute | solution.py:281
  50.3 5.4 %collective-permute-start.17 = (f32[8,128]{1,0:T(8,128)S(1)}, f32[8,128]{1,0:T(8,128)S(1)}, u32[]{:S(2)}, u32[]{:S(2)}) collective-permute-start(f32[8,128]{1,0:T(8,128)S(1)} %add_cores.2.refs_2_.refs_9_), channel_id=1, source_target_pairs={{0,2},{1,3},{2,0},{3,1},{4,6},{5,7},{6,4},{7,5},{8,10},{9,11},{10,... | collective-permute-start | bytes 12296 | tf_op jit(solution)/shard_map/ppermute | solution.py:281
  50.4 5.3 %collective-permute-start.18 = (f32[8,128]{1,0:T(8,128)S(1)}, f32[8,128]{1,0:T(8,128)S(1)}, u32[]{:S(2)}, u32[]{:S(2)}) collective-permute-start(f32[8,128]{1,0:T(8,128)S(1)} %add_cores.2.refs_2_.refs_9_), channel_id=1, source_target_pairs={{0,4},{1,5},{2,6},{3,7},{4,0},{5,1},{6,2},{7,3},{8,12},{9,13},{10,... | collective-permute-start | bytes 12296 | tf_op jit(solution)/shard_map/ppermute | solution.py:281
  53.9 5.5 %collective-permute-start.19 = (f32[8,128]{1,0:T(8,128)S(1)}, f32[8,128]{1,0:T(8,128)S(1)}, u32[]{:S(2)}, u32[]{:S(2)}) collective-permute-start(f32[8,128]{1,0:T(8,128)S(1)} %add_cores.2.refs_2_.refs_9_), channel_id=1, source_target_pairs={{0,6},{1,7},{2,4},{3,5},{4,2},{5,3},{6,0},{7,1},{8,14},{9,15},{10,... | collective-permute-start | bytes 12296 | tf_op jit(solution)/shard_map/ppermute | solution.py:281
  54.8 7.4 %collective-permute-start.16 = (bf16[1,128,512]{2,1,0:T(8,128)(2,1)S(1)}, bf16[1,128,512]{2,1,0:T(8,128)(2,1)S(1)}, u32[]{:S(2)}, u32[]{:S(2)}) collective-permute-start(bf16[1,128,512]{2,1,0:T(8,128)(2,1)S(1)} %get-tuple-element.54), channel_id=1, source_target_pairs={{0,4},{1,5},{2,6},{3,7},{4,0},{5,1},{6,2},{7,3},{8,12},{9,13},{10,... | collective-permute-start | bytes 393224 | tf_op jit(solution)/shard_map/ppermute | solution.py:281
  60.5 5.0 %collective-permute-start.20 = (f32[64,512]{1,0:T(8,128)S(1)}, f32[64,512]{1,0:T(8,128)S(1)}, u32[]{:S(2)}, u32[]{:S(2)}) collective-permute-start(f32[64,512]{1,0:T(8,128)S(1)} %get-tuple-element.62.refs_0_), channel_id=1, source_target_pairs={{0,8},{8,0},{16,24},{24,16},{1,9},{9,1},{17,25},{25,17},{2,10},{10... | collective-permute-start | bytes 393224 | tf_op jit(solution)/shard_map/ppermute | solution.py:281
  62.5 1.2 %collective-permute-start.21 = (f32[8,128]{1,0:T(8,128)S(1)}, f32[8,128]{1,0:T(8,128)S(1)}, u32[]{:S(2)}, u32[]{:S(2)}) collective-permute-start(f32[8,128]{1,0:T(8,128)S(1)} %get-tuple-element.63.refs_0_), channel_id=1, source_target_pairs={{0,1},{1,0},{2,3},{3,2},{4,5},{5,4},{6,7},{7,6},{8,9},{9,8},{10,11... | collective-permute-start | bytes 12296 | tf_op jit(solution)/shard_map/ppermute | solution.py:281
  65.5 6.0 %collective-permute-start.22 = (f32[64,512]{1,0:T(8,128)S(1)}, f32[64,512]{1,0:T(8,128)S(1)}, u32[]{:S(2)}, u32[]{:S(2)}) collective-permute-start(f32[64,512]{1,0:T(8,128)S(1)} %add_moves.2.refs_0_), channel_id=1, source_target_pairs={{0,16},{8,24},{16,0},{24,8},{1,17},{9,25},{17,1},{25,9},{2,18},{10... | collective-permute-start | bytes 393224 | tf_op jit(solution)/shard_map/ppermute | solution.py:281
  67.1 4.4 %collective-permute-start.23 = (f32[8,128]{1,0:T(8,128)S(1)}, f32[8,128]{1,0:T(8,128)S(1)}, u32[]{:S(2)}, u32[]{:S(2)}) collective-permute-start(f32[8,128]{1,0:T(8,128)S(1)} %add_cores.3.refs_2_.refs_9_), channel_id=1, source_target_pairs={{0,2},{1,3},{2,0},{3,1},{4,6},{5,7},{6,4},{7,5},{8,10},{9,11},{10,... | collective-permute-start | bytes 12296 | tf_op jit(solution)/shard_map/ppermute | solution.py:281
  67.1 4.5 %collective-permute-start.24 = (f32[8,128]{1,0:T(8,128)S(1)}, f32[8,128]{1,0:T(8,128)S(1)}, u32[]{:S(2)}, u32[]{:S(2)}) collective-permute-start(f32[8,128]{1,0:T(8,128)S(1)} %add_cores.3.refs_2_.refs_9_), channel_id=1, source_target_pairs={{0,4},{1,5},{2,6},{3,7},{4,0},{5,1},{6,2},{7,3},{8,12},{9,13},{10,... | collective-permute-start | bytes 12296 | tf_op jit(solution)/shard_map/ppermute | solution.py:281
  68.6 5.4 %collective-permute-start.25 = (f32[8,128]{1,0:T(8,128)S(1)}, f32[8,128]{1,0:T(8,128)S(1)}, u32[]{:S(2)}, u32[]{:S(2)}) collective-permute-start(f32[8,128]{1,0:T(8,128)S(1)} %add_cores.3.refs_2_.refs_9_), channel_id=1, source_target_pairs={{0,6},{1,7},{2,4},{3,5},{4,2},{5,3},{6,0},{7,1},{8,14},{9,15},{10,... | collective-permute-start | bytes 12296 | tf_op jit(solution)/shard_map/ppermute | solution.py:281
